TPU v7x, 32 devices: a whole 2x2x4 slice. The times are simulated.
32 devices in a mesh: groups: 2 (over y), wide: 4 (over z), narrow: 2 (over x), aux: 2 (over core).
Axes of the slice: x: 2, y: 2, z: 4, core: 2. Of those that a mesh axis runs over, the one named last changes fastest.
Arguments:
- dissimilarity: bfloat16 [10240, 5120], P(('groups', 'narrow', 'aux'), 'wide'), parts along dimension 0, may hold values from 0 to 37.5, as said below
- config: float32 [10240, 64], P(('groups', 'narrow', 'aux')), parts along dimension 0, may hold values from -8 to 8
Outputs:
- embedding: float32 [10240, 64], P(('groups', 'narrow', 'aux')), parts along dimension 0
- stress: float32 [2], P('groups'), parts along dimension 0
There are 2 independent parts, one for each index of `groups`. A program takes and returns all parts, laid end to end along the dimension named above; each array names one. Nothing has to cross between parts.
Inputs may be any that keep to these rules, and one draw needn't show every extreme that they name: `dissimilarity`: Symmetric, zero on the diagonal, positive off it.
All inputs are finite; a program needn't handle non-finite values.
Results may differ from a plain program's by a relative error of at most 0.0003.
Values sent between devices are 32-bit elements; how exact they have to be, the bound alone decides.
No kernel may reach another device: no remote copies, remote signals or barrier semaphores. Data moves between devices by JAX's collectives and lax.ppermute only.
A program may use at most 64 MiB of HBM per device.

v0:
```python
import jax
import jax.numpy as jnp
from jax import lax
from jax.sharding import PartitionSpec as P

ITERS = 2


floor_dist = 3.0


def tile_terms(dissim_tile, own_rows, far_rows):
    own_sq = jnp.sum(own_rows * own_rows, axis=1)
    far_sq = jnp.sum(far_rows * far_rows, axis=1)
    products = jnp.einsum("ip,jp->ij", own_rows, far_rows, precision=lax.Precision.HIGHEST)
    squared = own_sq[:, None] + far_sq[None, :] - 2.0 * products
    distance = jnp.sqrt(jnp.maximum(squared, 0.0))
    ratios = dissim_tile / jnp.maximum(distance, floor_dist)
    guttman = own_rows * jnp.sum(ratios, axis=1)[:, None] - jnp.dot(
        ratios, far_rows, precision=lax.Precision.HIGHEST
    )
    misfit = jnp.sum((dissim_tile - distance) ** 2)
    norm_sum = jnp.sum(dissim_tile * dissim_tile)
    return (guttman, misfit, norm_sum)


def shards(dissimilarity, config):
    dissim_tile = dissimilarity.astype(jnp.float32)
    points = dissim_tile.shape[1] * lax.axis_size("wide")
    block_rows = config.shape[0]
    own_rows = config
    misfit = jnp.zeros((), jnp.float32)
    norm_sum = jnp.zeros((), jnp.float32)
    for iteration in range(ITERS):
        everything = lax.all_gather(own_rows, ("narrow", "aux"), axis=0, tiled=True)
        far_rows = lax.dynamic_slice_in_dim(
            everything, lax.axis_index("wide") * block_rows, block_rows, 0
        )
        guttman, misfit, norm_sum = tile_terms(dissim_tile, own_rows, far_rows)
        share = lax.psum_scatter(guttman, "wide", scatter_dimension=0, tiled=True) / points
        own_rows = lax.all_gather(share, "wide", axis=0, tiled=True)
    totals = lax.psum((misfit, norm_sum), ("wide", "narrow", "aux"))
    return (own_rows, (totals[0] / totals[1]).reshape(1))


def solution(mesh):
    placed = (P(("groups", "narrow", "aux"), "wide"), P(("groups", "narrow", "aux"), None))
    return jax.shard_map(
        shards,
        mesh=mesh,
        in_specs=placed,
        out_specs=(P(("groups", "narrow", "aux"), None), P("groups")),
        check_vma=False,
    )
```

profile of v0, /device:TPU:0, one launch (start us, length us, event | category | flops | bytes accessed | tf_op | source)
XLA Modules:
  0.0 188.2 jit_solution(17633987088859473500)
XLA Ops:
  7.2 0.7 all-gather.5.cloned.1.call-update
  7.9 4.0 %copy.10 = bf16[1280,1280]{0,1:T(8,128)(2,1)S(1)} copy(bf16[1280,1280]{1,0:T(8,128)(2,1)} %param.2) | data formatting | bytes 6553600 | tf_op args[0]
  12.0 1.0 multiply_reduce_fusion.3
  13.0 17.5 %all-gather.5.cloned.1.call-done = f32[5120,64]{0,1:T(8,128)} async-done(((f32[1280,64]{0,1:T(8,128)}), f32[5120,64]{0,1:T(8,128)}) %all-gather.5.cloned.1.call-update) | async-done | bytes 1310736 | tf_op jit(solution)/shard_map/all_gather | solution.py:35
  30.5 1.0 multiply_reduce_fusion.2
  31.5 9.5 %fusion.21 = (f32[1280]{0:T(1024)S(1)}, f32[1280,1280]{0,1:T(8,128)S(1)}) fusion(f32[1280,64]{0,1:T(8,128)} %param.3, f32[5120,64]{0,1:T(8,128)} %all-gather.5.cloned.1.call-done, s32[]{:T(128)S(6)} %select_n.4, f32[1280]{0:T(1024)S(1)} %multiply_reduce_fusion.2, f32[1280]{0:T(1024)S(1)} %multiply_reduce_fusion.3, bf16[1280,1280]{0,1:T(8,128)(2,1)S(1)} %copy.10), kind=kOutput, calls=%fused_computation.35 | convolution fusion | flops 1271397120 | bytes 10501124 | tf_op jit(solution)/shard_map/ip,jp->ij/dot_general | solution.py:15
  41.0 6.2 %convolution_subtract_fusion.1 = f32[1280,64]{0,1:T(8,128)} fusion(f32[1280,1280]{0,1:T(8,128)S(1)} %get-tuple-element.8, f32[1280,64]{0,1:T(8,128)S(1)} %copy-done, f32[5120,64]{0,1:T(8,128)} %all-gather.5.cloned.1.call-done, s32[]{:T(128)S(6)} %select_n.4, f32[1280]{0:T(1024)S(1)} %get-tuple-element.7), kind=kOutput, calls=%fused_computation.18 | convolution fusion | flops 1258455040 | bytes 7541764 | tf_op jit(solution)/shard_map/dot_general | solution.py:19
  47.2 2.0 %copy.14 = f32[1280,64]{1,0:T(8,128)} copy(f32[1280,64]{0,1:T(8,128)} %convolution_subtract_fusion.1) | data formatting | bytes 655360
  49.3 22.3 %reduce-scatter.7.cloned.1.call-done = f32[320,64]{1,0:T(8,128)} async-done(((f32[1280,64]{1,0:T(8,128)}), f32[320,64]{1,0:T(8,128)}) %reduce-scatter.7.cloned.1.call-update) | async-done | bytes 81936
  71.6 1.0 copy.15
  72.6 15.1 %all-gather = f32[4,320,64]{1,2,0:T(8,128)S(1)} all-gather(f32[1,320,64]{1,2,0:T(8,128)S(1)} %multiply_bitcast_fusion.1), channel_id=1, replica_groups=mesh['groups'=2,'wide'=4,'narrow'=2,'aux'=2] {'wide'}, dimensions={0}, use_global_device_ids=true | all-gather | bytes 409600 | tf_op jit(solution)/shard_map/all_gather | solution.py:41
  87.7 1.0 copy.12
  88.7 2.0 %reshape.15 = f32[1280,64]{0,1:T(8,128)} reshape(f32[4,320,64]{1,0,2:T(4,128)} %copy.12) | data formatting | bytes 655360
  90.8 1.0 multiply_reduce_fusion.1
  91.8 16.3 %all-gather.7.cloned.1.call-done = f32[5120,64]{0,1:T(8,128)} async-done(((f32[1280,64]{0,1:T(8,128)}), f32[5120,64]{0,1:T(8,128)}) %all-gather.7.cloned.1.call-update) | async-done | bytes 1310736 | tf_op jit(solution)/shard_map/all_gather | solution.py:35
  108.1 1.0 multiply_reduce_fusion
  109.1 11.3 %fusion.9 = (f32[]{:T(128)}, f32[1280]{0:T(1024)S(1)}, f32[]{:T(128)}, f32[1280,1280]{0,1:T(8,128)S(1)}) fusion(bf16[1280,1280]{0,1:T(8,128)(2,1)S(1)} %copy.10, f32[1280,64]{0,1:T(8,128)} %reshape.15, f32[5120,64]{0,1:T(8,128)} %all-gather.7.cloned.1.call-done, s32[]{:T(128)S(6)} %select_n.4, f32[1280]{0:T(1024)S(1)} %multiply_reduce_fusion, ...), kind=kOutput, calls=%fused_computation.15 | convolution fusion | flops 1279589120 | bytes 10501132 | tf_op jit(solution)/shard_map/ip,jp->ij/dot_general | solution.py:15
  120.4 6.6 %convolution_subtract_fusion = f32[1280,64]{0,1:T(8,128)} fusion(bf16[1280,1280]{0,1:T(8,128)(2,1)S(1)} %copy.10, f32[1280,1280]{0,1:T(8,128)S(1)} %get-tuple-element.9, f32[1280,64]{0,1:T(8,128)S(1)} %copy-done.1, f32[5120,64]{0,1:T(8,128)} %all-gather.7.cloned.1.call-done, s32[]{:T(128)S(6)} %select_n.4, f32[1280]{0:T(1024)S(1)} %get-tuple-element.3), kind=kOutput, calls=%fused_computation.17 | convolution fusion | flops 1263370240 | bytes 10818564 | tf_op jit(solution)/shard_map/dot_general | solution.py:19
  127.0 2.0 %copy.16 = f32[1280,64]{1,0:T(8,128)} copy(f32[1280,64]{0,1:T(8,128)} %convolution_subtract_fusion) | data formatting | bytes 655360
  129.1 33.5 %all-reduce = (f32[]{:T(128)}, f32[]{:T(128)}) all-reduce(f32[]{:T(128)} %get-tuple-element.2, f32[]{:T(128)} %get-tuple-element.4), channel_id=1, replica_groups=mesh['groups'=2,'wide'=4,'narrow'=2,'aux'=2] {'wide','narrow','aux'}, use_global_device_ids=true, to_apply=%region_9.0 | all-reduce | flops 2 | bytes 16 | tf_op jit(solution)/shard_map/psum | solution.py:42
  164.0 1.0 copy.17
  165.0 14.3 %all-gather.1 = f32[4,320,64]{1,2,0:T(8,128)S(1)} all-gather(f32[1,320,64]{1,2,0:T(8,128)S(1)} %multiply_bitcast_fusion), channel_id=1, replica_groups=mesh['groups'=2,'wide'=4,'narrow'=2,'aux'=2] {'wide'}, dimensions={0}, use_global_device_ids=true | all-gather | bytes 409600 | tf_op jit(solution)/shard_map/all_gather | solution.py:41
  179.3 0.3 copy.13
  179.6 1.0 reshape.17
  (14 shorter events, 0.3 us)
Async XLA Ops:
  7.2 23.3 %all-gather.5.cloned.1.call-start = ((), (), s32[]{:S(2)}) async-start(), calls=%async_computation.2 | async-start | bytes 1638400 | tf_op jit(solution)/shard_map/all_gather | solution.py:35
  7.9 63.7 %reduce-scatter.7.cloned.1.call-start = ((), (), s32[]{:S(2)}) async-start(), calls=%async_computation.4 | async-start | bytes 819200
  31.5 9.5 %copy-start = (f32[1280,64]{0,1:T(8,128)S(1)}, f32[1280,64]{0,1:T(8,128)}, u32[]{:S(2)}) copy-start(f32[1280,64]{0,1:T(8,128)} %param.3) | copy-start | bytes 983044
  49.2 58.8 %all-gather.7.cloned.1.call-start = ((), (), s32[]{:S(2)}) async-start(), calls=%async_computation.3 | async-start | bytes 1638400 | tf_op jit(solution)/shard_map/all_gather | solution.py:35
  90.7 73.2 %reduce-scatter.9.cloned.1.call-start = ((), (), s32[]{:S(2)}) async-start(), calls=%async_computation.5 | async-start | bytes 819200
  109.1 11.3 %copy-start.1 = (f32[1280,64]{0,1:T(8,128)S(1)}, f32[1280,64]{0,1:T(8,128)}, u32[]{:S(2)}) copy-start(f32[1280,64]{0,1:T(8,128)} %reshape.15) | copy-start | bytes 983044
Sparse Core Ops, SparseCore 0:
  9.6 20.8 all-gather.4
  49.4 22.1 reduce-scatter.6
  90.9 17.1 all-gather.6
  129.2 22.4 reduce-scatter.8
where the time goes:
time: 189 us; the launch traced here: 188 us
  blocking collectives  63 us (33%)
  waiting for transfers between devices  56.8 us (30%)
  matrix products  33.5 us (18%)
  between operations  16.3 us (9%)
  local copies, waits for them, and re-layouts  14.4 us (8%)
  other arithmetic  4.06 us (2%)
    all_gather x2, waiting for transfers between devices, shards(): everything = lax.all_gather(own_rows, ('narrow', 'aux'), axis=0, tiled=True)  33.8 us
    psum x1, blocking collectives, shards(): totals = lax.psum((misfit, norm_sum), ('wide', 'narrow', 'aux'))  33.5 us
    all_gather x2, blocking collectives, shards(): own_rows = lax.all_gather(share, 'wide', axis=0, tiled=True)  29.4 us
    unnamed x6, waiting for transfers between devices  23 us
    dot_general x2, matrix products, tile_terms(): jnp.einsum('ip,jp->ij', own_rows, far_rows, precision=lax.Precision.HIGHEST)  20.8 us
    unnamed x11, local copies, waits for them, and re-layouts  13.2 us
    dot_general x2, matrix products, tile_terms(): jnp.dot(ratios, far_rows, precision=lax.Precision.HIGHEST)  12.8 us
  transfers between devices with their start and end apart: 4, of which 3 were waited for; matrix products, arithmetic and copies ran while one was open for 3% of the time, Pallas kernels for 0%

commit v1 on v0

v1 whole, which is shorter than its diff:
```python
import functools

import jax
import jax.numpy as jnp
from jax import lax
from jax.experimental import pallas as pl
from jax.experimental.pallas import tpu as pltpu
from jax.sharding import PartitionSpec as P

ITERS = 2
FLOOR = 3.0
TINY = 1e-30
DEPTH = 256
LANES = 128
EXTRA = 16
SUMS = 16

f32 = jnp.float32
bf16 = jnp.bfloat16
AXES = ("wide", "narrow", "aux")


def split2(values):
    high = values.astype(bf16)
    return high, (values - high.astype(f32)).astype(bf16)


def split3(values):
    high = values.astype(bf16)
    rest = values - high.astype(f32)
    middle = rest.astype(bf16)
    return high, middle, (rest - middle.astype(f32)).astype(bf16)


def norm_rows(points, first):
    count = points.shape[1]
    squares = jnp.sum(points * points, axis=0, keepdims=True)
    row = lax.broadcasted_iota(jnp.int32, (EXTRA, count), 0)
    ones = 3 if first else 0
    parts = 0 if first else 3
    rows = jnp.where((row >= ones) & (row < ones + 3), 1.0, 0.0)
    for k, part in enumerate(split3(squares)):
        rows = jnp.where(row == parts + k, part.astype(f32), rows)
    return rows.astype(bf16)


def tile_body(scale, stress, row_step, col_step, load, delta_ref, norm_ref, *refs):
    (keep_ref, send_ref, row_pts, col_pts, result, lhs, rhs, left, r_high, r_low) = refs[-10:]
    load(refs[:-10], row_pts, col_pts)
    dims, rows = row_pts.shape
    cols = col_pts.shape[1]
    points = row_pts[...]
    high, middle, low = split3(points)
    minus2 = lambda v: (v.astype(f32) * -2.0).astype(bf16)
    fill = DEPTH - 3 * dims - EXTRA
    lhs[...] = jnp.concatenate(
        [minus2(high), minus2(high), minus2(middle), norm_rows(points, True), jnp.zeros((fill, rows), bf16)], axis=0
    ).T
    left[...] = jnp.concatenate([high, middle, low, jnp.ones((EXTRA, rows), bf16)], axis=0)
    points = col_pts[...]
    high, middle = split2(points)
    rhs[...] = jnp.concatenate(
        [high, middle, high, norm_rows(points, False), jnp.zeros((fill, cols), bf16)], axis=0
    )
    misfit = jnp.zeros((8, LANES), f32)
    for jc in range(cols // col_step):
        js = pl.ds(jc * col_step, col_step)
        slot = jc % 2
        for ic in range(rows // row_step):
            rs = pl.ds(ic * row_step, row_step)
            squared = jnp.dot(lhs[rs, :], rhs[:, js], preferred_element_type=f32)
            delta = delta_ref[rs, js].astype(f32)
            if stress:
                inverse = lax.rsqrt(jnp.maximum(squared, TINY))
                ratio = delta * jnp.minimum(inverse, 1.0 / FLOOR)
                gap = delta - jnp.maximum(squared, 0.0) * inverse
                gap = gap * gap
                for c in range(col_step // LANES):
                    part = gap[:, c * LANES:(c + 1) * LANES]
                    misfit = misfit + jnp.sum(part.reshape(row_step // 8, 8, LANES), axis=0)
            else:
                ratio = delta * lax.rsqrt(jnp.maximum(squared, FLOOR * FLOOR))
            high, low = split2(ratio)
            r_high[slot, rs, :] = high
            r_low[slot, rs, :] = low
        terms = jnp.dot(left[...], r_high[slot], preferred_element_type=f32)
        terms = terms + jnp.dot(left[...], r_low[slot], preferred_element_type=f32)
        cross = terms[:dims] + terms[dims:2 * dims] + terms[2 * dims:3 * dims]
        result[:, js] = (col_pts[:, js] * terms[3 * dims:3 * dims + 1] - cross) * scale
    half = dims // 2
    mine = lax.axis_index("aux")
    for ref, which in ((keep_ref, mine), (send_ref, 1 - mine)):
        ref[:, :cols] = result[pl.ds(pl.multiple_of(which * half, 8), half), :]
        if stress:
            ref[:8, cols:] = misfit
            ref[8:16, cols:] = norm_ref[...]
            ref[16:, cols:] = jnp.zeros((half - 16, LANES), f32)


def tile_call(load, scale, stress, dims, delta, norm, *arrays):
    rows, cols = delta.shape
    wide = cols + (LANES if stress else 0)
    step = 256 if rows % 256 == 0 and cols % 256 == 0 else 128
    vmem = pl.BlockSpec(memory_space=pltpu.VMEM)
    out = jax.ShapeDtypeStruct((dims // 2, wide), f32)
    return pl.pallas_call(
        functools.partial(tile_body, scale, stress, step, step, load),
        out_shape=(out, out),
        in_specs=[vmem] * (2 + len(arrays)),
        out_specs=(vmem, vmem),
        scratch_shapes=[
            pltpu.VMEM((dims, rows), f32),
            pltpu.VMEM((dims, cols), f32),
            pltpu.VMEM((dims, cols), f32),
            pltpu.VMEM((rows, DEPTH), bf16),
            pltpu.VMEM((DEPTH, cols), bf16),
            pltpu.VMEM((3 * dims + EXTRA, rows), bf16),
            pltpu.VMEM((2, rows, step), bf16),
            pltpu.VMEM((2, rows, step), bf16),
        ],
        compiler_params=pltpu.CompilerParams(vmem_limit_bytes=40 << 20),
        name="tile",
    )(delta, norm, *arrays)


def norm_body(delta_ref, out_ref):
    rows, cols = delta_ref.shape
    total = jnp.zeros((8, LANES), f32)
    for ic in range(rows // LANES):
        for jc in range(cols // LANES):
            part = delta_ref[ic * LANES:(ic + 1) * LANES, jc * LANES:(jc + 1) * LANES].astype(f32)
            total = total + jnp.sum((part * part).reshape(LANES // 8, 8, LANES), axis=0)
    out_ref[...] = total


def norm_call(delta):
    vmem = pl.BlockSpec(memory_space=pltpu.VMEM)
    return pl.pallas_call(
        norm_body,
        out_shape=jax.ShapeDtypeStruct((8, LANES), f32),
        in_specs=[vmem],
        out_specs=vmem,
        compiler_params=pltpu.CompilerParams(vmem_limit_bytes=40 << 20),
        name="norm",
    )(delta)


class Grid:
    def __init__(self):
        self.narrow = lax.axis_size("narrow")
        self.wide = lax.axis_size("wide")
        self.x = lax.axis_index("narrow")
        self.a = lax.axis_index("aux")
        self.z = lax.axis_index("wide")
        assert lax.axis_size("aux") == 2 and self.wide == 2 * self.narrow

    def pairs(self, source):
        place = lambda x, a, z: (z * self.narrow + x) * 2 + a
        return [
            (place(*source(x, a, z)), place(x, a, z))
            for z in range(self.wide)
            for x in range(self.narrow)
            for a in range(2)
        ]

    def send(self, value, source):
        return lax.ppermute(value, AXES, self.pairs(source))

    def other_core(self, value):
        return lax.ppermute(value, "aux", [(0, 1), (1, 0)])

    def across(self, value, axis, bit):
        return lax.ppermute(value, axis, [(i, i ^ bit) for i in range(lax.axis_size(axis))])

    def spread(self, first):
        def source(x, a, z):
            block = 2 * x + a
            offset = z ^ block
            top, low = offset // self.narrow, offset % self.narrow
            if first:
                return x ^ low, a ^ (1 - top), block
            return x ^ low ^ (1 - top), a ^ top, block

        return source

    def spread_half(self):
        top = (self.z ^ (2 * self.x + self.a)) // self.narrow
        return self.a ^ (1 - top)


def bits(count):
    return [1 << k for k in range(count.bit_length() - 1)]


def first_columns(grid, own):
    x_home = lambda z: z // 2
    current = own
    steps = bits(grid.narrow)
    for place, bit in enumerate(reversed(steps)):

        def source(x, a, z):
            return (x ^ bit, a, z) if a == z % 2 else (x, 1 - a, z ^ 1)

        got = grid.send(current, source)
        if place < len(steps) - 1:
            rest = (grid.x ^ (grid.z // 2)) & (2 * bit - 1)
            current = jnp.where((rest == bit) & (grid.a == grid.z % 2), got, current)
        elif len(steps) > 1:
            rest = (grid.x ^ (grid.z // 2)) & (2 * bit - 1)
            got = jnp.where(rest == bit, got, current)
    return got, grid.other_core(got)


def load_first(narrow, refs, row_pts, col_pts):
    own, got, passed = refs
    x, a, z = (lax.axis_index(n) for n in ("narrow", "aux", "wide"))
    home = (x == z // 2) & (narrow == 2)
    core = a == z % 2
    row_pts[...] = own[...]

    @pl.when(home & core)
    def _():
        col_pts[...] = own[...]

    @pl.when(home != core)
    def _():
        col_pts[...] = got[...]

    @pl.when(jnp.logical_not(home | core))
    def _():
        col_pts[...] = passed[...]


def load_next(narrow, refs, row_pts, col_pts):
    kept, passed, first, second = refs
    x, a, z = (lax.axis_index(n) for n in ("narrow", "aux", "wide"))
    half = kept.shape[0]
    top = (z ^ (2 * x + a)) // narrow
    side = a ^ (1 - top)
    at = lambda which: pl.ds(pl.multiple_of(which * half, 8), half)
    col_pts[at(a), :] = kept[...]
    col_pts[at(1 - a), :] = passed[...]
    row_pts[at(side), :] = first[...]
    row_pts[at(1 - side), :] = second[...]


def shards(dissimilarity, config):
    grid = Grid()
    dims = config.shape[1]
    cols = dissimilarity.shape[1]
    scale = 1.0 / (cols * grid.wide)
    own = config.T
    got, passed = first_columns(grid, own)
    norm = norm_call(dissimilarity)

    keep, send = tile_call(functools.partial(load_first, grid.narrow), scale, False, dims, dissimilarity, norm, own, got, passed)
    for iteration in range(1, ITERS + 1):
        last = iteration == ITERS
        half = keep + grid.other_core(send)
        for bit in bits(grid.narrow):
            half = half + grid.across(half, "narrow", bit)
        part = half[:, :cols]
        first = grid.send(part, grid.spread(True))
        second = grid.send(part, grid.spread(False))
        if last:
            break
        other = grid.other_core(part)
        load = functools.partial(load_next, grid.narrow)
        keep, send = tile_call(
            load, scale, iteration + 1 == ITERS, dims, dissimilarity, norm, part, other, first, second
        )
    sums = half[:SUMS, cols:]
    for bit in bits(grid.wide):
        sums = sums + grid.across(sums, "wide", bit)
    in_order = grid.spread_half() == 0
    embedding = jnp.where(
        in_order, jnp.concatenate([first, second], axis=0), jnp.concatenate([second, first], axis=0)
    )
    stress = jnp.sum(sums[:8]) / jnp.sum(sums[8:])
    return embedding.T, stress.reshape(1)


def solution(mesh):
    placed = (P(("groups", "narrow", "aux"), "wide"), P(("groups", "narrow", "aux"), None))
    return jax.shard_map(
        shards,
        mesh=mesh,
        in_specs=placed,
        out_specs=(P(("groups", "narrow", "aux"), None), P("groups")),
        check_vma=False,
    )
```

time: 189 us -> 64.7 us (0.34)
  blocking collectives: 63 us -> 0 us
  matrix products: 33.5 us -> 0 us
  waiting for transfers between devices: 56.8 us -> 31.1 us
  starting transfers between devices: 0.16 us -> 18.4 us
  between operations: 16.3 us -> 3.19 us
  local copies, waits for them, and re-layouts: 14.4 us -> 2.26 us
  Pallas kernels: 0 us -> 8.07 us
  other arithmetic: 4.06 us -> 1.44 us
    all_gather x2 -> x0, waiting for transfers between devices: 33.8 us -> none  [shards(): everything = lax.all_gather(own_rows, ('narrow', 'aux'), axis=0, tiled=True)]
    psum x1 -> x0, blocking collectives: 33.5 us -> none  [shards(): totals = lax.psum((misfit, norm_sum), ('wide', 'narrow', 'aux'))]
    dot_general x4 -> x0, matrix products: 33.5 us -> none  [the longest x2 20.8 us: tile_terms(): jnp.einsum('ip,jp->ij', own_rows, far_rows, precision=lax.Precision.HIGHEST)]
    ppermute x0 -> x13, waiting for transfers between devices: none -> 31.1 us  [the longest x4 17 us: across(): lax.ppermute(value, axis, [(i, i ^ bit) for i in range(lax.axis_size(axis...]
    all_gather x2 -> x0, blocking collectives: 29.4 us -> none  [shards(): own_rows = lax.all_gather(share, 'wide', axis=0, tiled=True)]
    unnamed x6 -> x0, waiting for transfers between devices: 23 us -> none
    ppermute x0 -> x13, starting transfers between devices: none -> 18.4 us  [the longest x4 9.42 us: across(): lax.ppermute(value, axis, [(i, i ^ bit) for i in range(lax.axis_size(axis...]
    unnamed x11 -> x4, local copies, waits for them, and re-layouts: 13.2 us -> 2.25 us
  transfers between devices with their start and end apart: 4 -> 13, of which waited for: 3 -> 9; matrix products, arithmetic and copies ran while one was open for 3% -> 1% of each run, Pallas kernels for 0% -> 1%
where the time goes in v1:
time: 64.7 us; the launch traced here: 64.5 us
  waiting for transfers between devices  31.1 us (48%)
  starting transfers between devices  18.4 us (28%)
  Pallas kernels  8.07 us (12%)
  between operations  3.19 us (5%)
  local copies, waits for them, and re-layouts  2.26 us (3%)
  other arithmetic  1.44 us (2%)
    ppermute x4, waiting for transfers between devices, across(): lax.ppermute(value, axis, [(i, i ^ bit) for i in range(lax.axis_size(axis...  17 us
    ppermute x5, waiting for transfers between devices, send(): return lax.ppermute(value, AXES, self.pairs(source))  11.7 us
    ppermute x4, starting transfers between devices, across(): lax.ppermute(value, axis, [(i, i ^ bit) for i in range(lax.axis_size(axis...  9.42 us
    ppermute x5, starting transfers between devices, send(): return lax.ppermute(value, AXES, self.pairs(source))  8.25 us
    pallas_call x2, Pallas kernels, tile_call(): pl.pallas_call(functools.partial(tile_body, scale, stress, step, step, lo...  7.43 us
    ppermute x4, waiting for transfers between devices, other_core(): return lax.ppermute(value, 'aux', [(0, 1), (1, 0)])  2.44 us
    unnamed x4, local copies, waits for them, and re-layouts  2.25 us
  transfers between devices with their start and end apart: 13, of which 9 were waited for; matrix products, arithmetic and copies ran while one was open for 1% of the time, Pallas kernels for 1%

profile of v1, /device:TPU:0, one launch (start us, length us, event | category | flops | bytes accessed | tf_op | source)
XLA Modules:
  0.0 64.5 jit_solution(4931365069412729701)
XLA Ops:
  0.6 3.0 %collective-permute-start = (f32[64,1280]{1,0:T(8,128)}, f32[64,1280]{1,0:T(8,128)S(1)}, u32[]{:S(2)}, u32[]{:S(2)}) collective-permute-start(f32[64,1280]{1,0:T(8,128)} %bitcast.4), channel_id=1, source_target_pairs={{2,0},{4,1},{0,2},{6,3},{1,4},{7,5},{3,6},{5,7},{10,8},{12,9},{8,1... | collective-permute-start | bytes 983048 | tf_op jit(solution)/shard_map/ppermute | solution.py:167
  3.6 5.3 %collective-permute-done.refs_1_ = f32[64,1280]{1,0:T(8,128)S(1)} collective-permute-done((f32[64,1280]{1,0:T(8,128)}, f32[64,1280]{1,0:T(8,128)S(1)}, u32[]{:S(2)}, u32[]{:S(2)}) %collective-permute-start) | collective-permute-done | bytes 327712 | tf_op jit(solution)/shard_map/ppermute | solution.py:167
  9.0 1.9 %copy-done = bf16[1280,1280]{1,0:T(8,128)(2,1)S(1)} copy-done((bf16[1280,1280]{1,0:T(8,128)(2,1)S(1)}, bf16[1280,1280]{1,0:T(8,128)(2,1)}, u32[]{:S(2)}) %copy-start) | copy-done | bytes 3276824
  10.9 0.6 norm.1.norm_ref
  11.6 0.3 copy-done.1
  11.9 3.2 %tile.2 = (f32[32,1280]{1,0:T(8,128)S(1)}, f32[32,1280]{1,0:T(8,128)S(1)}) custom-call(bf16[1280,1280]{1,0:T(8,128)(2,1)S(1)} %copy-done, f32[8,128]{1,0:T(8,128)S(1)} %norm.1.norm_ref, f32[64,1280]{1,0:T(8,128)S(1)} %bitcast.5, f32[64,1280]{1,0:T(8,128)S(1)} %collective-permute-done.refs_1_, f32[64,1280]{1,0:T(8,128)S(1)} %collective-permute-done.1.refs_2_), custom_call_target="tpu_custom_call" | custom-call | tf_op jit(solution)/shard_map/tile/pallas_call | solution.py:106
  15.1 0.5 collective-permute-start.2
  15.5 1.0 %collective-permute-done.2 = f32[32,1280]{1,0:T(8,128)S(1)} collective-permute-done((f32[32,1280]{1,0:T(8,128)S(1)}, f32[32,1280]{1,0:T(8,128)S(1)}, u32[]{:S(2)}, u32[]{:S(2)}) %collective-permute-start.2) | collective-permute-done | bytes 163872 | tf_op jit(solution)/shard_map/ppermute | solution.py:170
  16.6 2.1 %collective-permute-start.3 = (f32[32,1280]{1,0:T(8,128)S(1)}, f32[32,1280]{1,0:T(8,128)S(1)}, u32[]{:S(2)}, u32[]{:S(2)}) collective-permute-start(f32[32,1280]{1,0:T(8,128)S(1)} %add.23), channel_id=1, source_target_pairs={{0,2},{2,0},{1,3},{3,1},{4,6},{6,4},{5,7},{7,5},{8,10},{10,8},{9,1... | collective-permute-start | bytes 491528 | tf_op jit(solution)/shard_map/ppermute | solution.py:173
  18.7 4.7 %collective-permute-done.3 = f32[32,1280]{1,0:T(8,128)S(1)} collective-permute-done((f32[32,1280]{1,0:T(8,128)S(1)}, f32[32,1280]{1,0:T(8,128)S(1)}, u32[]{:S(2)}, u32[]{:S(2)}) %collective-permute-start.3) | collective-permute-done | bytes 163872 | tf_op jit(solution)/shard_map/ppermute | solution.py:173
  23.5 2.9 %collective-permute-start.5 = (f32[32,1280]{1,0:T(8,128)S(1)}, f32[32,1280]{1,0:T(8,128)S(1)}, u32[]{:S(2)}, u32[]{:S(2)}) collective-permute-start(f32[32,1280]{1,0:T(8,128)S(1)} %add.24.refs_0_), channel_id=1, source_target_pairs={{1,0},{6,1},{10,2},{13,3},{3,4},{4,5},{8,6},{15,7},{0,8},{7,9},{11... | collective-permute-start | bytes 491528 | tf_op jit(solution)/shard_map/ppermute | solution.py:167
  26.4 4.4 %collective-permute-done.5.refs_2_ = f32[32,1280]{1,0:T(8,128)S(1)} collective-permute-done((f32[32,1280]{1,0:T(8,128)S(1)}, f32[32,1280]{1,0:T(8,128)S(1)}, u32[]{:S(2)}, u32[]{:S(2)}) %collective-permute-start.5) | collective-permute-done | bytes 163872 | tf_op jit(solution)/shard_map/ppermute | solution.py:167
  30.8 2.0 %collective-permute-done.6.refs_3_ = f32[32,1280]{1,0:T(8,128)S(1)} collective-permute-done((f32[32,1280]{1,0:T(8,128)S(1)}, f32[32,1280]{1,0:T(8,128)S(1)}, u32[]{:S(2)}, u32[]{:S(2)}) %collective-permute-start.6) | collective-permute-done | bytes 163872 | tf_op jit(solution)/shard_map/ppermute | solution.py:167
  32.8 4.3 %tile.3 = (f32[32,1408]{1,0:T(8,128)S(1)}, f32[32,1408]{1,0:T(8,128)S(1)}) custom-call(bf16[1280,1280]{1,0:T(8,128)(2,1)S(1)} %copy-done, f32[8,128]{1,0:T(8,128)S(1)} %norm.1.norm_ref, f32[32,1280]{1,0:T(8,128)S(1)} %add.24.refs_0_, f32[32,1280]{1,0:T(8,128)S(1)} %collective-permute-done.4.refs_1_, f32[32,1280]{1,0:T(8,128)S(1)} %collective-permute-done.5.refs_2_, ...), custom_call_target="tpu_custom_call" | custom-call | tf_op jit(solution)/shard_map/tile/pallas_call | solution.py:106
  37.2 1.4 %collective-permute-done.7 = f32[32,1408]{1,0:T(8,128)S(1)} collective-permute-done((f32[32,1408]{1,0:T(8,128)S(1)}, f32[32,1408]{1,0:T(8,128)S(1)}, u32[]{:S(2)}, u32[]{:S(2)}) %collective-permute-start.7) | collective-permute-done | bytes 180256 | tf_op jit(solution)/shard_map/ppermute | solution.py:170
  38.6 4.0 %collective-permute-start.8 = (f32[32,1408]{1,0:T(8,128)S(1)}, f32[32,1408]{1,0:T(8,128)S(1)}, u32[]{:S(2)}, u32[]{:S(2)}) collective-permute-start(f32[32,1408]{1,0:T(8,128)S(1)} %add.25), channel_id=1, source_target_pairs={{0,2},{2,0},{1,3},{3,1},{4,6},{6,4},{5,7},{7,5},{8,10},{10,8},{9,1... | collective-permute-start | bytes 540680 | tf_op jit(solution)/shard_map/ppermute | solution.py:173
  42.6 4.9 %collective-permute-done.8 = f32[32,1408]{1,0:T(8,128)S(1)} collective-permute-done((f32[32,1408]{1,0:T(8,128)S(1)}, f32[32,1408]{1,0:T(8,128)S(1)}, u32[]{:S(2)}, u32[]{:S(2)}) %collective-permute-start.8) | collective-permute-done | bytes 180256 | tf_op jit(solution)/shard_map/ppermute | solution.py:173
  47.5 1.2 %collective-permute-start.11 = (f32[16,128]{1,0:T(8,128)S(1)}, f32[16,128]{1,0:T(8,128)S(1)}, u32[]{:S(2)}, u32[]{:S(2)}) collective-permute-start(f32[16,128]{1,0:T(8,128)S(1)} %slice.17), channel_id=1, source_target_pairs={{0,4},{4,0},{8,12},{12,8},{1,5},{5,1},{9,13},{13,9},{2,6},{6,2},{1... | collective-permute-start | bytes 24584 | tf_op jit(solution)/shard_map/ppermute | solution.py:173
  48.6 1.0 %collective-permute-start.10 = (f32[32,1280]{1,0:T(8,128)S(1)}, f32[32,1280]{1,0:T(8,128)S(1)}, u32[]{:S(2)}, u32[]{:S(2)}) collective-permute-start(f32[32,1280]{1,0:T(8,128)S(1)} %slice.16), channel_id=1, source_target_pairs={{2,0},{5,1},{11,2},{12,3},{0,4},{7,5},{9,6},{14,7},{1,8},{6,9},{8,... | collective-permute-start | bytes 491528 | tf_op jit(solution)/shard_map/ppermute | solution.py:167
  49.6 1.4 %collective-permute-start.9 = (f32[32,1280]{1,0:T(8,128)S(1)}, f32[32,1280]{1,0:T(8,128)S(1)}, u32[]{:S(2)}, u32[]{:S(2)}) collective-permute-start(f32[32,1280]{1,0:T(8,128)S(1)} %slice.16), channel_id=1, source_target_pairs={{1,0},{6,1},{10,2},{13,3},{3,4},{4,5},{8,6},{15,7},{0,8},{7,9},{11... | collective-permute-start | bytes 491528 | tf_op jit(solution)/shard_map/ppermute | solution.py:167
  51.2 2.2 %collective-permute-start.12 = (f32[16,128]{1,0:T(8,128)S(1)}, f32[16,128]{1,0:T(8,128)S(1)}, u32[]{:S(2)}, u32[]{:S(2)}) collective-permute-start(f32[16,128]{1,0:T(8,128)S(1)} %slice_add_fusion), channel_id=1, source_target_pairs={{0,8},{4,12},{8,0},{12,4},{1,9},{5,13},{9,1},{13,5},{2,10},{6,14},... | collective-permute-start | bytes 24584 | tf_op jit(solution)/shard_map/ppermute | solution.py:173
  53.4 7.2 %collective-permute-done.12 = f32[16,128]{1,0:T(8,128)S(1)} collective-permute-done((f32[16,128]{1,0:T(8,128)S(1)}, f32[16,128]{1,0:T(8,128)S(1)}, u32[]{:S(2)}, u32[]{:S(2)}) %collective-permute-start.12) | collective-permute-done | bytes 8224 | tf_op jit(solution)/shard_map/ppermute | solution.py:173
  60.6 0.6 slice_reduce_fusion
  62.6 0.7 %fusion = f32[1280,64]{0,1:T(8,128)} fusion(f32[32,1280]{1,0:T(8,128)S(1)} %collective-permute-done.10, f32[32,1280]{1,0:T(8,128)S(1)} %collective-permute-done.9, pred[]{:T(512)S(6)} %eq.3), kind=kLoop, calls=%fused_computation.1 | loop fusion | flops 245760 | bytes 655361 | tf_op jit(solution)/shard_map/transpose | solution.py:280
  (19 shorter events, 0.6 us)
Async XLA Ops:
  0.6 8.3 %collective-permute-start = (f32[64,1280]{1,0:T(8,128)}, f32[64,1280]{1,0:T(8,128)S(1)}, u32[]{:S(2)}, u32[]{:S(2)}) collective-permute-start(f32[64,1280]{1,0:T(8,128)} %bitcast.4), channel_id=1, source_target_pairs={{2,0},{4,1},{0,2},{6,3},{1,4},{7,5},{3,6},{5,7},{10,8},{12,9},{8,1... | collective-permute-start | bytes 983048 | tf_op jit(solution)/shard_map/ppermute | solution.py:167
  8.9 2.7 %collective-permute-start.1 = (f32[64,1280]{1,0:T(8,128)S(1)}, f32[64,1280]{1,0:T(8,128)S(1)}, u32[]{:S(2)}, u32[]{:S(2)}) collective-permute-start(f32[64,1280]{1,0:T(8,128)S(1)} %collective-permute-done.refs_1_), channel_id=1, source_target_pairs={{0,1},{1,0},{2,3},{3,2},{4,5},{5,4},{6,7},{7,6},{8,9},{9,8},{10,11... | collective-permute-start | bytes 983048 | tf_op jit(solution)/shard_map/ppermute | solution.py:170
  9.0 1.9 %copy-start = (bf16[1280,1280]{1,0:T(8,128)(2,1)S(1)}, bf16[1280,1280]{1,0:T(8,128)(2,1)}, u32[]{:S(2)}) copy-start(bf16[1280,1280]{1,0:T(8,128)(2,1)} %delta_ref.5) | copy-start | bytes 9830404
  10.9 1.0 %copy-start.1 = (f32[1280,64]{0,1:T(8,128)S(1)}, f32[1280,64]{0,1:T(8,128)}, u32[]{:S(2)}) copy-start(f32[1280,64]{0,1:T(8,128)} %param.3) | copy-start | bytes 983044
  15.1 1.5 %collective-permute-start.2 = (f32[32,1280]{1,0:T(8,128)S(1)}, f32[32,1280]{1,0:T(8,128)S(1)}, u32[]{:S(2)}, u32[]{:S(2)}) collective-permute-start(f32[32,1280]{1,0:T(8,128)S(1)} %get-tuple-element.7), channel_id=1, source_target_pairs={{0,1},{1,0},{2,3},{3,2},{4,5},{5,4},{6,7},{7,6},{8,9},{9,8},{10,11... | collective-permute-start | bytes 491528 | tf_op jit(solution)/shard_map/ppermute | solution.py:170
  16.6 6.8 %collective-permute-start.3 = (f32[32,1280]{1,0:T(8,128)S(1)}, f32[32,1280]{1,0:T(8,128)S(1)}, u32[]{:S(2)}, u32[]{:S(2)}) collective-permute-start(f32[32,1280]{1,0:T(8,128)S(1)} %add.23), channel_id=1, source_target_pairs={{0,2},{2,0},{1,3},{3,1},{4,6},{6,4},{5,7},{7,5},{8,10},{10,8},{9,1... | collective-permute-start | bytes 491528 | tf_op jit(solution)/shard_map/ppermute | solution.py:173
  23.4 3.0 %collective-permute-start.4 = (f32[32,1280]{1,0:T(8,128)S(1)}, f32[32,1280]{1,0:T(8,128)S(1)}, u32[]{:S(2)}, u32[]{:S(2)}) collective-permute-start(f32[32,1280]{1,0:T(8,128)S(1)} %add.24.refs_0_), channel_id=1, source_target_pairs={{0,1},{1,0},{2,3},{3,2},{4,5},{5,4},{6,7},{7,6},{8,9},{9,8},{10,11... | collective-permute-start | bytes 491528 | tf_op jit(solution)/shard_map/ppermute | solution.py:170
  23.5 7.3 %collective-permute-start.5 = (f32[32,1280]{1,0:T(8,128)S(1)}, f32[32,1280]{1,0:T(8,128)S(1)}, u32[]{:S(2)}, u32[]{:S(2)}) collective-permute-start(f32[32,1280]{1,0:T(8,128)S(1)} %add.24.refs_0_), channel_id=1, source_target_pairs={{1,0},{6,1},{10,2},{13,3},{3,4},{4,5},{8,6},{15,7},{0,8},{7,9},{11... | collective-permute-start | bytes 491528 | tf_op jit(solution)/shard_map/ppermute | solution.py:167
  26.4 6.4 %collective-permute-start.6 = (f32[32,1280]{1,0:T(8,128)S(1)}, f32[32,1280]{1,0:T(8,128)S(1)}, u32[]{:S(2)}, u32[]{:S(2)}) collective-permute-start(f32[32,1280]{1,0:T(8,128)S(1)} %add.24.refs_0_), channel_id=1, source_target_pairs={{2,0},{5,1},{11,2},{12,3},{0,4},{7,5},{9,6},{14,7},{1,8},{6,9},{8,... | collective-permute-start | bytes 491528 | tf_op jit(solution)/shard_map/ppermute | solution.py:167
  37.1 1.5 %collective-permute-start.7 = (f32[32,1408]{1,0:T(8,128)S(1)}, f32[32,1408]{1,0:T(8,128)S(1)}, u32[]{:S(2)}, u32[]{:S(2)}) collective-permute-start(f32[32,1408]{1,0:T(8,128)S(1)} %get-tuple-element.9), channel_id=1, source_target_pairs={{0,1},{1,0},{2,3},{3,2},{4,5},{5,4},{6,7},{7,6},{8,9},{9,8},{10,11... | collective-permute-start | bytes 540680 | tf_op jit(solution)/shard_map/ppermute | solution.py:170
  38.6 8.8 %collective-permute-start.8 = (f32[32,1408]{1,0:T(8,128)S(1)}, f32[32,1408]{1,0:T(8,128)S(1)}, u32[]{:S(2)}, u32[]{:S(2)}) collective-permute-start(f32[32,1408]{1,0:T(8,128)S(1)} %add.25), channel_id=1, source_target_pairs={{0,2},{2,0},{1,3},{3,1},{4,6},{6,4},{5,7},{7,5},{8,10},{10,8},{9,1... | collective-permute-start | bytes 540680 | tf_op jit(solution)/shard_map/ppermute | solution.py:173
  47.5 3.7 %collective-permute-start.11 = (f32[16,128]{1,0:T(8,128)S(1)}, f32[16,128]{1,0:T(8,128)S(1)}, u32[]{:S(2)}, u32[]{:S(2)}) collective-permute-start(f32[16,128]{1,0:T(8,128)S(1)} %slice.17), channel_id=1, source_target_pairs={{0,4},{4,0},{8,12},{12,8},{1,5},{5,1},{9,13},{13,9},{2,6},{6,2},{1... | collective-permute-start | bytes 24584 | tf_op jit(solution)/shard_map/ppermute | solution.py:173
  48.6 13.9 %collective-permute-start.10 = (f32[32,1280]{1,0:T(8,128)S(1)}, f32[32,1280]{1,0:T(8,128)S(1)}, u32[]{:S(2)}, u32[]{:S(2)}) collective-permute-start(f32[32,1280]{1,0:T(8,128)S(1)} %slice.16), channel_id=1, source_target_pairs={{2,0},{5,1},{11,2},{12,3},{0,4},{7,5},{9,6},{14,7},{1,8},{6,9},{8,... | collective-permute-start | bytes 491528 | tf_op jit(solution)/shard_map/ppermute | solution.py:167
  49.6 12.9 %collective-permute-start.9 = (f32[32,1280]{1,0:T(8,128)S(1)}, f32[32,1280]{1,0:T(8,128)S(1)}, u32[]{:S(2)}, u32[]{:S(2)}) collective-permute-start(f32[32,1280]{1,0:T(8,128)S(1)} %slice.16), channel_id=1, source_target_pairs={{1,0},{6,1},{10,2},{13,3},{3,4},{4,5},{8,6},{15,7},{0,8},{7,9},{11... | collective-permute-start | bytes 491528 | tf_op jit(solution)/shard_map/ppermute | solution.py:167
  51.2 9.4 %collective-permute-start.12 = (f32[16,128]{1,0:T(8,128)S(1)}, f32[16,128]{1,0:T(8,128)S(1)}, u32[]{:S(2)}, u32[]{:S(2)}) collective-permute-start(f32[16,128]{1,0:T(8,128)S(1)} %slice_add_fusion), channel_id=1, source_target_pairs={{0,8},{4,12},{8,0},{12,4},{1,9},{5,13},{9,1},{13,5},{2,10},{6,14},... | collective-permute-start | bytes 24584 | tf_op jit(solution)/shard_map/ppermute | solution.py:173

commit v2 on v1

--- a/solution.py
+++ b/solution.py
@@ -119,6 +119,9 @@
             pltpu.VMEM((2, rows, step), bf16),
         ],
         compiler_params=pltpu.CompilerParams(vmem_limit_bytes=40 << 20),
+        cost_estimate=pl.CostEstimate(
+            flops=2 * 3 * rows * cols * DEPTH, bytes_accessed=2 * rows * cols, transcendentals=rows * cols
+        ),
         name="tile",
     )(delta, norm, *arrays)
 
@@ -141,8 +144,27 @@
         in_specs=[vmem],
         out_specs=vmem,
         compiler_params=pltpu.CompilerParams(vmem_limit_bytes=40 << 20),
+        cost_estimate=pl.CostEstimate(
+            flops=4 * delta.size, bytes_accessed=2 * delta.size, transcendentals=0
+        ),
         name="norm",
     )(delta)
+
+
+def stress_body(mine_ref, other_ref, out_ref):
+    total = mine_ref[...] + other_ref[...]
+    out_ref[0] = jnp.sum(total[:8]) / jnp.sum(total[8:])
+
+
+def stress_call(mine, other):
+    vmem = pl.BlockSpec(memory_space=pltpu.VMEM)
+    return pl.pallas_call(
+        stress_body,
+        out_shape=jax.ShapeDtypeStruct((1,), f32),
+        in_specs=[vmem] * 2,
+        out_specs=pl.BlockSpec(memory_space=pltpu.SMEM),
+        name="stress",
+    )(mine, other)
 
 
 class Grid:
@@ -208,7 +230,7 @@
         elif len(steps) > 1:
             rest = (grid.x ^ (grid.z // 2)) & (2 * bit - 1)
             got = jnp.where(rest == bit, got, current)
-    return got, grid.other_core(got)
+    return got
 
 
 def load_first(narrow, refs, row_pts, col_pts):
@@ -250,34 +272,48 @@
     cols = dissimilarity.shape[1]
     scale = 1.0 / (cols * grid.wide)
     own = config.T
-    got, passed = first_columns(grid, own)
-    norm = norm_call(dissimilarity)
-
-    keep, send = tile_call(functools.partial(load_first, grid.narrow), scale, False, dims, dissimilarity, norm, own, got, passed)
-    for iteration in range(1, ITERS + 1):
-        last = iteration == ITERS
+    got = first_columns(grid, own)
+    got, norm = lax.optimization_barrier((got, norm_call(dissimilarity)))
+    passed = grid.other_core(got)
+
+    keep, send = tile_call(
+        functools.partial(load_first, grid.narrow), scale, False, dims, dissimilarity, norm, own, got, passed
+    )
+    for iteration in range(1, ITERS):
         half = keep + grid.other_core(send)
         for bit in bits(grid.narrow):
             half = half + grid.across(half, "narrow", bit)
-        part = half[:, :cols]
-        first = grid.send(part, grid.spread(True))
-        second = grid.send(part, grid.spread(False))
-        if last:
-            break
-        other = grid.other_core(part)
-        load = functools.partial(load_next, grid.narrow)
+        first = grid.send(half, grid.spread(True))
+        second = grid.send(half, grid.spread(False))
+        other = grid.other_core(half)
         keep, send = tile_call(
-            load, scale, iteration + 1 == ITERS, dims, dissimilarity, norm, part, other, first, second
+            functools.partial(load_next, grid.narrow),
+            scale, iteration + 1 == ITERS, dims, dissimilarity, norm, half, other, first, second
         )
+
+    half = keep + grid.other_core(send)
+    early = []
+    if grid.wide == 4:
+        sums = half[:SUMS, cols:]
+        early = [grid.send(sums, lambda x, a, z: (x, a, z ^ 2)), grid.send(sums, lambda x, a, z: (x ^ 1, a, z ^ 2))]
+    for bit in bits(grid.narrow):
+        half = half + grid.across(half, "narrow", bit)
     sums = half[:SUMS, cols:]
-    for bit in bits(grid.wide):
-        sums = sums + grid.across(sums, "wide", bit)
+    for part in early:
+        sums = sums + part
+    if not early:
+        for bit in bits(grid.wide)[1:]:
+            sums = sums + grid.across(sums, "wide", bit)
+    half = half[:, :cols]
+    first = grid.send(half, grid.spread(True))
+    second = grid.send(half, grid.spread(False))
+    stress = stress_call(sums, grid.across(sums, "wide", 1))
+    first, second, stress = lax.optimization_barrier((first, second, stress))
     in_order = grid.spread_half() == 0
     embedding = jnp.where(
         in_order, jnp.concatenate([first, second], axis=0), jnp.concatenate([second, first], axis=0)
     )
-    stress = jnp.sum(sums[:8]) / jnp.sum(sums[8:])
-    return embedding.T, stress.reshape(1)
+    return embedding.T, stress
 
 
 def solution(mesh):

time: 64.7 us -> 56.9 us (0.88)
  waiting for transfers between devices: 31.1 us -> 25.3 us
  between operations: 3.19 us -> 0.77 us
  Pallas kernels: 8.07 us -> 9.47 us
  starting transfers between devices: 18.4 us -> 17.5 us
    ppermute x4 -> x3, waiting for transfers between devices: 17 us -> 12 us  [across(): lax.ppermute(value, axis, [(i, i ^ bit) for i in range(lax.axis_size(axis...]
    ppermute x4 -> x3, starting transfers between devices: 9.42 us -> 6.11 us  [across(): lax.ppermute(value, axis, [(i, i ^ bit) for i in range(lax.axis_size(axis...]
    ppermute x5 -> x7, starting transfers between devices: 8.25 us -> 10.9 us  [send(): return lax.ppermute(value, AXES, self.pairs(source))]
    ppermute x5 -> x7, waiting for transfers between devices: 11.7 us -> 9.09 us  [send(): return lax.ppermute(value, AXES, self.pairs(source))]
    ppermute x4, waiting for transfers between devices: 2.44 us -> 4.17 us  [other_core(): return lax.ppermute(value, 'aux', [(0, 1), (1, 0)])]
    pallas_call x0 -> x1, Pallas kernels: none -> 1.39 us  [stress_call(): pl.pallas_call(stress_body, out_shape=jax.ShapeDtypeStruct((1,), f32), in...]
    unnamed x4 -> x8, local copies, waits for them, and re-layouts: 2.25 us -> 2.53 us
  transfers between devices with their start and end apart: 13 -> 14, of which waited for: 9 -> 9; matrix products, arithmetic and copies ran while one was open for 1% -> 0% of each run, Pallas kernels for 1% -> 4%
where the time goes in v2:
time: 56.9 us; the launch traced here: 56.4 us
  waiting for transfers between devices  25.3 us (44%)
  starting transfers between devices  17.5 us (31%)
  Pallas kernels  9.47 us (17%)
  local copies, waits for them, and re-layouts  2.54 us (4%)
  other arithmetic  0.83 us (1%)
  between operations  0.77 us (1%)
    ppermute x3, waiting for transfers between devices, across(): lax.ppermute(value, axis, [(i, i ^ bit) for i in range(lax.axis_size(axis...  12 us
    ppermute x7, starting transfers between devices, send(): return lax.ppermute(value, AXES, self.pairs(source))  10.9 us
    ppermute x7, waiting for transfers between devices, send(): return lax.ppermute(value, AXES, self.pairs(source))  9.09 us
    pallas_call x2, Pallas kernels, tile_call(): pl.pallas_call(functools.partial(tile_body, scale, stress, step, step, lo...  7.44 us
    ppermute x3, starting transfers between devices, across(): lax.ppermute(value, axis, [(i, i ^ bit) for i in range(lax.axis_size(axis...  6.11 us
    ppermute x4, waiting for transfers between devices, other_core(): return lax.ppermute(value, 'aux', [(0, 1), (1, 0)])  4.17 us
    unnamed x8, local copies, waits for them, and re-layouts  2.53 us
    pallas_call x1, Pallas kernels, stress_call(): pl.pallas_call(stress_body, out_shape=jax.ShapeDtypeStruct((1,), f32), in...  1.39 us
  transfers between devices with their start and end apart: 14, of which 9 were waited for; matrix products, arithmetic and copies ran while one was open for 0% of the time, Pallas kernels for 4%

profile of v2, /device:TPU:0, one launch (start us, length us, event | category | flops | bytes accessed | tf_op | source)
XLA Modules:
  0.0 56.4 jit_solution(9304929394661443371)
XLA Ops:
  0.6 3.0 %collective-permute-start = (f32[64,1280]{1,0:T(8,128)}, f32[64,1280]{1,0:T(8,128)S(1)}, u32[]{:S(2)}, u32[]{:S(2)}) collective-permute-start(f32[64,1280]{1,0:T(8,128)} %bitcast.3), channel_id=1, source_target_pairs={{2,0},{4,1},{0,2},{6,3},{1,4},{7,5},{3,6},{5,7},{10,8},{12,9},{8,1... | collective-permute-start | bytes 983048 | tf_op jit(solution)/shard_map/ppermute | solution.py:189
  3.6 1.9 %copy-done = bf16[1280,1280]{1,0:T(8,128)(2,1)S(1)} copy-done((bf16[1280,1280]{1,0:T(8,128)(2,1)S(1)}, bf16[1280,1280]{1,0:T(8,128)(2,1)}, u32[]{:S(2)}) %copy-start) | copy-done | bytes 3276824
  5.6 0.6 %norm.1.norm_ref = f32[8,128]{1,0:T(8,128)S(1)} custom-call(bf16[1280,1280]{1,0:T(8,128)(2,1)S(1)} %copy-done), custom_call_target="tpu_custom_call" | custom-call | flops 6553600 | bytes 3276800 | tf_op jit(solution)/shard_map/norm/pallas_call | solution.py:141
  6.2 2.7 %collective-permute-done.refs_1_ = f32[64,1280]{1,0:T(8,128)S(1)} collective-permute-done((f32[64,1280]{1,0:T(8,128)}, f32[64,1280]{1,0:T(8,128)S(1)}, u32[]{:S(2)}, u32[]{:S(2)}) %collective-permute-start) | collective-permute-done | bytes 327712 | tf_op jit(solution)/shard_map/ppermute | solution.py:189
  9.0 1.5 %collective-permute-done.1.refs_2_ = f32[64,1280]{1,0:T(8,128)S(1)} collective-permute-done((f32[64,1280]{1,0:T(8,128)S(1)}, f32[64,1280]{1,0:T(8,128)S(1)}, u32[]{:S(2)}, u32[]{:S(2)}) %collective-permute-start.1) | collective-permute-done | bytes 327712 | tf_op jit(solution)/shard_map/ppermute | solution.py:192
  10.5 3.2 %tile.2 = (f32[32,1280]{1,0:T(8,128)S(1)}, f32[32,1280]{1,0:T(8,128)S(1)}) custom-call(bf16[1280,1280]{1,0:T(8,128)(2,1)S(1)} %copy-done, f32[8,128]{1,0:T(8,128)S(1)} %norm.1.norm_ref, f32[64,1280]{1,0:T(8,128)S(1)} %bitcast.4, f32[64,1280]{1,0:T(8,128)S(1)} %collective-permute-done.refs_1_, f32[64,1280]{1,0:T(8,128)S(1)} %collective-permute-done.1.refs_2_), custom_call_target="tpu_custom_call" | custom-call | flops 2516582400 | bytes 3276800 | tf_op jit(solution)/shard_map/tile/pallas_call | solution.py:106
  13.9 1.3 %collective-permute-done.2 = f32[32,1280]{1,0:T(8,128)S(1)} collective-permute-done((f32[32,1280]{1,0:T(8,128)S(1)}, f32[32,1280]{1,0:T(8,128)S(1)}, u32[]{:S(2)}, u32[]{:S(2)}) %collective-permute-start.2) | collective-permute-done | bytes 163872 | tf_op jit(solution)/shard_map/ppermute | solution.py:192
  15.2 2.1 %collective-permute-start.3 = (f32[32,1280]{1,0:T(8,128)S(1)}, f32[32,1280]{1,0:T(8,128)S(1)}, u32[]{:S(2)}, u32[]{:S(2)}) collective-permute-start(f32[32,1280]{1,0:T(8,128)S(1)} %add.23), channel_id=1, source_target_pairs={{0,2},{2,0},{1,3},{3,1},{4,6},{6,4},{5,7},{7,5},{8,10},{10,8},{9,1... | collective-permute-start | bytes 491528 | tf_op jit(solution)/shard_map/ppermute | solution.py:195
  17.3 4.5 %collective-permute-done.3 = f32[32,1280]{1,0:T(8,128)S(1)} collective-permute-done((f32[32,1280]{1,0:T(8,128)S(1)}, f32[32,1280]{1,0:T(8,128)S(1)}, u32[]{:S(2)}, u32[]{:S(2)}) %collective-permute-start.3) | collective-permute-done | bytes 163872 | tf_op jit(solution)/shard_map/ppermute | solution.py:195
  21.9 2.9 %collective-permute-start.5 = (f32[32,1280]{1,0:T(8,128)S(1)}, f32[32,1280]{1,0:T(8,128)S(1)}, u32[]{:S(2)}, u32[]{:S(2)}) collective-permute-start(f32[32,1280]{1,0:T(8,128)S(1)} %add.24.refs_0_), channel_id=1, source_target_pairs={{1,0},{6,1},{10,2},{13,3},{3,4},{4,5},{8,6},{15,7},{0,8},{7,9},{11... | collective-permute-start | bytes 491528 | tf_op jit(solution)/shard_map/ppermute | solution.py:189
  24.8 4.4 %collective-permute-done.5.refs_2_ = f32[32,1280]{1,0:T(8,128)S(1)} collective-permute-done((f32[32,1280]{1,0:T(8,128)S(1)}, f32[32,1280]{1,0:T(8,128)S(1)}, u32[]{:S(2)}, u32[]{:S(2)}) %collective-permute-start.5) | collective-permute-done | bytes 163872 | tf_op jit(solution)/shard_map/ppermute | solution.py:189
  29.2 2.0 %collective-permute-done.6.refs_3_ = f32[32,1280]{1,0:T(8,128)S(1)} collective-permute-done((f32[32,1280]{1,0:T(8,128)S(1)}, f32[32,1280]{1,0:T(8,128)S(1)}, u32[]{:S(2)}, u32[]{:S(2)}) %collective-permute-start.6) | collective-permute-done | bytes 163872 | tf_op jit(solution)/shard_map/ppermute | solution.py:189
  31.2 4.3 %tile.3 = (f32[32,1408]{1,0:T(8,128)S(1)}, f32[32,1408]{1,0:T(8,128)S(1)}) custom-call(bf16[1280,1280]{1,0:T(8,128)(2,1)S(1)} %copy-done, f32[8,128]{1,0:T(8,128)S(1)} %norm.1.norm_ref, f32[32,1280]{1,0:T(8,128)S(1)} %add.24.refs_0_, f32[32,1280]{1,0:T(8,128)S(1)} %collective-permute-done.4.refs_1_, f32[32,1280]{1,0:T(8,128)S(1)} %collective-permute-done.5.refs_2_, ...), custom_call_target="tpu_custom_call" | custom-call | flops 2516582400 | bytes 3276800 | tf_op jit(solution)/shard_map/tile/pallas_call | solution.py:106
  35.5 1.4 %collective-permute-done.7 = f32[32,1408]{1,0:T(8,128)S(1)} collective-permute-done((f32[32,1408]{1,0:T(8,128)S(1)}, f32[32,1408]{1,0:T(8,128)S(1)}, u32[]{:S(2)}, u32[]{:S(2)}) %collective-permute-start.7) | collective-permute-done | bytes 180256 | tf_op jit(solution)/shard_map/ppermute | solution.py:192
  37.0 4.0 %collective-permute-start.8 = (f32[32,1408]{1,0:T(8,128)S(1)}, f32[32,1408]{1,0:T(8,128)S(1)}, u32[]{:S(2)}, u32[]{:S(2)}) collective-permute-start(f32[32,1408]{1,0:T(8,128)S(1)} %add.25), channel_id=1, source_target_pairs={{0,2},{2,0},{1,3},{3,1},{4,6},{6,4},{5,7},{7,5},{8,10},{10,8},{9,1... | collective-permute-start | bytes 540680 | tf_op jit(solution)/shard_map/ppermute | solution.py:195
  40.9 0.3 collective-permute-start.11
  41.3 2.1 %collective-permute-start.12 = (f32[16,128]{1,0:T(8,128)S(1)}, f32[16,128]{1,0:T(8,128)S(1)}, u32[]{:S(2)}, u32[]{:S(2)}) collective-permute-start(f32[16,128]{1,0:T(8,128)S(1)} %slice.14), channel_id=1, source_target_pairs={{10,0},{11,1},{8,2},{9,3},{14,4},{15,5},{12,6},{13,7},{2,8},{3,9},... | collective-permute-start | bytes 24584 | tf_op jit(solution)/shard_map/ppermute | solution.py:189
  43.4 2.4 %collective-permute-done.8 = f32[32,1408]{1,0:T(8,128)S(1)} collective-permute-done((f32[32,1408]{1,0:T(8,128)S(1)}, f32[32,1408]{1,0:T(8,128)S(1)}, u32[]{:S(2)}, u32[]{:S(2)}) %collective-permute-start.8) | collective-permute-done | bytes 180256 | tf_op jit(solution)/shard_map/ppermute | solution.py:195
  45.8 1.2 %collective-permute-start.10 = (f32[32,1280]{1,0:T(8,128)S(1)}, f32[32,1280]{1,0:T(8,128)S(1)}, u32[]{:S(2)}, u32[]{:S(2)}) collective-permute-start(f32[32,1280]{1,0:T(8,128)S(1)} %slice.12), channel_id=1, source_target_pairs={{2,0},{5,1},{11,2},{12,3},{0,4},{7,5},{9,6},{14,7},{1,8},{6,9},{8,... | collective-permute-start | bytes 491528 | tf_op jit(solution)/shard_map/ppermute | solution.py:189
  47.1 1.3 %collective-permute-start.9 = (f32[32,1280]{1,0:T(8,128)S(1)}, f32[32,1280]{1,0:T(8,128)S(1)}, u32[]{:S(2)}, u32[]{:S(2)}) collective-permute-start(f32[32,1280]{1,0:T(8,128)S(1)} %slice.12), channel_id=1, source_target_pairs={{1,0},{6,1},{10,2},{13,3},{3,4},{4,5},{8,6},{15,7},{0,8},{7,9},{11... | collective-permute-start | bytes 491528 | tf_op jit(solution)/shard_map/ppermute | solution.py:189
  48.5 5.1 %collective-permute-done.13.other_ref = f32[16,128]{1,0:T(8,128)S(1)} collective-permute-done((f32[16,128]{1,0:T(8,128)S(1)}, f32[16,128]{1,0:T(8,128)S(1)}, u32[]{:S(2)}, u32[]{:S(2)}) %collective-permute-start.13) | collective-permute-done | bytes 8224 | tf_op jit(solution)/shard_map/ppermute | solution.py:195
  53.6 0.6 %copy-done.3 = f32[16,128]{1,0:T(8,128)} copy-done((f32[16,128]{1,0:T(8,128)}, f32[16,128]{1,0:T(8,128)S(1)}, u32[]{:S(2)}) %copy-start.3) | copy-done | bytes 8216
  54.2 1.4 %stress.1 = f32[1]{0:T(128)} custom-call(f32[16,128]{1,0:T(8,128)} %copy-done.2, f32[16,128]{1,0:T(8,128)} %copy-done.3), custom_call_target="tpu_custom_call" | custom-call | tf_op jit(solution)/shard_map/stress/pallas_call | solution.py:161
  55.6 0.7 %fusion = f32[1280,64]{0,1:T(8,128)} fusion(f32[32,1280]{1,0:T(8,128)S(1)} %collective-permute-done.10, f32[32,1280]{1,0:T(8,128)S(1)} %collective-permute-done.9, pred[]{:T(512)S(6)} %eq.3), kind=kLoop, calls=%fused_computation.1 | loop fusion | flops 245760 | bytes 655361 | tf_op jit(solution)/shard_map/transpose | solution.py:316
  (24 shorter events, 0.7 us)
Async XLA Ops:
  0.6 8.3 %collective-permute-start = (f32[64,1280]{1,0:T(8,128)}, f32[64,1280]{1,0:T(8,128)S(1)}, u32[]{:S(2)}, u32[]{:S(2)}) collective-permute-start(f32[64,1280]{1,0:T(8,128)} %bitcast.3), channel_id=1, source_target_pairs={{2,0},{4,1},{0,2},{6,3},{1,4},{7,5},{3,6},{5,7},{10,8},{12,9},{8,1... | collective-permute-start | bytes 983048 | tf_op jit(solution)/shard_map/ppermute | solution.py:189
  3.6 1.9 %copy-start = (bf16[1280,1280]{1,0:T(8,128)(2,1)S(1)}, bf16[1280,1280]{1,0:T(8,128)(2,1)}, u32[]{:S(2)}) copy-start(bf16[1280,1280]{1,0:T(8,128)(2,1)} %delta_ref.5) | copy-start | bytes 9830404
  5.6 5.0 %copy-start.1 = (f32[1280,64]{0,1:T(8,128)S(1)}, f32[1280,64]{0,1:T(8,128)}, u32[]{:S(2)}) copy-start(f32[1280,64]{0,1:T(8,128)} %param.3) | copy-start | bytes 983044
  8.9 1.6 %collective-permute-start.1 = (f32[64,1280]{1,0:T(8,128)S(1)}, f32[64,1280]{1,0:T(8,128)S(1)}, u32[]{:S(2)}, u32[]{:S(2)}) collective-permute-start(f32[64,1280]{1,0:T(8,128)S(1)} %collective-permute-done.refs_1_), channel_id=1, source_target_pairs={{0,1},{1,0},{2,3},{3,2},{4,5},{5,4},{6,7},{7,6},{8,9},{9,8},{10,11... | collective-permute-start | bytes 983048 | tf_op jit(solution)/shard_map/ppermute | solution.py:192
  13.7 1.5 %collective-permute-start.2 = (f32[32,1280]{1,0:T(8,128)S(1)}, f32[32,1280]{1,0:T(8,128)S(1)}, u32[]{:S(2)}, u32[]{:S(2)}) collective-permute-start(f32[32,1280]{1,0:T(8,128)S(1)} %get-tuple-element.14), channel_id=1, source_target_pairs={{0,1},{1,0},{2,3},{3,2},{4,5},{5,4},{6,7},{7,6},{8,9},{9,8},{10,11... | collective-permute-start | bytes 491528 | tf_op jit(solution)/shard_map/ppermute | solution.py:192
  15.2 6.6 %collective-permute-start.3 = (f32[32,1280]{1,0:T(8,128)S(1)}, f32[32,1280]{1,0:T(8,128)S(1)}, u32[]{:S(2)}, u32[]{:S(2)}) collective-permute-start(f32[32,1280]{1,0:T(8,128)S(1)} %add.23), channel_id=1, source_target_pairs={{0,2},{2,0},{1,3},{3,1},{4,6},{6,4},{5,7},{7,5},{8,10},{10,8},{9,1... | collective-permute-start | bytes 491528 | tf_op jit(solution)/shard_map/ppermute | solution.py:195
  21.8 3.0 %collective-permute-start.4 = (f32[32,1280]{1,0:T(8,128)S(1)}, f32[32,1280]{1,0:T(8,128)S(1)}, u32[]{:S(2)}, u32[]{:S(2)}) collective-permute-start(f32[32,1280]{1,0:T(8,128)S(1)} %add.24.refs_0_), channel_id=1, source_target_pairs={{0,1},{1,0},{2,3},{3,2},{4,5},{5,4},{6,7},{7,6},{8,9},{9,8},{10,11... | collective-permute-start | bytes 491528 | tf_op jit(solution)/shard_map/ppermute | solution.py:192
  21.9 7.3 %collective-permute-start.5 = (f32[32,1280]{1,0:T(8,128)S(1)}, f32[32,1280]{1,0:T(8,128)S(1)}, u32[]{:S(2)}, u32[]{:S(2)}) collective-permute-start(f32[32,1280]{1,0:T(8,128)S(1)} %add.24.refs_0_), channel_id=1, source_target_pairs={{1,0},{6,1},{10,2},{13,3},{3,4},{4,5},{8,6},{15,7},{0,8},{7,9},{11... | collective-permute-start | bytes 491528 | tf_op jit(solution)/shard_map/ppermute | solution.py:189
  24.8 6.4 %collective-permute-start.6 = (f32[32,1280]{1,0:T(8,128)S(1)}, f32[32,1280]{1,0:T(8,128)S(1)}, u32[]{:S(2)}, u32[]{:S(2)}) collective-permute-start(f32[32,1280]{1,0:T(8,128)S(1)} %add.24.refs_0_), channel_id=1, source_target_pairs={{2,0},{5,1},{11,2},{12,3},{0,4},{7,5},{9,6},{14,7},{1,8},{6,9},{8,... | collective-permute-start | bytes 491528 | tf_op jit(solution)/shard_map/ppermute | solution.py:189
  35.5 1.5 %collective-permute-start.7 = (f32[32,1408]{1,0:T(8,128)S(1)}, f32[32,1408]{1,0:T(8,128)S(1)}, u32[]{:S(2)}, u32[]{:S(2)}) collective-permute-start(f32[32,1408]{1,0:T(8,128)S(1)} %get-tuple-element.16), channel_id=1, source_target_pairs={{0,1},{1,0},{2,3},{3,2},{4,5},{5,4},{6,7},{7,6},{8,9},{9,8},{10,11... | collective-permute-start | bytes 540680 | tf_op jit(solution)/shard_map/ppermute | solution.py:192
  37.0 8.8 %collective-permute-start.8 = (f32[32,1408]{1,0:T(8,128)S(1)}, f32[32,1408]{1,0:T(8,128)S(1)}, u32[]{:S(2)}, u32[]{:S(2)}) collective-permute-start(f32[32,1408]{1,0:T(8,128)S(1)} %add.25), channel_id=1, source_target_pairs={{0,2},{2,0},{1,3},{3,1},{4,6},{6,4},{5,7},{7,5},{8,10},{10,8},{9,1... | collective-permute-start | bytes 540680 | tf_op jit(solution)/shard_map/ppermute | solution.py:195
  40.9 7.5 %collective-permute-start.11 = (f32[16,128]{1,0:T(8,128)S(1)}, f32[16,128]{1,0:T(8,128)S(1)}, u32[]{:S(2)}, u32[]{:S(2)}) collective-permute-start(f32[16,128]{1,0:T(8,128)S(1)} %slice.14), channel_id=1, source_target_pairs={{8,0},{9,1},{10,2},{11,3},{12,4},{13,5},{14,6},{15,7},{0,8},{1,9},... | collective-permute-start | bytes 24584 | tf_op jit(solution)/shard_map/ppermute | solution.py:189
  41.3 7.1 %collective-permute-start.12 = (f32[16,128]{1,0:T(8,128)S(1)}, f32[16,128]{1,0:T(8,128)S(1)}, u32[]{:S(2)}, u32[]{:S(2)}) collective-permute-start(f32[16,128]{1,0:T(8,128)S(1)} %slice.14), channel_id=1, source_target_pairs={{10,0},{11,1},{8,2},{9,3},{14,4},{15,5},{12,6},{13,7},{2,8},{3,9},... | collective-permute-start | bytes 24584 | tf_op jit(solution)/shard_map/ppermute | solution.py:189
  45.8 9.8 %collective-permute-start.10 = (f32[32,1280]{1,0:T(8,128)S(1)}, f32[32,1280]{1,0:T(8,128)S(1)}, u32[]{:S(2)}, u32[]{:S(2)}) collective-permute-start(f32[32,1280]{1,0:T(8,128)S(1)} %slice.12), channel_id=1, source_target_pairs={{2,0},{5,1},{11,2},{12,3},{0,4},{7,5},{9,6},{14,7},{1,8},{6,9},{8,... | collective-permute-start | bytes 491528 | tf_op jit(solution)/shard_map/ppermute | solution.py:189
  47.1 8.5 %collective-permute-start.9 = (f32[32,1280]{1,0:T(8,128)S(1)}, f32[32,1280]{1,0:T(8,128)S(1)}, u32[]{:S(2)}, u32[]{:S(2)}) collective-permute-start(f32[32,1280]{1,0:T(8,128)S(1)} %slice.12), channel_id=1, source_target_pairs={{1,0},{6,1},{10,2},{13,3},{3,4},{4,5},{8,6},{15,7},{0,8},{7,9},{11... | collective-permute-start | bytes 491528 | tf_op jit(solution)/shard_map/ppermute | solution.py:189
  48.4 5.2 %copy-start.2 = (f32[16,128]{1,0:T(8,128)}, f32[16,128]{1,0:T(8,128)S(1)}, u32[]{:S(2)}) copy-start(f32[16,128]{1,0:T(8,128)S(1)} %fusion.1.mine_ref) | copy-start | bytes 24580
  48.4 5.2 %collective-permute-start.13 = (f32[16,128]{1,0:T(8,128)S(1)}, f32[16,128]{1,0:T(8,128)S(1)}, u32[]{:S(2)}, u32[]{:S(2)}) collective-permute-start(f32[16,128]{1,0:T(8,128)S(1)} %fusion.1.mine_ref), channel_id=1, source_target_pairs={{0,4},{4,0},{8,12},{12,8},{1,5},{5,1},{9,13},{13,9},{2,6},{6,2},{1... | collective-permute-start | bytes 24584 | tf_op jit(solution)/shard_map/ppermute | solution.py:195
  53.6 0.6 %copy-start.3 = (f32[16,128]{1,0:T(8,128)}, f32[16,128]{1,0:T(8,128)S(1)}, u32[]{:S(2)}) copy-start(f32[16,128]{1,0:T(8,128)S(1)} %collective-permute-done.13.other_ref) | copy-start | bytes 24580

commit v3 on v2

v3 whole, which is shorter than its diff:
```python
import functools

import jax
import jax.numpy as jnp
from jax import lax
from jax.experimental import pallas as pl
from jax.experimental.pallas import tpu as pltpu
from jax.sharding import PartitionSpec as P

FLOOR = 3.0
TINY = 1e-30
DEPTH = 256
LANES = 128
EXTRA = 16
PIECE = 32
SUMS = 16

f32 = jnp.float32
bf16 = jnp.bfloat16
AXES = ("wide", "narrow", "aux")


def split2(values):
    high = values.astype(bf16)
    return high, (values - high.astype(f32)).astype(bf16)


def split3(values):
    high = values.astype(bf16)
    rest = values - high.astype(f32)
    middle = rest.astype(bf16)
    return high, middle, (rest - middle.astype(f32)).astype(bf16)


def norm_rows(points, first):
    count = points.shape[1]
    squares = jnp.sum(points * points, axis=0, keepdims=True)
    row = lax.broadcasted_iota(jnp.int32, (EXTRA, count), 0)
    ones = 3 if first else 0
    parts = 0 if first else 3
    rows = jnp.where((row >= ones) & (row < ones + 3), 1.0, 0.0)
    for k, part in enumerate(split3(squares)):
        rows = jnp.where(row == parts + k, part.astype(f32), rows)
    return rows.astype(bf16)


def tile_terms(row_pts, col_pts, delta_at, lhs, rhs, left, square, r_high, r_low, stress, emit):
    dims, rows = row_pts.shape
    cols = col_pts.shape[1]
    step = r_high.shape[2]
    points = row_pts[...]
    shift = jnp.sum(points, axis=1, keepdims=True) * (1.0 / rows)
    points = points - shift
    high, middle = split2(points)
    minus2 = lambda v: (v.astype(f32) * -2.0).astype(bf16)
    fill = DEPTH - 3 * dims - EXTRA
    lhs[...] = jnp.concatenate(
        [minus2(high), minus2(high), minus2(middle), norm_rows(points, True), jnp.zeros((fill, rows), bf16)], axis=0
    ).T
    left[...] = jnp.concatenate([high, middle, jnp.ones((EXTRA, rows), bf16)], axis=0)
    points = col_pts[...] - shift
    col_pts[...] = points
    high, middle = split2(points)
    rhs[...] = jnp.concatenate(
        [high, middle, high, norm_rows(points, False), jnp.zeros((fill, cols), bf16)], axis=0
    )

    def gram(c):
        square[c % 2] = jnp.dot(lhs[...], rhs[:, c * step:(c + 1) * step], preferred_element_type=f32)

    misfit = [jnp.zeros((16, step), f32)] * 2
    gram(0)
    for c in range(cols // step):
        if (c + 1) * step < cols:
            gram(c + 1)
        js = pl.ds(c * step, step)
        slot = c % 2
        for p in range(rows // PIECE):
            ps = pl.ds(p * PIECE, PIECE)
            squared = square[slot, ps, :]
            delta = delta_at(p * PIECE, js).astype(f32)
            above = c - p * PIECE // step
            if stress and above >= 0:
                inverse = lax.rsqrt(jnp.maximum(squared, TINY))
                ratio = delta * jnp.minimum(inverse, 1.0 / FLOOR)
                gap = delta - jnp.maximum(squared, 0.0) * inverse
                gap = gap * gap
                for q in range(0, PIECE, 16):
                    misfit[above > 0] = misfit[above > 0] + gap[q:q + 16]
            else:
                ratio = delta * lax.rsqrt(jnp.maximum(squared, FLOOR * FLOOR))
            high, low = split2(ratio)
            r_high[slot, ps, :] = high
            r_low[slot, ps, :] = low
        terms = jnp.dot(left[...], r_high[slot], preferred_element_type=f32)
        terms = terms + jnp.dot(left[...], r_low[slot], preferred_element_type=f32)
        cross = terms[:dims] + terms[dims:2 * dims]
        emit(js, col_pts[:, js] * terms[2 * dims:2 * dims + 1] - cross)
    return jnp.sum(misfit[0] + 2.0 * misfit[1]) if stress else None


def tile_scratch(dims, rows, cols):
    step = 256 if cols % 256 == 0 else 128
    return [
        pltpu.VMEM((dims, rows), f32),
        pltpu.VMEM((dims, cols), f32),
        pltpu.VMEM((rows, DEPTH), bf16),
        pltpu.VMEM((DEPTH, cols), bf16),
        pltpu.VMEM((2 * dims + EXTRA, rows), bf16),
        pltpu.VMEM((2, rows, step), f32),
        pltpu.VMEM((2, rows, step), bf16),
        pltpu.VMEM((2, rows, step), bf16),
    ]


def call(body, name, outs, scratch, cost, *arrays):
    vmem = pl.BlockSpec(memory_space=pltpu.VMEM)
    flops, size, roots = cost
    return pl.pallas_call(
        body,
        out_shape=[jax.ShapeDtypeStruct(shape, f32) for shape in outs],
        in_specs=[vmem] * len(arrays),
        out_specs=[vmem] * len(outs),
        scratch_shapes=scratch,
        compiler_params=pltpu.CompilerParams(vmem_limit_bytes=40 << 20),
        cost_estimate=pl.CostEstimate(flops=flops, bytes_accessed=size, transcendentals=roots),
        name=name,
    )(*arrays)


def tile_cost(rows, cols):
    return 2 * 3 * rows * cols * DEPTH, 2 * rows * cols, rows * cols


def first_tile(narrow, scale, delta, own, got, passed):
    dims, rows = own.shape
    cols = delta.shape[1]
    half = dims // 2

    def body(delta_ref, own_ref, got_ref, passed_ref, keep_ref, send_ref, result, row_pts, col_pts, *rest):
        x, a, z = (lax.axis_index(n) for n in ("narrow", "aux", "wide"))
        home = (x == z // 2) & (narrow == 2)
        core = a == z % 2
        row_pts[...] = own_ref[...]

        @pl.when(home & core)
        def _():
            col_pts[...] = own_ref[...]

        @pl.when(home != core)
        def _():
            col_pts[...] = got_ref[...]

        @pl.when(jnp.logical_not(home | core))
        def _():
            col_pts[...] = passed_ref[...]

        def emit(js, part):
            result[:, js] = part * scale

        tile_terms(row_pts, col_pts, lambda p, js: delta_ref[pl.ds(p, PIECE), js], *rest, False, emit)
        for ref, which in ((keep_ref, a), (send_ref, 1 - a)):
            ref[...] = result[pl.ds(pl.multiple_of(which * half, 8), half), :]

    scratch = [pltpu.VMEM((dims, cols), f32)] + tile_scratch(dims, rows, cols)
    outs = [(half, cols)] * 2
    return call(body, "tile_first", outs, scratch, tile_cost(rows, cols), delta, own, got, passed)


def next_tile(side_of, scale, delta, kept, passed, first, second, norm):
    half, rows = first.shape
    dims = 2 * half
    cols = delta.shape[1]

    def body(delta_ref, kept_ref, passed_ref, first_ref, second_ref, norm_ref, keep_ref, send_ref, result, *rest):
        row_pts, col_pts, *rest = rest
        a = lax.axis_index("aux")
        at = lambda which: pl.ds(pl.multiple_of(which * half, 8), half)
        side = side_of()
        col_pts[at(a), :] = kept_ref[...]
        col_pts[at(1 - a), :] = passed_ref[...]
        row_pts[at(side), :] = first_ref[...]
        row_pts[at(1 - side), :] = second_ref[...]

        def emit(js, part):
            result[:, js] = part * scale

        misfit = tile_terms(row_pts, col_pts, lambda p, js: delta_ref[pl.ds(p, PIECE), js], *rest, True, emit)
        for ref, which in ((keep_ref, a), (send_ref, 1 - a)):
            ref[:, :cols] = result[at(which), :]
            ref[:8, cols:] = jnp.full((8, LANES), misfit)
            ref[8:16, cols:] = norm_ref[...]
            ref[16:, cols:] = jnp.zeros((half - 16, LANES), f32)

    scratch = [pltpu.VMEM((dims, cols), f32)] + tile_scratch(dims, rows, cols)
    outs = [(half, cols + LANES)] * 2
    return call(body, "tile_next", outs, scratch, tile_cost(rows, cols), delta, kept, passed, first, second, norm)


def norm_body(delta_ref, out_ref):
    rows, cols = delta_ref.shape
    total = jnp.zeros((8, LANES), f32)
    for ic in range(rows // LANES):
        for jc in range(cols // LANES):
            part = delta_ref[ic * LANES:(ic + 1) * LANES, jc * LANES:(jc + 1) * LANES].astype(f32)
            total = total + jnp.sum((part * part).reshape(LANES // 8, 8, LANES), axis=0)
    out_ref[...] = jnp.full((8, LANES), jnp.sum(total))


def norm_call(delta):
    return call(norm_body, "norm", [(8, LANES)], [], (4 * delta.size, 2 * delta.size, 0), delta)[0]


class Grid:
    def __init__(self):
        self.narrow = lax.axis_size("narrow")
        self.wide = lax.axis_size("wide")
        assert lax.axis_size("aux") == 2 and self.wide == 2 * self.narrow

    def pairs(self, source):
        place = lambda x, a, z: (z * self.narrow + x) * 2 + a
        return [
            (place(*source(x, a, z)), place(x, a, z))
            for z in range(self.wide)
            for x in range(self.narrow)
            for a in range(2)
        ]

    def send(self, value, source):
        return lax.ppermute(value, AXES, self.pairs(source))

    def other_core(self, value):
        return lax.ppermute(value, "aux", [(0, 1), (1, 0)])

    def across(self, value, axis, bit):
        return lax.ppermute(value, axis, [(i, i ^ bit) for i in range(lax.axis_size(axis))])

    def spread(self, first):
        def source(x, a, z):
            block = 2 * x + a
            offset = z ^ block
            top, low = offset // self.narrow, offset % self.narrow
            if first:
                return x ^ low, a ^ (1 - top), block
            return x ^ low ^ (1 - top), a ^ top, block

        return source

    def spread_half(self):
        x, a, z = (lax.axis_index(n) for n in ("narrow", "aux", "wide"))
        return a ^ 1 ^ ((z ^ (2 * x + a)) >> (self.narrow.bit_length() - 1))


def bits(count):
    return [1 << k for k in range(count.bit_length() - 1)]


def first_columns(grid, own):
    x, a, z = (lax.axis_index(n) for n in ("narrow", "aux", "wide"))
    current = own
    steps = bits(grid.narrow)
    for place, bit in enumerate(reversed(steps)):

        def source(x, a, z):
            return (x ^ bit, a, z) if a == z % 2 else (x, 1 - a, z ^ 1)

        got = grid.send(current, source)
        if place < len(steps) - 1:
            rest = (x ^ (z // 2)) & (2 * bit - 1)
            current = jnp.where((rest == bit) & (a == z % 2), got, current)
        elif len(steps) > 1:
            rest = (x ^ (z // 2)) & (2 * bit - 1)
            got = jnp.where(rest == bit, got, current)
    return got


def shards(dissimilarity, config):
    grid = Grid()
    cols = dissimilarity.shape[1]
    scale = 1.0 / (cols * grid.wide)
    own = config.T
    got = first_columns(grid, own)
    got, norm = lax.optimization_barrier((got, norm_call(dissimilarity)))
    passed = grid.other_core(got)

    keep, send = first_tile(grid.narrow, scale, dissimilarity, own, got, passed)
    half = keep + grid.other_core(send)
    for bit in bits(grid.narrow):
        half = half + grid.across(half, "narrow", bit)
    first = grid.send(half, grid.spread(True))
    second = grid.send(half, grid.spread(False))
    other = grid.other_core(half)
    keep, send = next_tile(grid.spread_half, scale, dissimilarity, half, other, first, second, norm)

    half = keep + grid.other_core(send)
    early = []
    if grid.wide == 4:
        sums = half[:SUMS, cols:]
        early = [grid.send(sums, lambda x, a, z: (x, a, z ^ 2)), grid.send(sums, lambda x, a, z: (x ^ 1, a, z ^ 2))]
    for bit in bits(grid.narrow):
        half = half + grid.across(half, "narrow", bit)
    sums = half[:SUMS, cols:]
    if not early:
        for bit in bits(grid.wide)[1:]:
            sums = sums + grid.across(sums, "wide", bit)
    for part in early:
        sums = sums + part
    half = half[:, :cols]
    first = grid.send(half, grid.spread(True))
    second = grid.send(half, grid.spread(False))
    sums = sums + grid.across(sums, "wide", 1)
    first, second, sums = lax.optimization_barrier((first, second, sums))
    stress = lax.optimization_barrier(sums[:8] / sums[8:])[0, :1]
    in_order = grid.spread_half() == 0
    embedding = jnp.where(
        in_order, jnp.concatenate([first, second], axis=0), jnp.concatenate([second, first], axis=0)
    )
    return embedding.T, stress


def solution(mesh):
    placed = (P(("groups", "narrow", "aux"), "wide"), P(("groups", "narrow", "aux"), None))
    return jax.shard_map(
        shards,
        mesh=mesh,
        in_specs=placed,
        out_specs=(P(("groups", "narrow", "aux"), None), P("groups")),
        check_vma=False,
    )
```

time: 56.9 us -> 55.8 us (0.981)
  the two profiles are of different devices: /device:TPU:0 before, /device:TPU:6 now
where the time goes in v3:
time: 55.8 us; the launch traced here: 55.6 us
  waiting for transfers between devices  31.8 us (57%)
  starting transfers between devices  13 us (23%)
  Pallas kernels  6.88 us (12%)
  local copies, waits for them, and re-layouts  2.46 us (4%)
  other arithmetic  0.84 us (2%)
  between operations  0.72 us (1%)
    ppermute x7, waiting for transfers between devices, send(): return lax.ppermute(value, AXES, self.pairs(source))  15 us
    ppermute x3, waiting for transfers between devices, across(): lax.ppermute(value, axis, [(i, i ^ bit) for i in range(lax.axis_size(axis...  12.4 us
    ppermute x7, starting transfers between devices, send(): return lax.ppermute(value, AXES, self.pairs(source))  11.8 us
    pallas_call x3, Pallas kernels, call(): pl.pallas_call(body, out_shape=[jax.ShapeDtypeStruct(shape, f32) for shap...  6.88 us
    ppermute x4, waiting for transfers between devices, other_core(): return lax.ppermute(value, 'aux', [(0, 1), (1, 0)])  4.29 us
    unnamed x4, local copies, waits for them, and re-layouts  1.93 us
  transfers between devices with their start and end apart: 14, of which 11 were waited for; matrix products, arithmetic and copies ran while one was open for 0% of the time, Pallas kernels for 1%

profile of v3, /device:TPU:6, one launch (start us, length us, event | category | flops | bytes accessed | tf_op | source)
XLA Modules:
  0.0 55.6 jit_solution(12079848895592382203)
XLA Ops:
  0.6 0.6 %collective-permute-start = (f32[64,1280]{1,0:T(8,128)}, f32[64,1280]{1,0:T(8,128)S(1)}, u32[]{:S(2)}, u32[]{:S(2)}) collective-permute-start(f32[64,1280]{1,0:T(8,128)} %bitcast.4), channel_id=1, source_target_pairs={{2,0},{4,1},{0,2},{6,3},{1,4},{7,5},{3,6},{5,7},{10,8},{12,9},{8,1... | collective-permute-start | bytes 983048 | tf_op jit(solution)/shard_map/ppermute | solution.py:230
  1.2 1.9 %copy-done = bf16[1280,1280]{1,0:T(8,128)(2,1)S(1)} copy-done((bf16[1280,1280]{1,0:T(8,128)(2,1)S(1)}, bf16[1280,1280]{1,0:T(8,128)(2,1)}, u32[]{:S(2)}) %copy-start) | copy-done | bytes 3276824
  3.2 0.8 %norm.1.norm_ref = f32[8,128]{1,0:T(8,128)S(1)} custom-call(bf16[1280,1280]{1,0:T(8,128)(2,1)S(1)} %copy-done), custom_call_target="tpu_custom_call" | custom-call | flops 6553600 | bytes 3276800 | tf_op jit(solution)/shard_map/norm/pallas_call | solution.py:119
  3.9 4.1 %collective-permute-done.got_ref = f32[64,1280]{1,0:T(8,128)S(1)} collective-permute-done((f32[64,1280]{1,0:T(8,128)}, f32[64,1280]{1,0:T(8,128)S(1)}, u32[]{:S(2)}, u32[]{:S(2)}) %collective-permute-start) | collective-permute-done | bytes 327712 | tf_op jit(solution)/shard_map/ppermute | solution.py:230
  8.0 1.6 %collective-permute-done.1.passed_ref = f32[64,1280]{1,0:T(8,128)S(1)} collective-permute-done((f32[64,1280]{1,0:T(8,128)S(1)}, f32[64,1280]{1,0:T(8,128)S(1)}, u32[]{:S(2)}, u32[]{:S(2)}) %collective-permute-start.1) | collective-permute-done | bytes 327712 | tf_op jit(solution)/shard_map/ppermute | solution.py:233
  9.6 2.7 %tile_first.1 = (f32[32,1280]{1,0:T(8,128)S(1)}, f32[32,1280]{1,0:T(8,128)S(1)}) custom-call(bf16[1280,1280]{1,0:T(8,128)(2,1)S(1)} %copy-done, f32[64,1280]{1,0:T(8,128)S(1)} %bitcast.5, f32[64,1280]{1,0:T(8,128)S(1)} %collective-permute-done.got_ref, f32[64,1280]{1,0:T(8,128)S(1)} %collective-permute-done.1.passed_ref), custom_call_target="tpu_custom_call" | custom-call | flops 2516582400 | bytes 3276800 | tf_op jit(solution)/shard_map/tile_first/pallas_call | solution.py:119
  12.5 1.3 %collective-permute-done.2 = f32[32,1280]{1,0:T(8,128)S(1)} collective-permute-done((f32[32,1280]{1,0:T(8,128)S(1)}, f32[32,1280]{1,0:T(8,128)S(1)}, u32[]{:S(2)}, u32[]{:S(2)}) %collective-permute-start.2) | collective-permute-done | bytes 163872 | tf_op jit(solution)/shard_map/ppermute | solution.py:233
  13.8 0.6 %collective-permute-start.3 = (f32[32,1280]{1,0:T(8,128)S(1)}, f32[32,1280]{1,0:T(8,128)S(1)}, u32[]{:S(2)}, u32[]{:S(2)}) collective-permute-start(f32[32,1280]{1,0:T(8,128)S(1)} %add.25), channel_id=1, source_target_pairs={{0,2},{2,0},{1,3},{3,1},{4,6},{6,4},{5,7},{7,5},{8,10},{10,8},{9,1... | collective-permute-start | bytes 491528 | tf_op jit(solution)/shard_map/ppermute | solution.py:236
  14.4 5.7 %collective-permute-done.3 = f32[32,1280]{1,0:T(8,128)S(1)} collective-permute-done((f32[32,1280]{1,0:T(8,128)S(1)}, f32[32,1280]{1,0:T(8,128)S(1)}, u32[]{:S(2)}, u32[]{:S(2)}) %collective-permute-start.3) | collective-permute-done | bytes 163872 | tf_op jit(solution)/shard_map/ppermute | solution.py:236
  20.2 3.1 %collective-permute-start.5 = (f32[32,1280]{1,0:T(8,128)S(1)}, f32[32,1280]{1,0:T(8,128)S(1)}, u32[]{:S(2)}, u32[]{:S(2)}) collective-permute-start(f32[32,1280]{1,0:T(8,128)S(1)} %add.26.kept_ref), channel_id=1, source_target_pairs={{1,0},{6,1},{10,2},{13,3},{3,4},{4,5},{8,6},{15,7},{0,8},{7,9},{11... | collective-permute-start | bytes 491528 | tf_op jit(solution)/shard_map/ppermute | solution.py:230
  23.4 7.5 %collective-permute-done.5.first_ref = f32[32,1280]{1,0:T(8,128)S(1)} collective-permute-done((f32[32,1280]{1,0:T(8,128)S(1)}, f32[32,1280]{1,0:T(8,128)S(1)}, u32[]{:S(2)}, u32[]{:S(2)}) %collective-permute-start.5) | collective-permute-done | bytes 163872 | tf_op jit(solution)/shard_map/ppermute | solution.py:230
  30.8 0.8 %collective-permute-done.6.second_ref = f32[32,1280]{1,0:T(8,128)S(1)} collective-permute-done((f32[32,1280]{1,0:T(8,128)S(1)}, f32[32,1280]{1,0:T(8,128)S(1)}, u32[]{:S(2)}, u32[]{:S(2)}) %collective-permute-start.6) | collective-permute-done | bytes 163872 | tf_op jit(solution)/shard_map/ppermute | solution.py:230
  31.7 3.4 %tile_next.1 = (f32[32,1408]{1,0:T(8,128)S(1)}, f32[32,1408]{1,0:T(8,128)S(1)}) custom-call(bf16[1280,1280]{1,0:T(8,128)(2,1)S(1)} %copy-done, f32[32,1280]{1,0:T(8,128)S(1)} %add.26.kept_ref, f32[32,1280]{1,0:T(8,128)S(1)} %collective-permute-done.4.passed_ref, f32[32,1280]{1,0:T(8,128)S(1)} %collective-permute-done.5.first_ref, ...), custom_call_target="tpu_custom_call" | custom-call | flops 2516582400 | bytes 3276800 | tf_op jit(solution)/shard_map/tile_next/pallas_call | solution.py:119
  35.2 1.4 %collective-permute-done.7 = f32[32,1408]{1,0:T(8,128)S(1)} collective-permute-done((f32[32,1408]{1,0:T(8,128)S(1)}, f32[32,1408]{1,0:T(8,128)S(1)}, u32[]{:S(2)}, u32[]{:S(2)}) %collective-permute-start.7) | collective-permute-done | bytes 180256 | tf_op jit(solution)/shard_map/ppermute | solution.py:233
  36.7 2.2 %collective-permute-start.11 = (f32[16,128]{1,0:T(8,128)S(1)}, f32[16,128]{1,0:T(8,128)S(1)}, u32[]{:S(2)}, u32[]{:S(2)}) collective-permute-start(f32[16,128]{1,0:T(8,128)S(1)} %slice.26), channel_id=1, source_target_pairs={{8,0},{9,1},{10,2},{11,3},{12,4},{13,5},{14,6},{15,7},{0,8},{1,9},... | collective-permute-start | bytes 24584 | tf_op jit(solution)/shard_map/ppermute | solution.py:230
  38.9 2.1 %collective-permute-start.12 = (f32[16,128]{1,0:T(8,128)S(1)}, f32[16,128]{1,0:T(8,128)S(1)}, u32[]{:S(2)}, u32[]{:S(2)}) collective-permute-start(f32[16,128]{1,0:T(8,128)S(1)} %slice.26), channel_id=1, source_target_pairs={{10,0},{11,1},{8,2},{9,3},{14,4},{15,5},{12,6},{13,7},{2,8},{3,9},... | collective-permute-start | bytes 24584 | tf_op jit(solution)/shard_map/ppermute | solution.py:230
  41.1 2.3 %collective-permute-done.8 = f32[32,1408]{1,0:T(8,128)S(1)} collective-permute-done((f32[32,1408]{1,0:T(8,128)S(1)}, f32[32,1408]{1,0:T(8,128)S(1)}, u32[]{:S(2)}, u32[]{:S(2)}) %collective-permute-start.8) | collective-permute-done | bytes 180256 | tf_op jit(solution)/shard_map/ppermute | solution.py:236
  43.4 0.3 collective-permute-start.10
  43.7 3.3 %collective-permute-start.9 = (f32[32,1280]{1,0:T(8,128)S(1)}, f32[32,1280]{1,0:T(8,128)S(1)}, u32[]{:S(2)}, u32[]{:S(2)}) collective-permute-start(f32[32,1280]{1,0:T(8,128)S(1)} %slice.24), channel_id=1, source_target_pairs={{1,0},{6,1},{10,2},{13,3},{3,4},{4,5},{8,6},{15,7},{0,8},{7,9},{11... | collective-permute-start | bytes 491528 | tf_op jit(solution)/shard_map/ppermute | solution.py:230
  47.2 4.4 %collective-permute-done.13 = f32[16,128]{1,0:T(8,128)S(1)} collective-permute-done((f32[16,128]{1,0:T(8,128)S(1)}, f32[16,128]{1,0:T(8,128)S(1)}, u32[]{:S(2)}, u32[]{:S(2)}) %collective-permute-start.13) | collective-permute-done | bytes 8224 | tf_op jit(solution)/shard_map/ppermute | solution.py:236
  51.6 2.3 %collective-permute-done.10 = f32[32,1280]{1,0:T(8,128)S(1)} collective-permute-done((f32[32,1280]{1,0:T(8,128)S(1)}, f32[32,1280]{1,0:T(8,128)S(1)}, u32[]{:S(2)}, u32[]{:S(2)}) %collective-permute-start.10) | collective-permute-done | bytes 163872 | tf_op jit(solution)/shard_map/ppermute | solution.py:230
  54.0 0.4 collective-permute-done.9
  54.4 0.5 slice.23
  54.9 0.7 %fusion = f32[1280,64]{0,1:T(8,128)} fusion(f32[32,1280]{1,0:T(8,128)S(1)} %collective-permute-done.10, f32[32,1280]{1,0:T(8,128)S(1)} %collective-permute-done.9, pred[]{:T(512)S(6)} %eq.3), kind=kLoop, calls=%fused_computation.1 | loop fusion | flops 245760 | bytes 655361 | tf_op jit(solution)/shard_map/transpose | solution.py:318
  (22 shorter events, 0.8 us)
Async XLA Ops:
  0.6 7.3 %collective-permute-start = (f32[64,1280]{1,0:T(8,128)}, f32[64,1280]{1,0:T(8,128)S(1)}, u32[]{:S(2)}, u32[]{:S(2)}) collective-permute-start(f32[64,1280]{1,0:T(8,128)} %bitcast.4), channel_id=1, source_target_pairs={{2,0},{4,1},{0,2},{6,3},{1,4},{7,5},{3,6},{5,7},{10,8},{12,9},{8,1... | collective-permute-start | bytes 983048 | tf_op jit(solution)/shard_map/ppermute | solution.py:230
  1.2 1.9 %copy-start = (bf16[1280,1280]{1,0:T(8,128)(2,1)S(1)}, bf16[1280,1280]{1,0:T(8,128)(2,1)}, u32[]{:S(2)}) copy-start(bf16[1280,1280]{1,0:T(8,128)(2,1)} %delta_ref.5) | copy-start | bytes 9830404
  3.2 6.5 %copy-start.1 = (f32[1280,64]{0,1:T(8,128)S(1)}, f32[1280,64]{0,1:T(8,128)}, u32[]{:S(2)}) copy-start(f32[1280,64]{0,1:T(8,128)} %param.3) | copy-start | bytes 983044
  8.0 1.6 %collective-permute-start.1 = (f32[64,1280]{1,0:T(8,128)S(1)}, f32[64,1280]{1,0:T(8,128)S(1)}, u32[]{:S(2)}, u32[]{:S(2)}) collective-permute-start(f32[64,1280]{1,0:T(8,128)S(1)} %collective-permute-done.got_ref), channel_id=1, source_target_pairs={{0,1},{1,0},{2,3},{3,2},{4,5},{5,4},{6,7},{7,6},{8,9},{9,8},{10,11... | collective-permute-start | bytes 983048 | tf_op jit(solution)/shard_map/ppermute | solution.py:233
  12.3 1.5 %collective-permute-start.2 = (f32[32,1280]{1,0:T(8,128)S(1)}, f32[32,1280]{1,0:T(8,128)S(1)}, u32[]{:S(2)}, u32[]{:S(2)}) collective-permute-start(f32[32,1280]{1,0:T(8,128)S(1)} %get-tuple-element.13), channel_id=1, source_target_pairs={{0,1},{1,0},{2,3},{3,2},{4,5},{5,4},{6,7},{7,6},{8,9},{9,8},{10,11... | collective-permute-start | bytes 491528 | tf_op jit(solution)/shard_map/ppermute | solution.py:233
  13.8 6.3 %collective-permute-start.3 = (f32[32,1280]{1,0:T(8,128)S(1)}, f32[32,1280]{1,0:T(8,128)S(1)}, u32[]{:S(2)}, u32[]{:S(2)}) collective-permute-start(f32[32,1280]{1,0:T(8,128)S(1)} %add.25), channel_id=1, source_target_pairs={{0,2},{2,0},{1,3},{3,1},{4,6},{6,4},{5,7},{7,5},{8,10},{10,8},{9,1... | collective-permute-start | bytes 491528 | tf_op jit(solution)/shard_map/ppermute | solution.py:236
  20.1 3.3 %collective-permute-start.4 = (f32[32,1280]{1,0:T(8,128)S(1)}, f32[32,1280]{1,0:T(8,128)S(1)}, u32[]{:S(2)}, u32[]{:S(2)}) collective-permute-start(f32[32,1280]{1,0:T(8,128)S(1)} %add.26.kept_ref), channel_id=1, source_target_pairs={{0,1},{1,0},{2,3},{3,2},{4,5},{5,4},{6,7},{7,6},{8,9},{9,8},{10,11... | collective-permute-start | bytes 491528 | tf_op jit(solution)/shard_map/ppermute | solution.py:233
  20.2 10.6 %collective-permute-start.5 = (f32[32,1280]{1,0:T(8,128)S(1)}, f32[32,1280]{1,0:T(8,128)S(1)}, u32[]{:S(2)}, u32[]{:S(2)}) collective-permute-start(f32[32,1280]{1,0:T(8,128)S(1)} %add.26.kept_ref), channel_id=1, source_target_pairs={{1,0},{6,1},{10,2},{13,3},{3,4},{4,5},{8,6},{15,7},{0,8},{7,9},{11... | collective-permute-start | bytes 491528 | tf_op jit(solution)/shard_map/ppermute | solution.py:230
  23.3 8.4 %collective-permute-start.6 = (f32[32,1280]{1,0:T(8,128)S(1)}, f32[32,1280]{1,0:T(8,128)S(1)}, u32[]{:S(2)}, u32[]{:S(2)}) collective-permute-start(f32[32,1280]{1,0:T(8,128)S(1)} %add.26.kept_ref), channel_id=1, source_target_pairs={{2,0},{5,1},{11,2},{12,3},{0,4},{7,5},{9,6},{14,7},{1,8},{6,9},{8,... | collective-permute-start | bytes 491528 | tf_op jit(solution)/shard_map/ppermute | solution.py:230
  35.1 1.5 %collective-permute-start.7 = (f32[32,1408]{1,0:T(8,128)S(1)}, f32[32,1408]{1,0:T(8,128)S(1)}, u32[]{:S(2)}, u32[]{:S(2)}) collective-permute-start(f32[32,1408]{1,0:T(8,128)S(1)} %get-tuple-element.16), channel_id=1, source_target_pairs={{0,1},{1,0},{2,3},{3,2},{4,5},{5,4},{6,7},{7,6},{8,9},{9,8},{10,11... | collective-permute-start | bytes 540680 | tf_op jit(solution)/shard_map/ppermute | solution.py:233
  36.6 6.7 %collective-permute-start.8 = (f32[32,1408]{1,0:T(8,128)S(1)}, f32[32,1408]{1,0:T(8,128)S(1)}, u32[]{:S(2)}, u32[]{:S(2)}) collective-permute-start(f32[32,1408]{1,0:T(8,128)S(1)} %add.27), channel_id=1, source_target_pairs={{0,2},{2,0},{1,3},{3,1},{4,6},{6,4},{5,7},{7,5},{8,10},{10,8},{9,1... | collective-permute-start | bytes 540680 | tf_op jit(solution)/shard_map/ppermute | solution.py:236
  36.7 10.3 %collective-permute-start.11 = (f32[16,128]{1,0:T(8,128)S(1)}, f32[16,128]{1,0:T(8,128)S(1)}, u32[]{:S(2)}, u32[]{:S(2)}) collective-permute-start(f32[16,128]{1,0:T(8,128)S(1)} %slice.26), channel_id=1, source_target_pairs={{8,0},{9,1},{10,2},{11,3},{12,4},{13,5},{14,6},{15,7},{0,8},{1,9},... | collective-permute-start | bytes 24584 | tf_op jit(solution)/shard_map/ppermute | solution.py:230
  38.9 8.1 %collective-permute-start.12 = (f32[16,128]{1,0:T(8,128)S(1)}, f32[16,128]{1,0:T(8,128)S(1)}, u32[]{:S(2)}, u32[]{:S(2)}) collective-permute-start(f32[16,128]{1,0:T(8,128)S(1)} %slice.26), channel_id=1, source_target_pairs={{10,0},{11,1},{8,2},{9,3},{14,4},{15,5},{12,6},{13,7},{2,8},{3,9},... | collective-permute-start | bytes 24584 | tf_op jit(solution)/shard_map/ppermute | solution.py:230
  43.4 10.6 %collective-permute-start.10 = (f32[32,1280]{1,0:T(8,128)S(1)}, f32[32,1280]{1,0:T(8,128)S(1)}, u32[]{:S(2)}, u32[]{:S(2)}) collective-permute-start(f32[32,1280]{1,0:T(8,128)S(1)} %slice.24), channel_id=1, source_target_pairs={{2,0},{5,1},{11,2},{12,3},{0,4},{7,5},{9,6},{14,7},{1,8},{6,9},{8,... | collective-permute-start | bytes 491528 | tf_op jit(solution)/shard_map/ppermute | solution.py:230
  43.7 10.7 %collective-permute-start.9 = (f32[32,1280]{1,0:T(8,128)S(1)}, f32[32,1280]{1,0:T(8,128)S(1)}, u32[]{:S(2)}, u32[]{:S(2)}) collective-permute-start(f32[32,1280]{1,0:T(8,128)S(1)} %slice.24), channel_id=1, source_target_pairs={{1,0},{6,1},{10,2},{13,3},{3,4},{4,5},{8,6},{15,7},{0,8},{7,9},{11... | collective-permute-start | bytes 491528 | tf_op jit(solution)/shard_map/ppermute | solution.py:230
  47.0 4.6 %collective-permute-start.13 = (f32[16,128]{1,0:T(8,128)S(1)}, f32[16,128]{1,0:T(8,128)S(1)}, u32[]{:S(2)}, u32[]{:S(2)}) collective-permute-start(f32[16,128]{1,0:T(8,128)S(1)} %fusion.1), channel_id=1, source_target_pairs={{0,4},{4,0},{8,12},{12,8},{1,5},{5,1},{9,13},{13,9},{2,6},{6,2},{1... | collective-permute-start | bytes 24584 | tf_op jit(solution)/shard_map/ppermute | solution.py:236

commit v4 on v3

--- a/solution.py
+++ b/solution.py
@@ -57,7 +57,9 @@
     lhs[...] = jnp.concatenate(
         [minus2(high), minus2(high), minus2(middle), norm_rows(points, True), jnp.zeros((fill, rows), bf16)], axis=0
     ).T
-    left[...] = jnp.concatenate([high, middle, jnp.ones((EXTRA, rows), bf16)], axis=0)
+    lft = jnp.concatenate([high, middle, jnp.ones((EXTRA, rows), bf16)], axis=0)
+    left[:, :rows] = lft
+    left[:, rows:] = lft
     points = col_pts[...] - shift
     col_pts[...] = points
     high, middle = split2(points)
@@ -91,9 +93,8 @@
                 ratio = delta * lax.rsqrt(jnp.maximum(squared, FLOOR * FLOOR))
             high, low = split2(ratio)
             r_high[slot, ps, :] = high
-            r_low[slot, ps, :] = low
+            r_high[slot, pl.ds(rows + p * PIECE, PIECE), :] = low
         terms = jnp.dot(left[...], r_high[slot], preferred_element_type=f32)
-        terms = terms + jnp.dot(left[...], r_low[slot], preferred_element_type=f32)
         cross = terms[:dims] + terms[dims:2 * dims]
         emit(js, col_pts[:, js] * terms[2 * dims:2 * dims + 1] - cross)
     return jnp.sum(misfit[0] + 2.0 * misfit[1]) if stress else None
@@ -106,10 +107,10 @@
         pltpu.VMEM((dims, cols), f32),
         pltpu.VMEM((rows, DEPTH), bf16),
         pltpu.VMEM((DEPTH, cols), bf16),
-        pltpu.VMEM((2 * dims + EXTRA, rows), bf16),
+        pltpu.VMEM((2 * dims + EXTRA, 2 * rows), bf16),
         pltpu.VMEM((2, rows, step), f32),
-        pltpu.VMEM((2, rows, step), bf16),
-        pltpu.VMEM((2, rows, step), bf16),
+        pltpu.VMEM((2, 2 * rows, step), bf16),
+        pltpu.VMEM((8, LANES), bf16),
     ]
 
 
@@ -211,6 +212,23 @@
     return call(norm_body, "norm", [(8, LANES)], [], (4 * delta.size, 2 * delta.size, 0), delta)[0]
 
 
+def stress_body(mine_ref, other_ref, out_ref):
+    total = mine_ref[...] + other_ref[...]
+    out_ref[0] = (total[:8] / total[8:])[0, 0]
+
+
+def stress_call(mine, other):
+    vmem = pl.BlockSpec(memory_space=pltpu.VMEM)
+    return pl.pallas_call(
+        stress_body,
+        out_shape=jax.ShapeDtypeStruct((1,), f32),
+        in_specs=[vmem] * 2,
+        out_specs=pl.BlockSpec(memory_space=pltpu.SMEM),
+        compiler_params=pltpu.CompilerParams(vmem_limit_bytes=40 << 20),
+        name="stress",
+    )(mine, other)
+
+
 class Grid:
     def __init__(self):
         self.narrow = lax.axis_size("narrow")
@@ -235,16 +253,19 @@
     def across(self, value, axis, bit):
         return lax.ppermute(value, axis, [(i, i ^ bit) for i in range(lax.axis_size(axis))])
 
-    def spread(self, first):
+    def spread(self, late, flip=0):
         def source(x, a, z):
             block = 2 * x + a
             offset = z ^ block
             top, low = offset // self.narrow, offset % self.narrow
-            if first:
-                return x ^ low, a ^ (1 - top), block
-            return x ^ low ^ (1 - top), a ^ top, block
+            if late:
+                return x ^ low ^ (1 - top), a ^ top, block
+            return x ^ low ^ flip, a ^ (1 - top), block
 
         return source
+
+    def early(self, value):
+        return self.send(value, self.spread(False)), self.send(value, self.spread(False, 1))
 
     def spread_half(self):
         x, a, z = (lax.axis_index(n) for n in ("narrow", "aux", "wide"))
@@ -285,10 +306,12 @@
 
     keep, send = first_tile(grid.narrow, scale, dissimilarity, own, got, passed)
     half = keep + grid.other_core(send)
-    for bit in bits(grid.narrow):
+    for bit in bits(grid.narrow)[1:]:
         half = half + grid.across(half, "narrow", bit)
-    first = grid.send(half, grid.spread(True))
-    second = grid.send(half, grid.spread(False))
+    first = grid.early(half)
+    half = half + grid.across(half, "narrow", 1)
+    first = first[0] + first[1]
+    second = grid.send(half, grid.spread(True))
     other = grid.other_core(half)
     keep, send = next_tile(grid.spread_half, scale, dissimilarity, half, other, first, second, norm)
 
@@ -306,11 +329,10 @@
     for part in early:
         sums = sums + part
     half = half[:, :cols]
-    first = grid.send(half, grid.spread(True))
-    second = grid.send(half, grid.spread(False))
-    sums = sums + grid.across(sums, "wide", 1)
-    first, second, sums = lax.optimization_barrier((first, second, sums))
-    stress = lax.optimization_barrier(sums[:8] / sums[8:])[0, :1]
+    first = grid.send(half, grid.spread(False))
+    second = grid.send(half, grid.spread(True))
+    stress = stress_call(sums, grid.across(sums, "wide", 1))
+    first, second, stress = lax.optimization_barrier((first, second, stress))
     in_order = grid.spread_half() == 0
     embedding = jnp.where(
         in_order, jnp.concatenate([first, second], axis=0), jnp.concatenate([second, first], axis=0)

time: 55.8 us -> 52.9 us (0.948)
  the two profiles are of different devices: /device:TPU:6 before, /device:TPU:0 now
where the time goes in v4:
time: 52.9 us; the launch traced here: 51.9 us
  starting transfers between devices  21.3 us (40%)
  waiting for transfers between devices  19.8 us (37%)
  Pallas kernels  7.26 us (14%)
  local copies, waits for them, and re-layouts  1.94 us (4%)
  other arithmetic  0.86 us (2%)
  between operations  0.73 us (1%)
    ppermute x8, starting transfers between devices, send(): return lax.ppermute(value, AXES, self.pairs(source))  11.6 us
    ppermute x3, waiting for transfers between devices, across(): lax.ppermute(value, axis, [(i, i ^ bit) for i in range(lax.axis_size(axis...  9.05 us
    ppermute x3, starting transfers between devices, across(): lax.ppermute(value, axis, [(i, i ^ bit) for i in range(lax.axis_size(axis...  8.68 us
    ppermute x8, waiting for transfers between devices, send(): return lax.ppermute(value, AXES, self.pairs(source))  6.86 us
    pallas_call x3, Pallas kernels, call(): pl.pallas_call(body, out_shape=[jax.ShapeDtypeStruct(shape, f32) for shap...  6.71 us
    ppermute x4, waiting for transfers between devices, other_core(): return lax.ppermute(value, 'aux', [(0, 1), (1, 0)])  3.9 us
    unnamed x4, local copies, waits for them, and re-layouts  1.93 us
  transfers between devices with their start and end apart: 15, of which 10 were waited for; matrix products, arithmetic and copies ran while one was open for 0% of the time, Pallas kernels for 3%

profile of v4, /device:TPU:0, one launch (start us, length us, event | category | flops | bytes accessed | tf_op | source)
XLA Modules:
  0.0 51.9 jit_solution(5433233163350702799)
XLA Ops:
  0.6 3.0 %collective-permute-start = (f32[64,1280]{1,0:T(8,128)}, f32[64,1280]{1,0:T(8,128)S(1)}, u32[]{:S(2)}, u32[]{:S(2)}) collective-permute-start(f32[64,1280]{1,0:T(8,128)} %bitcast.3), channel_id=1, source_target_pairs={{2,0},{4,1},{0,2},{6,3},{1,4},{7,5},{3,6},{5,7},{10,8},{12,9},{8,1... | collective-permute-start | bytes 983048 | tf_op jit(solution)/shard_map/ppermute | solution.py:248
  3.6 1.9 %copy-done = bf16[1280,1280]{1,0:T(8,128)(2,1)S(1)} copy-done((bf16[1280,1280]{1,0:T(8,128)(2,1)S(1)}, bf16[1280,1280]{1,0:T(8,128)(2,1)}, u32[]{:S(2)}) %copy-start) | copy-done | bytes 3276824
  5.6 0.8 %norm.1.norm_ref = f32[8,128]{1,0:T(8,128)S(1)} custom-call(bf16[1280,1280]{1,0:T(8,128)(2,1)S(1)} %copy-done), custom_call_target="tpu_custom_call" | custom-call | flops 6553600 | bytes 3276800 | tf_op jit(solution)/shard_map/norm/pallas_call | solution.py:120
  6.3 2.6 %collective-permute-done.got_ref = f32[64,1280]{1,0:T(8,128)S(1)} collective-permute-done((f32[64,1280]{1,0:T(8,128)}, f32[64,1280]{1,0:T(8,128)S(1)}, u32[]{:S(2)}, u32[]{:S(2)}) %collective-permute-start) | collective-permute-done | bytes 327712 | tf_op jit(solution)/shard_map/ppermute | solution.py:248
  9.0 1.5 %collective-permute-done.1.passed_ref = f32[64,1280]{1,0:T(8,128)S(1)} collective-permute-done((f32[64,1280]{1,0:T(8,128)S(1)}, f32[64,1280]{1,0:T(8,128)S(1)}, u32[]{:S(2)}, u32[]{:S(2)}) %collective-permute-start.1) | collective-permute-done | bytes 327712 | tf_op jit(solution)/shard_map/ppermute | solution.py:251
  10.5 2.6 %tile_first.1 = (f32[32,1280]{1,0:T(8,128)S(1)}, f32[32,1280]{1,0:T(8,128)S(1)}) custom-call(bf16[1280,1280]{1,0:T(8,128)(2,1)S(1)} %copy-done, f32[64,1280]{1,0:T(8,128)S(1)} %bitcast.4, f32[64,1280]{1,0:T(8,128)S(1)} %collective-permute-done.got_ref, f32[64,1280]{1,0:T(8,128)S(1)} %collective-permute-done.1.passed_ref), custom_call_target="tpu_custom_call" | custom-call | flops 2516582400 | bytes 3276800 | tf_op jit(solution)/shard_map/tile_first/pallas_call | solution.py:120
  13.3 1.3 %collective-permute-done.2 = f32[32,1280]{1,0:T(8,128)S(1)} collective-permute-done((f32[32,1280]{1,0:T(8,128)S(1)}, f32[32,1280]{1,0:T(8,128)S(1)}, u32[]{:S(2)}, u32[]{:S(2)}) %collective-permute-start.2) | collective-permute-done | bytes 163872 | tf_op jit(solution)/shard_map/ppermute | solution.py:251
  14.6 2.1 %collective-permute-start.3 = (f32[32,1280]{1,0:T(8,128)S(1)}, f32[32,1280]{1,0:T(8,128)S(1)}, u32[]{:S(2)}, u32[]{:S(2)}) collective-permute-start(f32[32,1280]{1,0:T(8,128)S(1)} %add.25), channel_id=1, source_target_pairs={{0,2},{2,0},{1,3},{3,1},{4,6},{6,4},{5,7},{7,5},{8,10},{10,8},{9,1... | collective-permute-start | bytes 491528 | tf_op jit(solution)/shard_map/ppermute | solution.py:254
  16.7 2.6 %collective-permute-start.5 = (f32[32,1280]{1,0:T(8,128)S(1)}, f32[32,1280]{1,0:T(8,128)S(1)}, u32[]{:S(2)}, u32[]{:S(2)}) collective-permute-start(f32[32,1280]{1,0:T(8,128)S(1)} %add.25), channel_id=1, source_target_pairs={{1,0},{6,1},{10,2},{13,3},{3,4},{4,5},{8,6},{15,7},{0,8},{7,9},{11... | collective-permute-start | bytes 491528 | tf_op jit(solution)/shard_map/ppermute | solution.py:248
  19.3 0.9 %collective-permute-start.6 = (f32[32,1280]{1,0:T(8,128)S(1)}, f32[32,1280]{1,0:T(8,128)S(1)}, u32[]{:S(2)}, u32[]{:S(2)}) collective-permute-start(f32[32,1280]{1,0:T(8,128)S(1)} %add.25), channel_id=1, source_target_pairs={{3,0},{4,1},{8,2},{15,3},{1,4},{6,5},{10,6},{13,7},{2,8},{5,9},{9,... | collective-permute-start | bytes 491528 | tf_op jit(solution)/shard_map/ppermute | solution.py:248
  20.2 3.1 %collective-permute-done.3 = f32[32,1280]{1,0:T(8,128)S(1)} collective-permute-done((f32[32,1280]{1,0:T(8,128)S(1)}, f32[32,1280]{1,0:T(8,128)S(1)}, u32[]{:S(2)}, u32[]{:S(2)}) %collective-permute-start.3) | collective-permute-done | bytes 163872 | tf_op jit(solution)/shard_map/ppermute | solution.py:254
  23.3 1.0 %collective-permute-start.7 = (f32[32,1280]{1,0:T(8,128)S(1)}, f32[32,1280]{1,0:T(8,128)S(1)}, u32[]{:S(2)}, u32[]{:S(2)}) collective-permute-start(f32[32,1280]{1,0:T(8,128)S(1)} %add.26.kept_ref), channel_id=1, source_target_pairs={{2,0},{5,1},{11,2},{12,3},{0,4},{7,5},{9,6},{14,7},{1,8},{6,9},{8,... | collective-permute-start | bytes 491528 | tf_op jit(solution)/shard_map/ppermute | solution.py:248
  24.7 4.0 %collective-permute-done.7.second_ref = f32[32,1280]{1,0:T(8,128)S(1)} collective-permute-done((f32[32,1280]{1,0:T(8,128)S(1)}, f32[32,1280]{1,0:T(8,128)S(1)}, u32[]{:S(2)}, u32[]{:S(2)}) %collective-permute-start.7) | collective-permute-done | bytes 163872 | tf_op jit(solution)/shard_map/ppermute | solution.py:248
  28.7 3.4 %tile_next.1 = (f32[32,1408]{1,0:T(8,128)S(1)}, f32[32,1408]{1,0:T(8,128)S(1)}) custom-call(bf16[1280,1280]{1,0:T(8,128)(2,1)S(1)} %copy-done, f32[32,1280]{1,0:T(8,128)S(1)} %add.26.kept_ref, f32[32,1280]{1,0:T(8,128)S(1)} %collective-permute-done.4.passed_ref, f32[32,1280]{1,0:T(8,128)S(1)} %add.27.first_ref, ...), custom_call_target="tpu_custom_call" | custom-call | flops 2516582400 | bytes 3276800 | tf_op jit(solution)/shard_map/tile_next/pallas_call | solution.py:120
  32.1 0.7 %collective-permute-start.8 = (f32[32,1408]{1,0:T(8,128)S(1)}, f32[32,1408]{1,0:T(8,128)S(1)}, u32[]{:S(2)}, u32[]{:S(2)}) collective-permute-start(f32[32,1408]{1,0:T(8,128)S(1)} %get-tuple-element.16), channel_id=1, source_target_pairs={{0,1},{1,0},{2,3},{3,2},{4,5},{5,4},{6,7},{7,6},{8,9},{9,8},{10,11... | collective-permute-start | bytes 540680 | tf_op jit(solution)/shard_map/ppermute | solution.py:251
  32.8 1.0 %collective-permute-done.8 = f32[32,1408]{1,0:T(8,128)S(1)} collective-permute-done((f32[32,1408]{1,0:T(8,128)S(1)}, f32[32,1408]{1,0:T(8,128)S(1)}, u32[]{:S(2)}, u32[]{:S(2)}) %collective-permute-start.8) | collective-permute-done | bytes 180256 | tf_op jit(solution)/shard_map/ppermute | solution.py:251
  33.8 4.0 %collective-permute-start.9 = (f32[32,1408]{1,0:T(8,128)S(1)}, f32[32,1408]{1,0:T(8,128)S(1)}, u32[]{:S(2)}, u32[]{:S(2)}) collective-permute-start(f32[32,1408]{1,0:T(8,128)S(1)} %add.28), channel_id=1, source_target_pairs={{0,2},{2,0},{1,3},{3,1},{4,6},{6,4},{5,7},{7,5},{8,10},{10,8},{9,1... | collective-permute-start | bytes 540680 | tf_op jit(solution)/shard_map/ppermute | solution.py:254
  37.9 0.6 %collective-permute-start.12 = (f32[16,128]{1,0:T(8,128)S(1)}, f32[16,128]{1,0:T(8,128)S(1)}, u32[]{:S(2)}, u32[]{:S(2)}) collective-permute-start(f32[16,128]{1,0:T(8,128)S(1)} %slice.14), channel_id=1, source_target_pairs={{8,0},{9,1},{10,2},{11,3},{12,4},{13,5},{14,6},{15,7},{0,8},{1,9},... | collective-permute-start | bytes 24584 | tf_op jit(solution)/shard_map/ppermute | solution.py:248
  38.5 1.8 %collective-permute-start.13 = (f32[16,128]{1,0:T(8,128)S(1)}, f32[16,128]{1,0:T(8,128)S(1)}, u32[]{:S(2)}, u32[]{:S(2)}) collective-permute-start(f32[16,128]{1,0:T(8,128)S(1)} %slice.14), channel_id=1, source_target_pairs={{10,0},{11,1},{8,2},{9,3},{14,4},{15,5},{12,6},{13,7},{2,8},{3,9},... | collective-permute-start | bytes 24584 | tf_op jit(solution)/shard_map/ppermute | solution.py:248
  40.3 2.5 %collective-permute-done.9 = f32[32,1408]{1,0:T(8,128)S(1)} collective-permute-done((f32[32,1408]{1,0:T(8,128)S(1)}, f32[32,1408]{1,0:T(8,128)S(1)}, u32[]{:S(2)}, u32[]{:S(2)}) %collective-permute-start.9) | collective-permute-done | bytes 180256 | tf_op jit(solution)/shard_map/ppermute | solution.py:254
  42.9 1.7 %collective-permute-start.10 = (f32[32,1280]{1,0:T(8,128)S(1)}, f32[32,1280]{1,0:T(8,128)S(1)}, u32[]{:S(2)}, u32[]{:S(2)}) collective-permute-start(f32[32,1280]{1,0:T(8,128)S(1)} %slice.12), channel_id=1, source_target_pairs={{1,0},{6,1},{10,2},{13,3},{3,4},{4,5},{8,6},{15,7},{0,8},{7,9},{11... | collective-permute-start | bytes 491528 | tf_op jit(solution)/shard_map/ppermute | solution.py:248
  44.6 2.6 %collective-permute-start.14 = (f32[16,128]{1,0:T(8,128)S(1)}, f32[16,128]{1,0:T(8,128)S(1)}, u32[]{:S(2)}, u32[]{:S(2)}) collective-permute-start(f32[16,128]{1,0:T(8,128)S(1)} %fusion.1.mine_ref), channel_id=1, source_target_pairs={{0,4},{4,0},{8,12},{12,8},{1,5},{5,1},{9,13},{13,9},{2,6},{6,2},{1... | collective-permute-start | bytes 24584 | tf_op jit(solution)/shard_map/ppermute | solution.py:254
  47.1 3.5 %collective-permute-done.14.other_ref = f32[16,128]{1,0:T(8,128)S(1)} collective-permute-done((f32[16,128]{1,0:T(8,128)S(1)}, f32[16,128]{1,0:T(8,128)S(1)}, u32[]{:S(2)}, u32[]{:S(2)}) %collective-permute-start.14) | collective-permute-done | bytes 8224 | tf_op jit(solution)/shard_map/ppermute | solution.py:254
  51.2 0.7 %fusion = f32[1280,64]{0,1:T(8,128)} fusion(f32[32,1280]{1,0:T(8,128)S(1)} %collective-permute-done.11, f32[32,1280]{1,0:T(8,128)S(1)} %collective-permute-done.10, pred[]{:T(512)S(6)} %eq.3), kind=kLoop, calls=%fused_computation.1 | loop fusion | flops 245760 | bytes 655361 | tf_op jit(solution)/shard_map/transpose | solution.py:340
  (23 shorter events, 1.4 us)
Async XLA Ops:
  0.6 8.3 %collective-permute-start = (f32[64,1280]{1,0:T(8,128)}, f32[64,1280]{1,0:T(8,128)S(1)}, u32[]{:S(2)}, u32[]{:S(2)}) collective-permute-start(f32[64,1280]{1,0:T(8,128)} %bitcast.3), channel_id=1, source_target_pairs={{2,0},{4,1},{0,2},{6,3},{1,4},{7,5},{3,6},{5,7},{10,8},{12,9},{8,1... | collective-permute-start | bytes 983048 | tf_op jit(solution)/shard_map/ppermute | solution.py:248
  3.6 1.9 %copy-start = (bf16[1280,1280]{1,0:T(8,128)(2,1)S(1)}, bf16[1280,1280]{1,0:T(8,128)(2,1)}, u32[]{:S(2)}) copy-start(bf16[1280,1280]{1,0:T(8,128)(2,1)} %delta_ref.5) | copy-start | bytes 9830404
  5.6 5.0 %copy-start.1 = (f32[1280,64]{0,1:T(8,128)S(1)}, f32[1280,64]{0,1:T(8,128)}, u32[]{:S(2)}) copy-start(f32[1280,64]{0,1:T(8,128)} %param.3) | copy-start | bytes 983044
  8.9 1.6 %collective-permute-start.1 = (f32[64,1280]{1,0:T(8,128)S(1)}, f32[64,1280]{1,0:T(8,128)S(1)}, u32[]{:S(2)}, u32[]{:S(2)}) collective-permute-start(f32[64,1280]{1,0:T(8,128)S(1)} %collective-permute-done.got_ref), channel_id=1, source_target_pairs={{0,1},{1,0},{2,3},{3,2},{4,5},{5,4},{6,7},{7,6},{8,9},{9,8},{10,11... | collective-permute-start | bytes 983048 | tf_op jit(solution)/shard_map/ppermute | solution.py:251
  13.1 1.5 %collective-permute-start.2 = (f32[32,1280]{1,0:T(8,128)S(1)}, f32[32,1280]{1,0:T(8,128)S(1)}, u32[]{:S(2)}, u32[]{:S(2)}) collective-permute-start(f32[32,1280]{1,0:T(8,128)S(1)} %get-tuple-element.13), channel_id=1, source_target_pairs={{0,1},{1,0},{2,3},{3,2},{4,5},{5,4},{6,7},{7,6},{8,9},{9,8},{10,11... | collective-permute-start | bytes 491528 | tf_op jit(solution)/shard_map/ppermute | solution.py:251
  14.6 8.6 %collective-permute-start.3 = (f32[32,1280]{1,0:T(8,128)S(1)}, f32[32,1280]{1,0:T(8,128)S(1)}, u32[]{:S(2)}, u32[]{:S(2)}) collective-permute-start(f32[32,1280]{1,0:T(8,128)S(1)} %add.25), channel_id=1, source_target_pairs={{0,2},{2,0},{1,3},{3,1},{4,6},{6,4},{5,7},{7,5},{8,10},{10,8},{9,1... | collective-permute-start | bytes 491528 | tf_op jit(solution)/shard_map/ppermute | solution.py:254
  16.7 7.7 %collective-permute-start.5 = (f32[32,1280]{1,0:T(8,128)S(1)}, f32[32,1280]{1,0:T(8,128)S(1)}, u32[]{:S(2)}, u32[]{:S(2)}) collective-permute-start(f32[32,1280]{1,0:T(8,128)S(1)} %add.25), channel_id=1, source_target_pairs={{1,0},{6,1},{10,2},{13,3},{3,4},{4,5},{8,6},{15,7},{0,8},{7,9},{11... | collective-permute-start | bytes 491528 | tf_op jit(solution)/shard_map/ppermute | solution.py:248
  19.3 5.4 %collective-permute-start.6 = (f32[32,1280]{1,0:T(8,128)S(1)}, f32[32,1280]{1,0:T(8,128)S(1)}, u32[]{:S(2)}, u32[]{:S(2)}) collective-permute-start(f32[32,1280]{1,0:T(8,128)S(1)} %add.25), channel_id=1, source_target_pairs={{3,0},{4,1},{8,2},{15,3},{1,4},{6,5},{10,6},{13,7},{2,8},{5,9},{9,... | collective-permute-start | bytes 491528 | tf_op jit(solution)/shard_map/ppermute | solution.py:248
  23.3 1.5 %collective-permute-start.4 = (f32[32,1280]{1,0:T(8,128)S(1)}, f32[32,1280]{1,0:T(8,128)S(1)}, u32[]{:S(2)}, u32[]{:S(2)}) collective-permute-start(f32[32,1280]{1,0:T(8,128)S(1)} %add.26.kept_ref), channel_id=1, source_target_pairs={{0,1},{1,0},{2,3},{3,2},{4,5},{5,4},{6,7},{7,6},{8,9},{9,8},{10,11... | collective-permute-start | bytes 491528 | tf_op jit(solution)/shard_map/ppermute | solution.py:251
  23.3 5.4 %collective-permute-start.7 = (f32[32,1280]{1,0:T(8,128)S(1)}, f32[32,1280]{1,0:T(8,128)S(1)}, u32[]{:S(2)}, u32[]{:S(2)}) collective-permute-start(f32[32,1280]{1,0:T(8,128)S(1)} %add.26.kept_ref), channel_id=1, source_target_pairs={{2,0},{5,1},{11,2},{12,3},{0,4},{7,5},{9,6},{14,7},{1,8},{6,9},{8,... | collective-permute-start | bytes 491528 | tf_op jit(solution)/shard_map/ppermute | solution.py:248
  32.1 1.7 %collective-permute-start.8 = (f32[32,1408]{1,0:T(8,128)S(1)}, f32[32,1408]{1,0:T(8,128)S(1)}, u32[]{:S(2)}, u32[]{:S(2)}) collective-permute-start(f32[32,1408]{1,0:T(8,128)S(1)} %get-tuple-element.16), channel_id=1, source_target_pairs={{0,1},{1,0},{2,3},{3,2},{4,5},{5,4},{6,7},{7,6},{8,9},{9,8},{10,11... | collective-permute-start | bytes 540680 | tf_op jit(solution)/shard_map/ppermute | solution.py:251
  33.8 9.0 %collective-permute-start.9 = (f32[32,1408]{1,0:T(8,128)S(1)}, f32[32,1408]{1,0:T(8,128)S(1)}, u32[]{:S(2)}, u32[]{:S(2)}) collective-permute-start(f32[32,1408]{1,0:T(8,128)S(1)} %add.28), channel_id=1, source_target_pairs={{0,2},{2,0},{1,3},{3,1},{4,6},{6,4},{5,7},{7,5},{8,10},{10,8},{9,1... | collective-permute-start | bytes 540680 | tf_op jit(solution)/shard_map/ppermute | solution.py:254
  37.9 6.7 %collective-permute-start.12 = (f32[16,128]{1,0:T(8,128)S(1)}, f32[16,128]{1,0:T(8,128)S(1)}, u32[]{:S(2)}, u32[]{:S(2)}) collective-permute-start(f32[16,128]{1,0:T(8,128)S(1)} %slice.14), channel_id=1, source_target_pairs={{8,0},{9,1},{10,2},{11,3},{12,4},{13,5},{14,6},{15,7},{0,8},{1,9},... | collective-permute-start | bytes 24584 | tf_op jit(solution)/shard_map/ppermute | solution.py:248
  38.5 6.0 %collective-permute-start.13 = (f32[16,128]{1,0:T(8,128)S(1)}, f32[16,128]{1,0:T(8,128)S(1)}, u32[]{:S(2)}, u32[]{:S(2)}) collective-permute-start(f32[16,128]{1,0:T(8,128)S(1)} %slice.14), channel_id=1, source_target_pairs={{10,0},{11,1},{8,2},{9,3},{14,4},{15,5},{12,6},{13,7},{2,8},{3,9},... | collective-permute-start | bytes 24584 | tf_op jit(solution)/shard_map/ppermute | solution.py:248
  42.9 8.3 %collective-permute-start.10 = (f32[32,1280]{1,0:T(8,128)S(1)}, f32[32,1280]{1,0:T(8,128)S(1)}, u32[]{:S(2)}, u32[]{:S(2)}) collective-permute-start(f32[32,1280]{1,0:T(8,128)S(1)} %slice.12), channel_id=1, source_target_pairs={{1,0},{6,1},{10,2},{13,3},{3,4},{4,5},{8,6},{15,7},{0,8},{7,9},{11... | collective-permute-start | bytes 491528 | tf_op jit(solution)/shard_map/ppermute | solution.py:248
  44.5 6.6 %collective-permute-start.11 = (f32[32,1280]{1,0:T(8,128)S(1)}, f32[32,1280]{1,0:T(8,128)S(1)}, u32[]{:S(2)}, u32[]{:S(2)}) collective-permute-start(f32[32,1280]{1,0:T(8,128)S(1)} %slice.12), channel_id=1, source_target_pairs={{2,0},{5,1},{11,2},{12,3},{0,4},{7,5},{9,6},{14,7},{1,8},{6,9},{8,... | collective-permute-start | bytes 491528 | tf_op jit(solution)/shard_map/ppermute | solution.py:248
  44.6 6.0 %collective-permute-start.14 = (f32[16,128]{1,0:T(8,128)S(1)}, f32[16,128]{1,0:T(8,128)S(1)}, u32[]{:S(2)}, u32[]{:S(2)}) collective-permute-start(f32[16,128]{1,0:T(8,128)S(1)} %fusion.1.mine_ref), channel_id=1, source_target_pairs={{0,4},{4,0},{8,12},{12,8},{1,5},{5,1},{9,13},{13,9},{2,6},{6,2},{1... | collective-permute-start | bytes 24584 | tf_op jit(solution)/shard_map/ppermute | solution.py:254

commit v5 on v4

--- a/solution.py
+++ b/solution.py
@@ -13,6 +13,7 @@
 LANES = 128
 EXTRA = 16
 PIECE = 32
+TILE_SCRATCH = 8
 SUMS = 16
 
 f32 = jnp.float32
@@ -70,7 +71,7 @@
     def gram(c):
         square[c % 2] = jnp.dot(lhs[...], rhs[:, c * step:(c + 1) * step], preferred_element_type=f32)
 
-    misfit = [jnp.zeros((16, step), f32)] * 2
+    misfit = jnp.zeros((16, step), f32)
     gram(0)
     for c in range(cols // step):
         if (c + 1) * step < cols:
@@ -81,14 +82,13 @@
             ps = pl.ds(p * PIECE, PIECE)
             squared = square[slot, ps, :]
             delta = delta_at(p * PIECE, js).astype(f32)
-            above = c - p * PIECE // step
-            if stress and above >= 0:
+            if stress:
                 inverse = lax.rsqrt(jnp.maximum(squared, TINY))
                 ratio = delta * jnp.minimum(inverse, 1.0 / FLOOR)
                 gap = delta - jnp.maximum(squared, 0.0) * inverse
                 gap = gap * gap
                 for q in range(0, PIECE, 16):
-                    misfit[above > 0] = misfit[above > 0] + gap[q:q + 16]
+                    misfit = misfit + gap[q:q + 16]
             else:
                 ratio = delta * lax.rsqrt(jnp.maximum(squared, FLOOR * FLOOR))
             high, low = split2(ratio)
@@ -97,7 +97,7 @@
         terms = jnp.dot(left[...], r_high[slot], preferred_element_type=f32)
         cross = terms[:dims] + terms[dims:2 * dims]
         emit(js, col_pts[:, js] * terms[2 * dims:2 * dims + 1] - cross)
-    return jnp.sum(misfit[0] + 2.0 * misfit[1]) if stress else None
+    return jnp.sum(misfit) if stress else None
 
 
 def tile_scratch(dims, rows, cols):
@@ -136,7 +136,7 @@
 def first_tile(narrow, scale, delta, own, got, passed):
     dims, rows = own.shape
     cols = delta.shape[1]
-    half = dims // 2
+    half = cols // 2
 
     def body(delta_ref, own_ref, got_ref, passed_ref, keep_ref, send_ref, result, row_pts, col_pts, *rest):
         x, a, z = (lax.axis_index(n) for n in ("narrow", "aux", "wide"))
@@ -161,41 +161,62 @@
 
         tile_terms(row_pts, col_pts, lambda p, js: delta_ref[pl.ds(p, PIECE), js], *rest, False, emit)
         for ref, which in ((keep_ref, a), (send_ref, 1 - a)):
-            ref[...] = result[pl.ds(pl.multiple_of(which * half, 8), half), :]
+            ref[...] = result[:, pl.ds(pl.multiple_of(which * half, LANES), half)]
 
     scratch = [pltpu.VMEM((dims, cols), f32)] + tile_scratch(dims, rows, cols)
-    outs = [(half, cols)] * 2
+    outs = [(dims, half)] * 2
     return call(body, "tile_first", outs, scratch, tile_cost(rows, cols), delta, own, got, passed)
 
 
-def next_tile(side_of, scale, delta, kept, passed, first, second, norm):
-    half, rows = first.shape
-    dims = 2 * half
+def next_tile(side_of, scale, delta, rows_in, kept, passed, norm, before=None):
+    dims, rows = rows_in.shape
     cols = delta.shape[1]
-
-    def body(delta_ref, kept_ref, passed_ref, first_ref, second_ref, norm_ref, keep_ref, send_ref, result, *rest):
-        row_pts, col_pts, *rest = rest
+    half, less = cols // 2, dims // 2
+    closing = before is not None
+
+    def body(delta_ref, rows_ref, kept_ref, passed_ref, sums_ref, *refs):
+        row_pts, col_pts, *rest = refs[-TILE_SCRATCH:]
+        refs = refs[:-TILE_SCRATCH]
         a = lax.axis_index("aux")
-        at = lambda which: pl.ds(pl.multiple_of(which * half, 8), half)
-        side = side_of()
-        col_pts[at(a), :] = kept_ref[...]
-        col_pts[at(1 - a), :] = passed_ref[...]
-        row_pts[at(side), :] = first_ref[...]
-        row_pts[at(1 - side), :] = second_ref[...]
+        at = lambda which: pl.ds(pl.multiple_of(which * half, LANES), half)
+        base = side_of() * rows
+        row_pts[...] = rows_ref[...]
+        col_pts[:, at(a)] = kept_ref[...]
+        col_pts[:, at(1 - a)] = passed_ref[...]
+
+        def delta_at(p, js):
+            return delta_ref[pl.ds(pl.multiple_of(base + p, PIECE), PIECE), js]
+
+        if not closing:
+            part_ref, out_sums_ref = refs
+
+            def emit(js, part):
+                part_ref[:, js] = part
+
+            misfit = tile_terms(row_pts, col_pts, delta_at, *rest, True, emit)
+            out_sums_ref[:8] = jnp.full((8, LANES), misfit)
+            out_sums_ref[8:] = sums_ref[...]
+            return
+        before_ref, keep_ref, send_ref, result = refs
 
         def emit(js, part):
-            result[:, js] = part * scale
-
-        misfit = tile_terms(row_pts, col_pts, lambda p, js: delta_ref[pl.ds(p, PIECE), js], *rest, True, emit)
+            result[:, js] = (before_ref[:, js] + part) * scale
+
+        misfit = tile_terms(row_pts, col_pts, delta_at, *rest, True, emit)
         for ref, which in ((keep_ref, a), (send_ref, 1 - a)):
-            ref[:, :cols] = result[at(which), :]
-            ref[:8, cols:] = jnp.full((8, LANES), misfit)
-            ref[8:16, cols:] = norm_ref[...]
-            ref[16:, cols:] = jnp.zeros((half - 16, LANES), f32)
-
-    scratch = [pltpu.VMEM((dims, cols), f32)] + tile_scratch(dims, rows, cols)
-    outs = [(half, cols + LANES)] * 2
-    return call(body, "tile_next", outs, scratch, tile_cost(rows, cols), delta, kept, passed, first, second, norm)
+            ref[:, :cols] = result[pl.ds(pl.multiple_of(which * less, 8), less), :]
+            ref[:8, cols:] = sums_ref[:8] + misfit
+            ref[8:16, cols:] = sums_ref[8:]
+            ref[16:, cols:] = jnp.zeros((less - 16, LANES), f32)
+
+    scratch = tile_scratch(dims, rows, cols)
+    cost = tile_cost(rows, cols)
+    if not closing:
+        outs = [(dims, cols), (SUMS, LANES)]
+        return call(body, "tile_open", outs, scratch, cost, delta, rows_in, kept, passed, norm)
+    scratch = [pltpu.VMEM((dims, cols), f32)] + scratch
+    outs = [(less, cols + LANES)] * 2
+    return call(body, "tile_close", outs, scratch, cost, delta, rows_in, kept, passed, norm, before)
 
 
 def norm_body(delta_ref, out_ref):
@@ -313,7 +334,8 @@
     first = first[0] + first[1]
     second = grid.send(half, grid.spread(True))
     other = grid.other_core(half)
-    keep, send = next_tile(grid.spread_half, scale, dissimilarity, half, other, first, second, norm)
+    part, sums = next_tile(grid.spread_half, scale, dissimilarity, first, half, other, norm)
+    keep, send = next_tile(lambda: 1 - grid.spread_half(), scale, dissimilarity, second, half, other, sums, part)
 
     half = keep + grid.other_core(send)
     early = []

time: 52.9 us -> 51.7 us (0.977)
  waiting for transfers between devices: 19.8 us -> 17.6 us
  Pallas kernels: 7.26 us -> 8.24 us
    ppermute x8, waiting for transfers between devices: 6.86 us -> 4.68 us  [send(): return lax.ppermute(value, AXES, self.pairs(source))]
    pallas_call x3 -> x4, Pallas kernels: 6.71 us -> 7.68 us  [call(): pl.pallas_call(body, out_shape=[jax.ShapeDtypeStruct(shape, f32) for shap...]
  transfers between devices with their start and end apart: 15 -> 15, of which waited for: 10 -> 10; matrix products, arithmetic and copies ran while one was open for 0% -> 0% of each run, Pallas kernels for 3% -> 7%
where the time goes in v5:
time: 51.7 us; the launch traced here: 50.8 us
  starting transfers between devices  21.3 us (41%)
  waiting for transfers between devices  17.6 us (34%)
  Pallas kernels  8.24 us (16%)
  local copies, waits for them, and re-layouts  1.94 us (4%)
  other arithmetic  0.87 us (2%)
  between operations  0.73 us (1%)
    ppermute x8, starting transfers between devices, send(): return lax.ppermute(value, AXES, self.pairs(source))  11.6 us
    ppermute x3, waiting for transfers between devices, across(): lax.ppermute(value, axis, [(i, i ^ bit) for i in range(lax.axis_size(axis...  9.06 us
    ppermute x3, starting transfers between devices, across(): lax.ppermute(value, axis, [(i, i ^ bit) for i in range(lax.axis_size(axis...  8.66 us
    pallas_call x4, Pallas kernels, call(): pl.pallas_call(body, out_shape=[jax.ShapeDtypeStruct(shape, f32) for shap...  7.68 us
    ppermute x8, waiting for transfers between devices, send(): return lax.ppermute(value, AXES, self.pairs(source))  4.68 us
    ppermute x4, waiting for transfers between devices, other_core(): return lax.ppermute(value, 'aux', [(0, 1), (1, 0)])  3.89 us
    unnamed x4, local copies, waits for them, and re-layouts  1.93 us
    ppermute x4, starting transfers between devices, other_core(): return lax.ppermute(value, 'aux', [(0, 1), (1, 0)])  1.05 us
  transfers between devices with their start and end apart: 15, of which 10 were waited for; matrix products, arithmetic and copies ran while one was open for 0% of the time, Pallas kernels for 7%

profile of v5, /device:TPU:0, one launch (start us, length us, event | category | flops | bytes accessed | tf_op | source)
XLA Modules:
  0.0 50.8 jit_solution(4219253922629795239)
XLA Ops:
  0.6 3.0 %collective-permute-start = (f32[64,1280]{1,0:T(8,128)}, f32[64,1280]{1,0:T(8,128)S(1)}, u32[]{:S(2)}, u32[]{:S(2)}) collective-permute-start(f32[64,1280]{1,0:T(8,128)} %bitcast.3), channel_id=1, source_target_pairs={{2,0},{4,1},{0,2},{6,3},{1,4},{7,5},{3,6},{5,7},{10,8},{12,9},{8,1... | collective-permute-start | bytes 983048 | tf_op jit(solution)/shard_map/ppermute | solution.py:269
  3.6 1.9 %copy-done = bf16[1280,1280]{1,0:T(8,128)(2,1)S(1)} copy-done((bf16[1280,1280]{1,0:T(8,128)(2,1)S(1)}, bf16[1280,1280]{1,0:T(8,128)(2,1)}, u32[]{:S(2)}) %copy-start) | copy-done | bytes 3276824
  5.6 0.8 %norm.1.sums_ref = f32[8,128]{1,0:T(8,128)S(1)} custom-call(bf16[1280,1280]{1,0:T(8,128)(2,1)S(1)} %copy-done), custom_call_target="tpu_custom_call" | custom-call | flops 6553600 | bytes 3276800 | tf_op jit(solution)/shard_map/norm/pallas_call | solution.py:120
  6.3 2.6 %collective-permute-done.got_ref = f32[64,1280]{1,0:T(8,128)S(1)} collective-permute-done((f32[64,1280]{1,0:T(8,128)}, f32[64,1280]{1,0:T(8,128)S(1)}, u32[]{:S(2)}, u32[]{:S(2)}) %collective-permute-start) | collective-permute-done | bytes 327712 | tf_op jit(solution)/shard_map/ppermute | solution.py:269
  9.0 1.5 %collective-permute-done.1.passed_ref = f32[64,1280]{1,0:T(8,128)S(1)} collective-permute-done((f32[64,1280]{1,0:T(8,128)S(1)}, f32[64,1280]{1,0:T(8,128)S(1)}, u32[]{:S(2)}, u32[]{:S(2)}) %collective-permute-start.1) | collective-permute-done | bytes 327712 | tf_op jit(solution)/shard_map/ppermute | solution.py:272
  10.5 2.5 %tile_first.1 = (f32[64,640]{1,0:T(8,128)S(1)}, f32[64,640]{1,0:T(8,128)S(1)}) custom-call(bf16[1280,1280]{1,0:T(8,128)(2,1)S(1)} %copy-done, f32[64,1280]{1,0:T(8,128)S(1)} %bitcast.4, f32[64,1280]{1,0:T(8,128)S(1)} %collective-permute-done.got_ref, f32[64,1280]{1,0:T(8,128)S(1)} %collective-permute-done.1.passed_ref), custom_call_target="tpu_custom_call" | custom-call | flops 2516582400 | bytes 3276800 | tf_op jit(solution)/shard_map/tile_first/pallas_call | solution.py:120
  13.3 1.3 %collective-permute-done.2 = f32[64,640]{1,0:T(8,128)S(1)} collective-permute-done((f32[64,640]{1,0:T(8,128)S(1)}, f32[64,640]{1,0:T(8,128)S(1)}, u32[]{:S(2)}, u32[]{:S(2)}) %collective-permute-start.2) | collective-permute-done | bytes 163872 | tf_op jit(solution)/shard_map/ppermute | solution.py:272
  14.6 2.1 %collective-permute-start.3 = (f32[64,640]{1,0:T(8,128)S(1)}, f32[64,640]{1,0:T(8,128)S(1)}, u32[]{:S(2)}, u32[]{:S(2)}) collective-permute-start(f32[64,640]{1,0:T(8,128)S(1)} %add.25), channel_id=1, source_target_pairs={{0,2},{2,0},{1,3},{3,1},{4,6},{6,4},{5,7},{7,5},{8,10},{10,8},{9,1... | collective-permute-start | bytes 491528 | tf_op jit(solution)/shard_map/ppermute | solution.py:275
  16.6 2.6 %collective-permute-start.6 = (f32[64,640]{1,0:T(8,128)S(1)}, f32[64,640]{1,0:T(8,128)S(1)}, u32[]{:S(2)}, u32[]{:S(2)}) collective-permute-start(f32[64,640]{1,0:T(8,128)S(1)} %add.25), channel_id=1, source_target_pairs={{1,0},{6,1},{10,2},{13,3},{3,4},{4,5},{8,6},{15,7},{0,8},{7,9},{11... | collective-permute-start | bytes 491528 | tf_op jit(solution)/shard_map/ppermute | solution.py:269
  19.2 0.9 %collective-permute-start.7 = (f32[64,640]{1,0:T(8,128)S(1)}, f32[64,640]{1,0:T(8,128)S(1)}, u32[]{:S(2)}, u32[]{:S(2)}) collective-permute-start(f32[64,640]{1,0:T(8,128)S(1)} %add.25), channel_id=1, source_target_pairs={{3,0},{4,1},{8,2},{15,3},{1,4},{6,5},{10,6},{13,7},{2,8},{5,9},{9,... | collective-permute-start | bytes 491528 | tf_op jit(solution)/shard_map/ppermute | solution.py:269
  20.1 3.1 %collective-permute-done.3 = f32[64,640]{1,0:T(8,128)S(1)} collective-permute-done((f32[64,640]{1,0:T(8,128)S(1)}, f32[64,640]{1,0:T(8,128)S(1)}, u32[]{:S(2)}, u32[]{:S(2)}) %collective-permute-start.3) | collective-permute-done | bytes 163872 | tf_op jit(solution)/shard_map/ppermute | solution.py:275
  23.3 1.0 %collective-permute-start.4 = (f32[64,640]{1,0:T(8,128)S(1)}, f32[64,640]{1,0:T(8,128)S(1)}, u32[]{:S(2)}, u32[]{:S(2)}) collective-permute-start(f32[64,640]{1,0:T(8,128)S(1)} %add.26.kept_ref), channel_id=1, source_target_pairs={{2,0},{5,1},{11,2},{12,3},{0,4},{7,5},{9,6},{14,7},{1,8},{6,9},{8,... | collective-permute-start | bytes 491528 | tf_op jit(solution)/shard_map/ppermute | solution.py:269
  24.7 2.2 %tile_open.1 = (f32[64,1280]{1,0:T(8,128)S(1)}, f32[16,128]{1,0:T(8,128)S(1)}) custom-call(bf16[1280,1280]{1,0:T(8,128)(2,1)S(1)} %copy-done, f32[64,640]{1,0:T(8,128)S(1)} %add.27.rows_ref, f32[64,640]{1,0:T(8,128)S(1)} %add.26.kept_ref, f32[64,640]{1,0:T(8,128)S(1)} %collective-permute-done.5.passed_ref, f32[8,128]{1,0:T(8,128)S(1)} %norm.1.sums_ref), custom_call_target="tpu_custom_call" | custom-call | flops 1258291200 | bytes 1638400 | tf_op jit(solution)/shard_map/tile_open/pallas_call | solution.py:120
  26.9 1.8 %collective-permute-done.4.rows_ref = f32[64,640]{1,0:T(8,128)S(1)} collective-permute-done((f32[64,640]{1,0:T(8,128)S(1)}, f32[64,640]{1,0:T(8,128)S(1)}, u32[]{:S(2)}, u32[]{:S(2)}) %collective-permute-start.4) | collective-permute-done | bytes 163872 | tf_op jit(solution)/shard_map/ppermute | solution.py:269
  28.7 2.2 %tile_close.1 = (f32[32,1408]{1,0:T(8,128)S(1)}, f32[32,1408]{1,0:T(8,128)S(1)}) custom-call(bf16[1280,1280]{1,0:T(8,128)(2,1)S(1)} %copy-done, f32[64,640]{1,0:T(8,128)S(1)} %collective-permute-done.4.rows_ref, f32[64,640]{1,0:T(8,128)S(1)} %add.26.kept_ref, f32[64,640]{1,0:T(8,128)S(1)} %collective-permute-done.5.passed_ref, ...), custom_call_target="tpu_custom_call" | custom-call | flops 1258291200 | bytes 1638400 | tf_op jit(solution)/shard_map/tile_close/pallas_call | solution.py:120
  30.9 0.7 %collective-permute-start.8 = (f32[32,1408]{1,0:T(8,128)S(1)}, f32[32,1408]{1,0:T(8,128)S(1)}, u32[]{:S(2)}, u32[]{:S(2)}) collective-permute-start(f32[32,1408]{1,0:T(8,128)S(1)} %get-tuple-element.20), channel_id=1, source_target_pairs={{0,1},{1,0},{2,3},{3,2},{4,5},{5,4},{6,7},{7,6},{8,9},{9,8},{10,11... | collective-permute-start | bytes 540680 | tf_op jit(solution)/shard_map/ppermute | solution.py:272
  31.6 1.0 %collective-permute-done.8 = f32[32,1408]{1,0:T(8,128)S(1)} collective-permute-done((f32[32,1408]{1,0:T(8,128)S(1)}, f32[32,1408]{1,0:T(8,128)S(1)}, u32[]{:S(2)}, u32[]{:S(2)}) %collective-permute-start.8) | collective-permute-done | bytes 180256 | tf_op jit(solution)/shard_map/ppermute | solution.py:272
  32.7 4.0 %collective-permute-start.9 = (f32[32,1408]{1,0:T(8,128)S(1)}, f32[32,1408]{1,0:T(8,128)S(1)}, u32[]{:S(2)}, u32[]{:S(2)}) collective-permute-start(f32[32,1408]{1,0:T(8,128)S(1)} %add.28), channel_id=1, source_target_pairs={{0,2},{2,0},{1,3},{3,1},{4,6},{6,4},{5,7},{7,5},{8,10},{10,8},{9,1... | collective-permute-start | bytes 540680 | tf_op jit(solution)/shard_map/ppermute | solution.py:275
  37.3 1.8 %collective-permute-start.13 = (f32[16,128]{1,0:T(8,128)S(1)}, f32[16,128]{1,0:T(8,128)S(1)}, u32[]{:S(2)}, u32[]{:S(2)}) collective-permute-start(f32[16,128]{1,0:T(8,128)S(1)} %slice.14), channel_id=1, source_target_pairs={{10,0},{11,1},{8,2},{9,3},{14,4},{15,5},{12,6},{13,7},{2,8},{3,9},... | collective-permute-start | bytes 24584 | tf_op jit(solution)/shard_map/ppermute | solution.py:269
  39.1 2.5 %collective-permute-done.9 = f32[32,1408]{1,0:T(8,128)S(1)} collective-permute-done((f32[32,1408]{1,0:T(8,128)S(1)}, f32[32,1408]{1,0:T(8,128)S(1)}, u32[]{:S(2)}, u32[]{:S(2)}) %collective-permute-start.9) | collective-permute-done | bytes 180256 | tf_op jit(solution)/shard_map/ppermute | solution.py:275
  41.7 1.7 %collective-permute-start.10 = (f32[32,1280]{1,0:T(8,128)S(1)}, f32[32,1280]{1,0:T(8,128)S(1)}, u32[]{:S(2)}, u32[]{:S(2)}) collective-permute-start(f32[32,1280]{1,0:T(8,128)S(1)} %slice.12), channel_id=1, source_target_pairs={{1,0},{6,1},{10,2},{13,3},{3,4},{4,5},{8,6},{15,7},{0,8},{7,9},{11... | collective-permute-start | bytes 491528 | tf_op jit(solution)/shard_map/ppermute | solution.py:269
  43.4 2.5 %collective-permute-start.14 = (f32[16,128]{1,0:T(8,128)S(1)}, f32[16,128]{1,0:T(8,128)S(1)}, u32[]{:S(2)}, u32[]{:S(2)}) collective-permute-start(f32[16,128]{1,0:T(8,128)S(1)} %fusion.1.mine_ref), channel_id=1, source_target_pairs={{0,4},{4,0},{8,12},{12,8},{1,5},{5,1},{9,13},{13,9},{2,6},{6,2},{1... | collective-permute-start | bytes 24584 | tf_op jit(solution)/shard_map/ppermute | solution.py:275
  45.9 3.5 %collective-permute-done.14.other_ref = f32[16,128]{1,0:T(8,128)S(1)} collective-permute-done((f32[16,128]{1,0:T(8,128)S(1)}, f32[16,128]{1,0:T(8,128)S(1)}, u32[]{:S(2)}, u32[]{:S(2)}) %collective-permute-start.14) | collective-permute-done | bytes 8224 | tf_op jit(solution)/shard_map/ppermute | solution.py:275
  50.0 0.7 %fusion = f32[1280,64]{0,1:T(8,128)} fusion(f32[32,1280]{1,0:T(8,128)S(1)} %collective-permute-done.11, f32[32,1280]{1,0:T(8,128)S(1)} %collective-permute-done.10, pred[]{:T(512)S(6)} %eq.3), kind=kLoop, calls=%fused_computation.1 | loop fusion | flops 245760 | bytes 655361 | tf_op jit(solution)/shard_map/transpose | solution.py:362
  (24 shorter events, 2.1 us)
Async XLA Ops:
  0.6 8.3 %collective-permute-start = (f32[64,1280]{1,0:T(8,128)}, f32[64,1280]{1,0:T(8,128)S(1)}, u32[]{:S(2)}, u32[]{:S(2)}) collective-permute-start(f32[64,1280]{1,0:T(8,128)} %bitcast.3), channel_id=1, source_target_pairs={{2,0},{4,1},{0,2},{6,3},{1,4},{7,5},{3,6},{5,7},{10,8},{12,9},{8,1... | collective-permute-start | bytes 983048 | tf_op jit(solution)/shard_map/ppermute | solution.py:269
  3.6 1.9 %copy-start = (bf16[1280,1280]{1,0:T(8,128)(2,1)S(1)}, bf16[1280,1280]{1,0:T(8,128)(2,1)}, u32[]{:S(2)}) copy-start(bf16[1280,1280]{1,0:T(8,128)(2,1)} %delta_ref.7) | copy-start | bytes 9830404
  5.6 5.0 %copy-start.1 = (f32[1280,64]{0,1:T(8,128)S(1)}, f32[1280,64]{0,1:T(8,128)}, u32[]{:S(2)}) copy-start(f32[1280,64]{0,1:T(8,128)} %param.3) | copy-start | bytes 983044
  8.9 1.6 %collective-permute-start.1 = (f32[64,1280]{1,0:T(8,128)S(1)}, f32[64,1280]{1,0:T(8,128)S(1)}, u32[]{:S(2)}, u32[]{:S(2)}) collective-permute-start(f32[64,1280]{1,0:T(8,128)S(1)} %collective-permute-done.got_ref), channel_id=1, source_target_pairs={{0,1},{1,0},{2,3},{3,2},{4,5},{5,4},{6,7},{7,6},{8,9},{9,8},{10,11... | collective-permute-start | bytes 983048 | tf_op jit(solution)/shard_map/ppermute | solution.py:272
  13.1 1.5 %collective-permute-start.2 = (f32[64,640]{1,0:T(8,128)S(1)}, f32[64,640]{1,0:T(8,128)S(1)}, u32[]{:S(2)}, u32[]{:S(2)}) collective-permute-start(f32[64,640]{1,0:T(8,128)S(1)} %get-tuple-element.15), channel_id=1, source_target_pairs={{0,1},{1,0},{2,3},{3,2},{4,5},{5,4},{6,7},{7,6},{8,9},{9,8},{10,11... | collective-permute-start | bytes 491528 | tf_op jit(solution)/shard_map/ppermute | solution.py:272
  14.6 8.6 %collective-permute-start.3 = (f32[64,640]{1,0:T(8,128)S(1)}, f32[64,640]{1,0:T(8,128)S(1)}, u32[]{:S(2)}, u32[]{:S(2)}) collective-permute-start(f32[64,640]{1,0:T(8,128)S(1)} %add.25), channel_id=1, source_target_pairs={{0,2},{2,0},{1,3},{3,1},{4,6},{6,4},{5,7},{7,5},{8,10},{10,8},{9,1... | collective-permute-start | bytes 491528 | tf_op jit(solution)/shard_map/ppermute | solution.py:275
  16.6 7.7 %collective-permute-start.6 = (f32[64,640]{1,0:T(8,128)S(1)}, f32[64,640]{1,0:T(8,128)S(1)}, u32[]{:S(2)}, u32[]{:S(2)}) collective-permute-start(f32[64,640]{1,0:T(8,128)S(1)} %add.25), channel_id=1, source_target_pairs={{1,0},{6,1},{10,2},{13,3},{3,4},{4,5},{8,6},{15,7},{0,8},{7,9},{11... | collective-permute-start | bytes 491528 | tf_op jit(solution)/shard_map/ppermute | solution.py:269
  19.2 5.4 %collective-permute-start.7 = (f32[64,640]{1,0:T(8,128)S(1)}, f32[64,640]{1,0:T(8,128)S(1)}, u32[]{:S(2)}, u32[]{:S(2)}) collective-permute-start(f32[64,640]{1,0:T(8,128)S(1)} %add.25), channel_id=1, source_target_pairs={{3,0},{4,1},{8,2},{15,3},{1,4},{6,5},{10,6},{13,7},{2,8},{5,9},{9,... | collective-permute-start | bytes 491528 | tf_op jit(solution)/shard_map/ppermute | solution.py:269
  23.2 1.5 %collective-permute-start.5 = (f32[64,640]{1,0:T(8,128)S(1)}, f32[64,640]{1,0:T(8,128)S(1)}, u32[]{:S(2)}, u32[]{:S(2)}) collective-permute-start(f32[64,640]{1,0:T(8,128)S(1)} %add.26.kept_ref), channel_id=1, source_target_pairs={{0,1},{1,0},{2,3},{3,2},{4,5},{5,4},{6,7},{7,6},{8,9},{9,8},{10,11... | collective-permute-start | bytes 491528 | tf_op jit(solution)/shard_map/ppermute | solution.py:272
  23.3 5.4 %collective-permute-start.4 = (f32[64,640]{1,0:T(8,128)S(1)}, f32[64,640]{1,0:T(8,128)S(1)}, u32[]{:S(2)}, u32[]{:S(2)}) collective-permute-start(f32[64,640]{1,0:T(8,128)S(1)} %add.26.kept_ref), channel_id=1, source_target_pairs={{2,0},{5,1},{11,2},{12,3},{0,4},{7,5},{9,6},{14,7},{1,8},{6,9},{8,... | collective-permute-start | bytes 491528 | tf_op jit(solution)/shard_map/ppermute | solution.py:269
  30.9 1.7 %collective-permute-start.8 = (f32[32,1408]{1,0:T(8,128)S(1)}, f32[32,1408]{1,0:T(8,128)S(1)}, u32[]{:S(2)}, u32[]{:S(2)}) collective-permute-start(f32[32,1408]{1,0:T(8,128)S(1)} %get-tuple-element.20), channel_id=1, source_target_pairs={{0,1},{1,0},{2,3},{3,2},{4,5},{5,4},{6,7},{7,6},{8,9},{9,8},{10,11... | collective-permute-start | bytes 540680 | tf_op jit(solution)/shard_map/ppermute | solution.py:272
  32.7 9.0 %collective-permute-start.9 = (f32[32,1408]{1,0:T(8,128)S(1)}, f32[32,1408]{1,0:T(8,128)S(1)}, u32[]{:S(2)}, u32[]{:S(2)}) collective-permute-start(f32[32,1408]{1,0:T(8,128)S(1)} %add.28), channel_id=1, source_target_pairs={{0,2},{2,0},{1,3},{3,1},{4,6},{6,4},{5,7},{7,5},{8,10},{10,8},{9,1... | collective-permute-start | bytes 540680 | tf_op jit(solution)/shard_map/ppermute | solution.py:275
  36.7 6.7 %collective-permute-start.12 = (f32[16,128]{1,0:T(8,128)S(1)}, f32[16,128]{1,0:T(8,128)S(1)}, u32[]{:S(2)}, u32[]{:S(2)}) collective-permute-start(f32[16,128]{1,0:T(8,128)S(1)} %slice.14), channel_id=1, source_target_pairs={{8,0},{9,1},{10,2},{11,3},{12,4},{13,5},{14,6},{15,7},{0,8},{1,9},... | collective-permute-start | bytes 24584 | tf_op jit(solution)/shard_map/ppermute | solution.py:269
  37.3 6.0 %collective-permute-start.13 = (f32[16,128]{1,0:T(8,128)S(1)}, f32[16,128]{1,0:T(8,128)S(1)}, u32[]{:S(2)}, u32[]{:S(2)}) collective-permute-start(f32[16,128]{1,0:T(8,128)S(1)} %slice.14), channel_id=1, source_target_pairs={{10,0},{11,1},{8,2},{9,3},{14,4},{15,5},{12,6},{13,7},{2,8},{3,9},... | collective-permute-start | bytes 24584 | tf_op jit(solution)/shard_map/ppermute | solution.py:269
  41.7 8.3 %collective-permute-start.10 = (f32[32,1280]{1,0:T(8,128)S(1)}, f32[32,1280]{1,0:T(8,128)S(1)}, u32[]{:S(2)}, u32[]{:S(2)}) collective-permute-start(f32[32,1280]{1,0:T(8,128)S(1)} %slice.12), channel_id=1, source_target_pairs={{1,0},{6,1},{10,2},{13,3},{3,4},{4,5},{8,6},{15,7},{0,8},{7,9},{11... | collective-permute-start | bytes 491528 | tf_op jit(solution)/shard_map/ppermute | solution.py:269
  43.4 6.6 %collective-permute-start.11 = (f32[32,1280]{1,0:T(8,128)S(1)}, f32[32,1280]{1,0:T(8,128)S(1)}, u32[]{:S(2)}, u32[]{:S(2)}) collective-permute-start(f32[32,1280]{1,0:T(8,128)S(1)} %slice.12), channel_id=1, source_target_pairs={{2,0},{5,1},{11,2},{12,3},{0,4},{7,5},{9,6},{14,7},{1,8},{6,9},{8,... | collective-permute-start | bytes 491528 | tf_op jit(solution)/shard_map/ppermute | solution.py:269
  43.4 6.0 %collective-permute-start.14 = (f32[16,128]{1,0:T(8,128)S(1)}, f32[16,128]{1,0:T(8,128)S(1)}, u32[]{:S(2)}, u32[]{:S(2)}) collective-permute-start(f32[16,128]{1,0:T(8,128)S(1)} %fusion.1.mine_ref), channel_id=1, source_target_pairs={{0,4},{4,0},{8,12},{12,8},{1,5},{5,1},{9,13},{13,9},{2,6},{6,2},{1... | collective-permute-start | bytes 24584 | tf_op jit(solution)/shard_map/ppermute | solution.py:275

commit v6 on v5

--- a/solution.py
+++ b/solution.py
@@ -13,7 +13,6 @@
 LANES = 128
 EXTRA = 16
 PIECE = 32
-TILE_SCRATCH = 8
 SUMS = 16
 
 f32 = jnp.float32
@@ -45,10 +44,10 @@
     return rows.astype(bf16)
 
 
-def tile_terms(row_pts, col_pts, delta_at, lhs, rhs, left, square, r_high, r_low, stress, emit):
+def tile_terms(row_pts, col_pts, delta_at, lhs, rhs, left, square, r_both, stress, emit):
     dims, rows = row_pts.shape
     cols = col_pts.shape[1]
-    step = r_high.shape[2]
+    step = r_both.shape[2]
     points = row_pts[...]
     shift = jnp.sum(points, axis=1, keepdims=True) * (1.0 / rows)
     points = points - shift
@@ -58,9 +57,11 @@
     lhs[...] = jnp.concatenate(
         [minus2(high), minus2(high), minus2(middle), norm_rows(points, True), jnp.zeros((fill, rows), bf16)], axis=0
     ).T
-    lft = jnp.concatenate([high, middle, jnp.ones((EXTRA, rows), bf16)], axis=0)
-    left[:, :rows] = lft
-    left[:, rows:] = lft
+    factors = jnp.concatenate([high, middle, jnp.ones((EXTRA, rows), bf16)], axis=0)
+    tall = r_both.shape[1] // 2
+    for row in range(0, rows, tall):
+        left[:, 2 * row:2 * row + tall] = factors[:, row:row + tall]
+        left[:, 2 * row + tall:2 * (row + tall)] = factors[:, row:row + tall]
     points = col_pts[...] - shift
     col_pts[...] = points
     high, middle = split2(points)
@@ -68,20 +69,22 @@
         [high, middle, high, norm_rows(points, False), jnp.zeros((fill, cols), bf16)], axis=0
     )
 
-    def gram(c):
-        square[c % 2] = jnp.dot(lhs[...], rhs[:, c * step:(c + 1) * step], preferred_element_type=f32)
+    units = [(row, col) for col in range(0, cols, step) for row in range(0, rows, tall)]
+
+    def gram(u):
+        row, col = units[u]
+        square[u % 2] = jnp.dot(lhs[row:row + tall, :], rhs[:, col:col + step], preferred_element_type=f32)
 
     misfit = jnp.zeros((16, step), f32)
+    terms = None
     gram(0)
-    for c in range(cols // step):
-        if (c + 1) * step < cols:
-            gram(c + 1)
-        js = pl.ds(c * step, step)
-        slot = c % 2
-        for p in range(rows // PIECE):
-            ps = pl.ds(p * PIECE, PIECE)
-            squared = square[slot, ps, :]
-            delta = delta_at(p * PIECE, js).astype(f32)
+    for u, (row, col) in enumerate(units):
+        if u + 1 < len(units):
+            gram(u + 1)
+        slot = u % 2
+        for p in range(0, tall, PIECE):
+            squared = square[slot, p:p + PIECE, :]
+            delta = delta_at(row + p, col, step).astype(f32)
             if stress:
                 inverse = lax.rsqrt(jnp.maximum(squared, TINY))
                 ratio = delta * jnp.minimum(inverse, 1.0 / FLOOR)
@@ -92,25 +95,29 @@
             else:
                 ratio = delta * lax.rsqrt(jnp.maximum(squared, FLOOR * FLOOR))
             high, low = split2(ratio)
-            r_high[slot, ps, :] = high
-            r_high[slot, pl.ds(rows + p * PIECE, PIECE), :] = low
-        terms = jnp.dot(left[...], r_high[slot], preferred_element_type=f32)
-        cross = terms[:dims] + terms[dims:2 * dims]
-        emit(js, col_pts[:, js] * terms[2 * dims:2 * dims + 1] - cross)
+            r_both[slot, p:p + PIECE, :] = high
+            r_both[slot, tall + p:tall + p + PIECE, :] = low
+        part = jnp.dot(left[:, 2 * row:2 * (row + tall)], r_both[slot], preferred_element_type=f32)
+        terms = part if terms is None else terms + part
+        if row + tall == rows:
+            cross = terms[:dims] + terms[dims:2 * dims]
+            js = pl.ds(col, step)
+            emit(js, col_pts[:, js] * terms[2 * dims:2 * dims + 1] - cross)
+            terms = None
     return jnp.sum(misfit) if stress else None
 
 
-def tile_scratch(dims, rows, cols):
-    step = 256 if cols % 256 == 0 else 128
+def tile_scratch(dims, rows, cols, tall=None, step=None):
+    tall = tall or rows
+    step = step or (256 if cols % 256 == 0 else LANES)
     return [
         pltpu.VMEM((dims, rows), f32),
         pltpu.VMEM((dims, cols), f32),
         pltpu.VMEM((rows, DEPTH), bf16),
         pltpu.VMEM((DEPTH, cols), bf16),
         pltpu.VMEM((2 * dims + EXTRA, 2 * rows), bf16),
-        pltpu.VMEM((2, rows, step), f32),
-        pltpu.VMEM((2, 2 * rows, step), bf16),
-        pltpu.VMEM((8, LANES), bf16),
+        pltpu.VMEM((2, tall, step), f32),
+        pltpu.VMEM((2, 2 * tall, step), bf16),
     ]
 
 
@@ -159,7 +166,7 @@
         def emit(js, part):
             result[:, js] = part * scale
 
-        tile_terms(row_pts, col_pts, lambda p, js: delta_ref[pl.ds(p, PIECE), js], *rest, False, emit)
+        tile_terms(row_pts, col_pts, lambda row, col, width: delta_ref[pl.ds(row, PIECE), pl.ds(col, width)], *rest, False, emit)
         for ref, which in ((keep_ref, a), (send_ref, 1 - a)):
             ref[...] = result[:, pl.ds(pl.multiple_of(which * half, LANES), half)]
 
@@ -168,15 +175,12 @@
     return call(body, "tile_first", outs, scratch, tile_cost(rows, cols), delta, own, got, passed)
 
 
-def next_tile(side_of, scale, delta, rows_in, kept, passed, norm, before=None):
+def open_tile(side_of, delta, rows_in, kept, passed, norm):
     dims, rows = rows_in.shape
     cols = delta.shape[1]
-    half, less = cols // 2, dims // 2
-    closing = before is not None
-
-    def body(delta_ref, rows_ref, kept_ref, passed_ref, sums_ref, *refs):
-        row_pts, col_pts, *rest = refs[-TILE_SCRATCH:]
-        refs = refs[:-TILE_SCRATCH]
+    half = cols // 2
+
+    def body(delta_ref, rows_ref, kept_ref, passed_ref, norm_ref, part_ref, sums_ref, row_pts, col_pts, *rest):
         a = lax.axis_index("aux")
         at = lambda which: pl.ds(pl.multiple_of(which * half, LANES), half)
         base = side_of() * rows
@@ -184,39 +188,47 @@
         col_pts[:, at(a)] = kept_ref[...]
         col_pts[:, at(1 - a)] = passed_ref[...]
 
-        def delta_at(p, js):
-            return delta_ref[pl.ds(pl.multiple_of(base + p, PIECE), PIECE), js]
-
-        if not closing:
-            part_ref, out_sums_ref = refs
-
-            def emit(js, part):
-                part_ref[:, js] = part
-
-            misfit = tile_terms(row_pts, col_pts, delta_at, *rest, True, emit)
-            out_sums_ref[:8] = jnp.full((8, LANES), misfit)
-            out_sums_ref[8:] = sums_ref[...]
-            return
-        before_ref, keep_ref, send_ref, result = refs
+        def delta_at(row, col, width):
+            return delta_ref[pl.ds(pl.multiple_of(base + row, PIECE), PIECE), pl.ds(col, width)]
 
         def emit(js, part):
-            result[:, js] = (before_ref[:, js] + part) * scale
+            part_ref[:, js] = part
 
         misfit = tile_terms(row_pts, col_pts, delta_at, *rest, True, emit)
-        for ref, which in ((keep_ref, a), (send_ref, 1 - a)):
-            ref[:, :cols] = result[pl.ds(pl.multiple_of(which * less, 8), less), :]
-            ref[:8, cols:] = sums_ref[:8] + misfit
-            ref[8:16, cols:] = sums_ref[8:]
-            ref[16:, cols:] = jnp.zeros((less - 16, LANES), f32)
-
+        sums_ref[:8] = jnp.full((8, LANES), misfit)
+        sums_ref[8:] = norm_ref[...]
+
+    outs = [(dims, cols), (SUMS, LANES)]
     scratch = tile_scratch(dims, rows, cols)
-    cost = tile_cost(rows, cols)
-    if not closing:
-        outs = [(dims, cols), (SUMS, LANES)]
-        return call(body, "tile_open", outs, scratch, cost, delta, rows_in, kept, passed, norm)
-    scratch = [pltpu.VMEM((dims, cols), f32)] + scratch
-    outs = [(less, cols + LANES)] * 2
-    return call(body, "tile_close", outs, scratch, cost, delta, rows_in, kept, passed, norm, before)
+    return call(body, "tile_open", outs, scratch, tile_cost(rows, cols), delta, rows_in, kept, passed, norm)
+
+
+def close_tile(side_of, which_of, scale, delta, rows_in, columns, part, sums):
+    dims, rows = rows_in.shape
+    half = columns.shape[1]
+
+    def body(delta_ref, rows_ref, columns_ref, part_ref, sums_ref, out_ref, out_sums_ref, row_pts, col_pts, *rest):
+        base = side_of() * rows
+        first = which_of() * half
+        row_pts[...] = rows_ref[...]
+        col_pts[...] = columns_ref[...]
+
+        def delta_at(row, col, width):
+            return delta_ref[
+                pl.ds(pl.multiple_of(base + row, PIECE), PIECE), pl.ds(pl.multiple_of(first + col, LANES), width)
+            ]
+
+        def emit(js, new):
+            before = part_ref[:, pl.ds(pl.multiple_of(first + js.start, LANES), js.size)]
+            out_ref[:, js] = (before + new) * scale
+
+        misfit = tile_terms(row_pts, col_pts, delta_at, *rest, True, emit)
+        out_sums_ref[:8] = sums_ref[:8] + misfit
+        out_sums_ref[8:] = sums_ref[8:]
+
+    outs = [(dims, half), (SUMS, LANES)]
+    scratch = tile_scratch(dims, rows, half, rows, half)
+    return call(body, "tile_close", outs, scratch, tile_cost(rows, half), delta, rows_in, columns, part, sums)
 
 
 def norm_body(delta_ref, out_ref):
@@ -334,30 +346,31 @@
     first = first[0] + first[1]
     second = grid.send(half, grid.spread(True))
     other = grid.other_core(half)
-    part, sums = next_tile(grid.spread_half, scale, dissimilarity, first, half, other, norm)
-    keep, send = next_tile(lambda: 1 - grid.spread_half(), scale, dissimilarity, second, half, other, sums, part)
+    part, sums = open_tile(grid.spread_half, dissimilarity, first, half, other, norm)
+    late = lambda: 1 - grid.spread_half()
+    mine = lambda: lax.axis_index("aux")
+    send, sums = close_tile(late, lambda: 1 - mine(), scale, dissimilarity, second, other, part, sums)
+    keep, sums = close_tile(late, mine, scale, dissimilarity, second, half, part, sums)
 
     half = keep + grid.other_core(send)
-    early = []
     if grid.wide == 4:
-        sums = half[:SUMS, cols:]
-        early = [grid.send(sums, lambda x, a, z: (x, a, z ^ 2)), grid.send(sums, lambda x, a, z: (x ^ 1, a, z ^ 2))]
+        across = [grid.send(sums, lambda x, a, z, m=m, n=n: (x ^ m, a, z ^ n)) for m, n in ((0, 2), (1, 2), (1, 0))]
+        sums = sums + across[0] + across[1] + across[2]
+    else:
+        for bit in bits(grid.narrow):
+            sums = sums + grid.across(sums, "narrow", bit)
+        for bit in bits(grid.wide)[1:]:
+            sums = sums + grid.across(sums, "wide", bit)
     for bit in bits(grid.narrow):
         half = half + grid.across(half, "narrow", bit)
-    sums = half[:SUMS, cols:]
-    if not early:
-        for bit in bits(grid.wide)[1:]:
-            sums = sums + grid.across(sums, "wide", bit)
-    for part in early:
-        sums = sums + part
-    half = half[:, :cols]
     first = grid.send(half, grid.spread(False))
     second = grid.send(half, grid.spread(True))
+    sums = sums + grid.other_core(sums)
     stress = stress_call(sums, grid.across(sums, "wide", 1))
     first, second, stress = lax.optimization_barrier((first, second, stress))
     in_order = grid.spread_half() == 0
     embedding = jnp.where(
-        in_order, jnp.concatenate([first, second], axis=0), jnp.concatenate([second, first], axis=0)
+        in_order, jnp.concatenate([first, second], axis=1), jnp.concatenate([second, first], axis=1)
     )
     return embedding.T, stress
 

time: 51.7 us -> 51.2 us (level); the launches traced: 50.8 us -> 50.9 us
  waiting for transfers between devices: 17.6 us -> 14.3 us
  starting transfers between devices: 21.3 us -> 23.9 us
  Pallas kernels: 8.24 us -> 9.07 us
    ppermute x3, waiting for transfers between devices: 9.06 us -> 5.98 us  [across(): lax.ppermute(value, axis, [(i, i ^ bit) for i in range(lax.axis_size(axis...]
    ppermute x8 -> x9, starting transfers between devices: 11.6 us -> 13.3 us  [send(): return lax.ppermute(value, AXES, self.pairs(source))]
    pallas_call x4 -> x5, Pallas kernels: 7.68 us -> 8.51 us  [call(): pl.pallas_call(body, out_shape=[jax.ShapeDtypeStruct(shape, f32) for shap...]
    ppermute x4 -> x5, starting transfers between devices: 1.05 us -> 1.5 us  [other_core(): return lax.ppermute(value, 'aux', [(0, 1), (1, 0)])]
    ppermute x4 -> x5, waiting for transfers between devices: 3.89 us -> 3.67 us  [other_core(): return lax.ppermute(value, 'aux', [(0, 1), (1, 0)])]
    ppermute x8 -> x9, waiting for transfers between devices: 4.68 us -> 4.69 us  [send(): return lax.ppermute(value, AXES, self.pairs(source))]
  transfers between devices with their start and end apart: 15 -> 17, of which waited for: 10 -> 10; matrix products, arithmetic and copies ran while one was open for 0% -> 0% of each run, Pallas kernels for 7% -> 10%
where the time goes in v6:
time: 51.2 us; the launch traced here: 50.9 us
  starting transfers between devices  23.9 us (47%)
  waiting for transfers between devices  14.3 us (28%)
  Pallas kernels  9.07 us (18%)
  local copies, waits for them, and re-layouts  1.93 us (4%)
  other arithmetic  0.87 us (2%)
  between operations  0.75 us (1%)
    ppermute x9, starting transfers between devices, send(): return lax.ppermute(value, AXES, self.pairs(source))  13.3 us
    ppermute x3, starting transfers between devices, across(): lax.ppermute(value, axis, [(i, i ^ bit) for i in range(lax.axis_size(axis...  9.11 us
    pallas_call x5, Pallas kernels, call(): pl.pallas_call(body, out_shape=[jax.ShapeDtypeStruct(shape, f32) for shap...  8.51 us
    ppermute x3, waiting for transfers between devices, across(): lax.ppermute(value, axis, [(i, i ^ bit) for i in range(lax.axis_size(axis...  5.98 us
    ppermute x9, waiting for transfers between devices, send(): return lax.ppermute(value, AXES, self.pairs(source))  4.69 us
    ppermute x5, waiting for transfers between devices, other_core(): return lax.ppermute(value, 'aux', [(0, 1), (1, 0)])  3.67 us
    unnamed x4, local copies, waits for them, and re-layouts  1.93 us
    ppermute x5, starting transfers between devices, other_core(): return lax.ppermute(value, 'aux', [(0, 1), (1, 0)])  1.5 us
  transfers between devices with their start and end apart: 17, of which 10 were waited for; matrix products, arithmetic and copies ran while one was open for 0% of the time, Pallas kernels for 10%

profile of v6, /device:TPU:0, one launch (start us, length us, event | category | flops | bytes accessed | tf_op | source)
XLA Modules:
  0.0 50.9 jit_solution(10620305302460088765)
XLA Ops:
  0.6 3.0 %collective-permute-start = (f32[64,1280]{1,0:T(8,128)}, f32[64,1280]{1,0:T(8,128)S(1)}, u32[]{:S(2)}, u32[]{:S(2)}) collective-permute-start(f32[64,1280]{1,0:T(8,128)} %bitcast.3), channel_id=1, source_target_pairs={{2,0},{4,1},{0,2},{6,3},{1,4},{7,5},{3,6},{5,7},{10,8},{12,9},{8,1... | collective-permute-start | bytes 983048 | tf_op jit(solution)/shard_map/ppermute | solution.py:281
  3.6 1.9 %copy-done = bf16[1280,1280]{1,0:T(8,128)(2,1)S(1)} copy-done((bf16[1280,1280]{1,0:T(8,128)(2,1)S(1)}, bf16[1280,1280]{1,0:T(8,128)(2,1)}, u32[]{:S(2)}) %copy-start) | copy-done | bytes 3276824
  5.6 0.8 %norm.1.norm_ref = f32[8,128]{1,0:T(8,128)S(1)} custom-call(bf16[1280,1280]{1,0:T(8,128)(2,1)S(1)} %copy-done), custom_call_target="tpu_custom_call" | custom-call | flops 6553600 | bytes 3276800 | tf_op jit(solution)/shard_map/norm/pallas_call | solution.py:127
  6.3 2.6 %collective-permute-done.got_ref = f32[64,1280]{1,0:T(8,128)S(1)} collective-permute-done((f32[64,1280]{1,0:T(8,128)}, f32[64,1280]{1,0:T(8,128)S(1)}, u32[]{:S(2)}, u32[]{:S(2)}) %collective-permute-start) | collective-permute-done | bytes 327712 | tf_op jit(solution)/shard_map/ppermute | solution.py:281
  9.0 1.5 %collective-permute-done.1.passed_ref = f32[64,1280]{1,0:T(8,128)S(1)} collective-permute-done((f32[64,1280]{1,0:T(8,128)S(1)}, f32[64,1280]{1,0:T(8,128)S(1)}, u32[]{:S(2)}, u32[]{:S(2)}) %collective-permute-start.1) | collective-permute-done | bytes 327712 | tf_op jit(solution)/shard_map/ppermute | solution.py:284
  10.5 2.5 %tile_first.1 = (f32[64,640]{1,0:T(8,128)S(1)}, f32[64,640]{1,0:T(8,128)S(1)}) custom-call(bf16[1280,1280]{1,0:T(8,128)(2,1)S(1)} %copy-done, f32[64,1280]{1,0:T(8,128)S(1)} %bitcast.4, f32[64,1280]{1,0:T(8,128)S(1)} %collective-permute-done.got_ref, f32[64,1280]{1,0:T(8,128)S(1)} %collective-permute-done.1.passed_ref), custom_call_target="tpu_custom_call" | custom-call | flops 2516582400 | bytes 3276800 | tf_op jit(solution)/shard_map/tile_first/pallas_call | solution.py:127
  13.3 1.3 %collective-permute-done.2 = f32[64,640]{1,0:T(8,128)S(1)} collective-permute-done((f32[64,640]{1,0:T(8,128)S(1)}, f32[64,640]{1,0:T(8,128)S(1)}, u32[]{:S(2)}, u32[]{:S(2)}) %collective-permute-start.2) | collective-permute-done | bytes 163872 | tf_op jit(solution)/shard_map/ppermute | solution.py:284
  14.6 2.1 %collective-permute-start.3 = (f32[64,640]{1,0:T(8,128)S(1)}, f32[64,640]{1,0:T(8,128)S(1)}, u32[]{:S(2)}, u32[]{:S(2)}) collective-permute-start(f32[64,640]{1,0:T(8,128)S(1)} %add.31), channel_id=1, source_target_pairs={{0,2},{2,0},{1,3},{3,1},{4,6},{6,4},{5,7},{7,5},{8,10},{10,8},{9,1... | collective-permute-start | bytes 491528 | tf_op jit(solution)/shard_map/ppermute | solution.py:287
  16.6 2.6 %collective-permute-start.5 = (f32[64,640]{1,0:T(8,128)S(1)}, f32[64,640]{1,0:T(8,128)S(1)}, u32[]{:S(2)}, u32[]{:S(2)}) collective-permute-start(f32[64,640]{1,0:T(8,128)S(1)} %add.31), channel_id=1, source_target_pairs={{1,0},{6,1},{10,2},{13,3},{3,4},{4,5},{8,6},{15,7},{0,8},{7,9},{11... | collective-permute-start | bytes 491528 | tf_op jit(solution)/shard_map/ppermute | solution.py:281
  19.2 0.9 %collective-permute-start.6 = (f32[64,640]{1,0:T(8,128)S(1)}, f32[64,640]{1,0:T(8,128)S(1)}, u32[]{:S(2)}, u32[]{:S(2)}) collective-permute-start(f32[64,640]{1,0:T(8,128)S(1)} %add.31), channel_id=1, source_target_pairs={{3,0},{4,1},{8,2},{15,3},{1,4},{6,5},{10,6},{13,7},{2,8},{5,9},{9,... | collective-permute-start | bytes 491528 | tf_op jit(solution)/shard_map/ppermute | solution.py:281
  20.1 3.1 %collective-permute-done.3 = f32[64,640]{1,0:T(8,128)S(1)} collective-permute-done((f32[64,640]{1,0:T(8,128)S(1)}, f32[64,640]{1,0:T(8,128)S(1)}, u32[]{:S(2)}, u32[]{:S(2)}) %collective-permute-start.3) | collective-permute-done | bytes 163872 | tf_op jit(solution)/shard_map/ppermute | solution.py:287
  23.3 1.0 %collective-permute-start.4 = (f32[64,640]{1,0:T(8,128)S(1)}, f32[64,640]{1,0:T(8,128)S(1)}, u32[]{:S(2)}, u32[]{:S(2)}) collective-permute-start(f32[64,640]{1,0:T(8,128)S(1)} %add.32.kept_ref.columns_ref), channel_id=1, source_target_pairs={{2,0},{5,1},{11,2},{12,3},{0,4},{7,5},{9,6},{14,7},{1,8},{6,9},{8,... | collective-permute-start | bytes 491528 | tf_op jit(solution)/shard_map/ppermute | solution.py:281
  24.7 2.2 %tile_open.1 = (f32[64,1280]{1,0:T(8,128)S(1)}, f32[16,128]{1,0:T(8,128)S(1)}) custom-call(bf16[1280,1280]{1,0:T(8,128)(2,1)S(1)} %copy-done, f32[64,640]{1,0:T(8,128)S(1)} %add.33.rows_ref, f32[64,640]{1,0:T(8,128)S(1)} %add.32.kept_ref.columns_ref, f32[64,640]{1,0:T(8,128)S(1)} %collective-permute-done.7.passed_ref.columns_ref, f32[8,128]{1,0:T(8,128)S(1)} %norm.1.norm_ref), custom_call_target="tpu_custom_call" | custom-call | flops 1258291200 | bytes 1638400 | tf_op jit(solution)/shard_map/tile_open/pallas_call | solution.py:127
  26.9 1.8 %collective-permute-done.4.rows_ref = f32[64,640]{1,0:T(8,128)S(1)} collective-permute-done((f32[64,640]{1,0:T(8,128)S(1)}, f32[64,640]{1,0:T(8,128)S(1)}, u32[]{:S(2)}, u32[]{:S(2)}) %collective-permute-start.4) | collective-permute-done | bytes 163872 | tf_op jit(solution)/shard_map/ppermute | solution.py:281
  28.7 1.5 %tile_close.2 = (f32[64,640]{1,0:T(8,128)S(1)}, f32[16,128]{1,0:T(8,128)S(1)}) custom-call(bf16[1280,1280]{1,0:T(8,128)(2,1)S(1)} %copy-done, f32[64,640]{1,0:T(8,128)S(1)} %collective-permute-done.4.rows_ref, f32[64,640]{1,0:T(8,128)S(1)} %collective-permute-done.7.passed_ref.columns_ref, f32[64,1280]{1,0:T(8,128)S(1)} %get-tuple-element.19.part_ref, ...), custom_call_target="tpu_custom_call" | custom-call | flops 629145600 | bytes 819200 | tf_op jit(solution)/shard_map/tile_close/pallas_call | solution.py:127
  30.9 1.5 %tile_close.3 = (f32[64,640]{1,0:T(8,128)S(1)}, f32[16,128]{1,0:T(8,128)S(1)}) custom-call(bf16[1280,1280]{1,0:T(8,128)(2,1)S(1)} %copy-done, f32[64,640]{1,0:T(8,128)S(1)} %collective-permute-done.4.rows_ref, f32[64,640]{1,0:T(8,128)S(1)} %add.32.kept_ref.columns_ref, f32[64,1280]{1,0:T(8,128)S(1)} %get-tuple-element.19.part_ref, ...), custom_call_target="tpu_custom_call" | custom-call | flops 629145600 | bytes 819200 | tf_op jit(solution)/shard_map/tile_close/pallas_call | solution.py:127
  32.4 3.7 %collective-permute-start.9 = (f32[64,640]{1,0:T(8,128)S(1)}, f32[64,640]{1,0:T(8,128)S(1)}, u32[]{:S(2)}, u32[]{:S(2)}) collective-permute-start(f32[64,640]{1,0:T(8,128)S(1)} %add.34), channel_id=1, source_target_pairs={{0,2},{2,0},{1,3},{3,1},{4,6},{6,4},{5,7},{7,5},{8,10},{10,8},{9,1... | collective-permute-start | bytes 491528 | tf_op jit(solution)/shard_map/ppermute | solution.py:287
  36.8 1.8 %collective-permute-start.13 = (f32[16,128]{1,0:T(8,128)S(1)}, f32[16,128]{1,0:T(8,128)S(1)}, u32[]{:S(2)}, u32[]{:S(2)}) collective-permute-start(f32[16,128]{1,0:T(8,128)S(1)} %get-tuple-element.24), channel_id=1, source_target_pairs={{10,0},{11,1},{8,2},{9,3},{14,4},{15,5},{12,6},{13,7},{2,8},{3,9},... | collective-permute-start | bytes 24584 | tf_op jit(solution)/shard_map/ppermute | solution.py:281
  38.6 1.9 %collective-permute-start.14 = (f32[16,128]{1,0:T(8,128)S(1)}, f32[16,128]{1,0:T(8,128)S(1)}, u32[]{:S(2)}, u32[]{:S(2)}) collective-permute-start(f32[16,128]{1,0:T(8,128)S(1)} %get-tuple-element.24), channel_id=1, source_target_pairs={{2,0},{3,1},{0,2},{1,3},{6,4},{7,5},{4,6},{5,7},{10,8},{11,9},{8,1... | collective-permute-start | bytes 24584 | tf_op jit(solution)/shard_map/ppermute | solution.py:281
  41.0 1.4 %collective-permute-start.10 = (f32[64,640]{1,0:T(8,128)S(1)}, f32[64,640]{1,0:T(8,128)S(1)}, u32[]{:S(2)}, u32[]{:S(2)}) collective-permute-start(f32[64,640]{1,0:T(8,128)S(1)} %add.35), channel_id=1, source_target_pairs={{1,0},{6,1},{10,2},{13,3},{3,4},{4,5},{8,6},{15,7},{0,8},{7,9},{11... | collective-permute-start | bytes 491528 | tf_op jit(solution)/shard_map/ppermute | solution.py:281
  42.9 0.8 %collective-permute-done.15 = f32[16,128]{1,0:T(8,128)S(1)} collective-permute-done((f32[16,128]{1,0:T(8,128)S(1)}, f32[16,128]{1,0:T(8,128)S(1)}, u32[]{:S(2)}, u32[]{:S(2)}) %collective-permute-start.15) | collective-permute-done | bytes 8224 | tf_op jit(solution)/shard_map/ppermute | solution.py:284
  43.8 3.3 %collective-permute-start.16 = (f32[16,128]{1,0:T(8,128)S(1)}, f32[16,128]{1,0:T(8,128)S(1)}, u32[]{:S(2)}, u32[]{:S(2)}) collective-permute-start(f32[16,128]{1,0:T(8,128)S(1)} %add.39.mine_ref), channel_id=1, source_target_pairs={{0,4},{4,0},{8,12},{12,8},{1,5},{5,1},{9,13},{13,9},{2,6},{6,2},{1... | collective-permute-start | bytes 24584 | tf_op jit(solution)/shard_map/ppermute | solution.py:287
  47.1 2.4 %collective-permute-done.16.other_ref = f32[16,128]{1,0:T(8,128)S(1)} collective-permute-done((f32[16,128]{1,0:T(8,128)S(1)}, f32[16,128]{1,0:T(8,128)S(1)}, u32[]{:S(2)}, u32[]{:S(2)}) %collective-permute-start.16) | collective-permute-done | bytes 8224 | tf_op jit(solution)/shard_map/ppermute | solution.py:287
  50.1 0.7 %fusion = f32[1280,64]{0,1:T(8,128)} fusion(f32[64,640]{1,0:T(8,128)S(1)} %collective-permute-done.11, f32[64,640]{1,0:T(8,128)S(1)} %collective-permute-done.10, pred[]{:T(512)S(6)} %eq.3), kind=kLoop, calls=%fused_computation.1 | loop fusion | flops 245760 | bytes 655361 | tf_op jit(solution)/shard_map/transpose | solution.py:375
  (28 shorter events, 3.7 us)
Async XLA Ops:
  0.6 8.3 %collective-permute-start = (f32[64,1280]{1,0:T(8,128)}, f32[64,1280]{1,0:T(8,128)S(1)}, u32[]{:S(2)}, u32[]{:S(2)}) collective-permute-start(f32[64,1280]{1,0:T(8,128)} %bitcast.3), channel_id=1, source_target_pairs={{2,0},{4,1},{0,2},{6,3},{1,4},{7,5},{3,6},{5,7},{10,8},{12,9},{8,1... | collective-permute-start | bytes 983048 | tf_op jit(solution)/shard_map/ppermute | solution.py:281
  3.6 1.9 %copy-start = (bf16[1280,1280]{1,0:T(8,128)(2,1)S(1)}, bf16[1280,1280]{1,0:T(8,128)(2,1)}, u32[]{:S(2)}) copy-start(bf16[1280,1280]{1,0:T(8,128)(2,1)} %delta_ref.9) | copy-start | bytes 9830404
  5.6 5.0 %copy-start.1 = (f32[1280,64]{0,1:T(8,128)S(1)}, f32[1280,64]{0,1:T(8,128)}, u32[]{:S(2)}) copy-start(f32[1280,64]{0,1:T(8,128)} %param.3) | copy-start | bytes 983044
  8.9 1.6 %collective-permute-start.1 = (f32[64,1280]{1,0:T(8,128)S(1)}, f32[64,1280]{1,0:T(8,128)S(1)}, u32[]{:S(2)}, u32[]{:S(2)}) collective-permute-start(f32[64,1280]{1,0:T(8,128)S(1)} %collective-permute-done.got_ref), channel_id=1, source_target_pairs={{0,1},{1,0},{2,3},{3,2},{4,5},{5,4},{6,7},{7,6},{8,9},{9,8},{10,11... | collective-permute-start | bytes 983048 | tf_op jit(solution)/shard_map/ppermute | solution.py:284
  13.1 1.5 %collective-permute-start.2 = (f32[64,640]{1,0:T(8,128)S(1)}, f32[64,640]{1,0:T(8,128)S(1)}, u32[]{:S(2)}, u32[]{:S(2)}) collective-permute-start(f32[64,640]{1,0:T(8,128)S(1)} %get-tuple-element.17), channel_id=1, source_target_pairs={{0,1},{1,0},{2,3},{3,2},{4,5},{5,4},{6,7},{7,6},{8,9},{9,8},{10,11... | collective-permute-start | bytes 491528 | tf_op jit(solution)/shard_map/ppermute | solution.py:284
  14.6 8.6 %collective-permute-start.3 = (f32[64,640]{1,0:T(8,128)S(1)}, f32[64,640]{1,0:T(8,128)S(1)}, u32[]{:S(2)}, u32[]{:S(2)}) collective-permute-start(f32[64,640]{1,0:T(8,128)S(1)} %add.31), channel_id=1, source_target_pairs={{0,2},{2,0},{1,3},{3,1},{4,6},{6,4},{5,7},{7,5},{8,10},{10,8},{9,1... | collective-permute-start | bytes 491528 | tf_op jit(solution)/shard_map/ppermute | solution.py:287
  16.6 7.7 %collective-permute-start.5 = (f32[64,640]{1,0:T(8,128)S(1)}, f32[64,640]{1,0:T(8,128)S(1)}, u32[]{:S(2)}, u32[]{:S(2)}) collective-permute-start(f32[64,640]{1,0:T(8,128)S(1)} %add.31), channel_id=1, source_target_pairs={{1,0},{6,1},{10,2},{13,3},{3,4},{4,5},{8,6},{15,7},{0,8},{7,9},{11... | collective-permute-start | bytes 491528 | tf_op jit(solution)/shard_map/ppermute | solution.py:281
  19.2 5.4 %collective-permute-start.6 = (f32[64,640]{1,0:T(8,128)S(1)}, f32[64,640]{1,0:T(8,128)S(1)}, u32[]{:S(2)}, u32[]{:S(2)}) collective-permute-start(f32[64,640]{1,0:T(8,128)S(1)} %add.31), channel_id=1, source_target_pairs={{3,0},{4,1},{8,2},{15,3},{1,4},{6,5},{10,6},{13,7},{2,8},{5,9},{9,... | collective-permute-start | bytes 491528 | tf_op jit(solution)/shard_map/ppermute | solution.py:281
  23.2 1.5 %collective-permute-start.7 = (f32[64,640]{1,0:T(8,128)S(1)}, f32[64,640]{1,0:T(8,128)S(1)}, u32[]{:S(2)}, u32[]{:S(2)}) collective-permute-start(f32[64,640]{1,0:T(8,128)S(1)} %add.32.kept_ref.columns_ref), channel_id=1, source_target_pairs={{0,1},{1,0},{2,3},{3,2},{4,5},{5,4},{6,7},{7,6},{8,9},{9,8},{10,11... | collective-permute-start | bytes 491528 | tf_op jit(solution)/shard_map/ppermute | solution.py:284
  23.3 5.4 %collective-permute-start.4 = (f32[64,640]{1,0:T(8,128)S(1)}, f32[64,640]{1,0:T(8,128)S(1)}, u32[]{:S(2)}, u32[]{:S(2)}) collective-permute-start(f32[64,640]{1,0:T(8,128)S(1)} %add.32.kept_ref.columns_ref), channel_id=1, source_target_pairs={{2,0},{5,1},{11,2},{12,3},{0,4},{7,5},{9,6},{14,7},{1,8},{6,9},{8,... | collective-permute-start | bytes 491528 | tf_op jit(solution)/shard_map/ppermute | solution.py:281
  30.2 2.2 %collective-permute-start.8 = (f32[64,640]{1,0:T(8,128)S(1)}, f32[64,640]{1,0:T(8,128)S(1)}, u32[]{:S(2)}, u32[]{:S(2)}) collective-permute-start(f32[64,640]{1,0:T(8,128)S(1)} %get-tuple-element.23), channel_id=1, source_target_pairs={{0,1},{1,0},{2,3},{3,2},{4,5},{5,4},{6,7},{7,6},{8,9},{9,8},{10,11... | collective-permute-start | bytes 491528 | tf_op jit(solution)/shard_map/ppermute | solution.py:284
  32.4 8.6 %collective-permute-start.9 = (f32[64,640]{1,0:T(8,128)S(1)}, f32[64,640]{1,0:T(8,128)S(1)}, u32[]{:S(2)}, u32[]{:S(2)}) collective-permute-start(f32[64,640]{1,0:T(8,128)S(1)} %add.34), channel_id=1, source_target_pairs={{0,2},{2,0},{1,3},{3,1},{4,6},{6,4},{5,7},{7,5},{8,10},{10,8},{9,1... | collective-permute-start | bytes 491528 | tf_op jit(solution)/shard_map/ppermute | solution.py:287
  36.1 6.3 %collective-permute-start.12 = (f32[16,128]{1,0:T(8,128)S(1)}, f32[16,128]{1,0:T(8,128)S(1)}, u32[]{:S(2)}, u32[]{:S(2)}) collective-permute-start(f32[16,128]{1,0:T(8,128)S(1)} %get-tuple-element.24), channel_id=1, source_target_pairs={{8,0},{9,1},{10,2},{11,3},{12,4},{13,5},{14,6},{15,7},{0,8},{1,9},... | collective-permute-start | bytes 24584 | tf_op jit(solution)/shard_map/ppermute | solution.py:281
  36.8 5.7 %collective-permute-start.13 = (f32[16,128]{1,0:T(8,128)S(1)}, f32[16,128]{1,0:T(8,128)S(1)}, u32[]{:S(2)}, u32[]{:S(2)}) collective-permute-start(f32[16,128]{1,0:T(8,128)S(1)} %get-tuple-element.24), channel_id=1, source_target_pairs={{10,0},{11,1},{8,2},{9,3},{14,4},{15,5},{12,6},{13,7},{2,8},{3,9},... | collective-permute-start | bytes 24584 | tf_op jit(solution)/shard_map/ppermute | solution.py:281
  38.6 3.9 %collective-permute-start.14 = (f32[16,128]{1,0:T(8,128)S(1)}, f32[16,128]{1,0:T(8,128)S(1)}, u32[]{:S(2)}, u32[]{:S(2)}) collective-permute-start(f32[16,128]{1,0:T(8,128)S(1)} %get-tuple-element.24), channel_id=1, source_target_pairs={{2,0},{3,1},{0,2},{1,3},{6,4},{7,5},{4,6},{5,7},{10,8},{11,9},{8,1... | collective-permute-start | bytes 24584 | tf_op jit(solution)/shard_map/ppermute | solution.py:281
  41.0 9.0 %collective-permute-start.10 = (f32[64,640]{1,0:T(8,128)S(1)}, f32[64,640]{1,0:T(8,128)S(1)}, u32[]{:S(2)}, u32[]{:S(2)}) collective-permute-start(f32[64,640]{1,0:T(8,128)S(1)} %add.35), channel_id=1, source_target_pairs={{1,0},{6,1},{10,2},{13,3},{3,4},{4,5},{8,6},{15,7},{0,8},{7,9},{11... | collective-permute-start | bytes 491528 | tf_op jit(solution)/shard_map/ppermute | solution.py:281
  42.4 7.7 %collective-permute-start.11 = (f32[64,640]{1,0:T(8,128)S(1)}, f32[64,640]{1,0:T(8,128)S(1)}, u32[]{:S(2)}, u32[]{:S(2)}) collective-permute-start(f32[64,640]{1,0:T(8,128)S(1)} %add.35), channel_id=1, source_target_pairs={{2,0},{5,1},{11,2},{12,3},{0,4},{7,5},{9,6},{14,7},{1,8},{6,9},{8,... | collective-permute-start | bytes 491528 | tf_op jit(solution)/shard_map/ppermute | solution.py:281
  42.5 1.3 %collective-permute-start.15 = (f32[16,128]{1,0:T(8,128)S(1)}, f32[16,128]{1,0:T(8,128)S(1)}, u32[]{:S(2)}, u32[]{:S(2)}) collective-permute-start(f32[16,128]{1,0:T(8,128)S(1)} %add_add_fusion), channel_id=1, source_target_pairs={{0,1},{1,0},{2,3},{3,2},{4,5},{5,4},{6,7},{7,6},{8,9},{9,8},{10,11... | collective-permute-start | bytes 24584 | tf_op jit(solution)/shard_map/ppermute | solution.py:284
  43.8 5.7 %collective-permute-start.16 = (f32[16,128]{1,0:T(8,128)S(1)}, f32[16,128]{1,0:T(8,128)S(1)}, u32[]{:S(2)}, u32[]{:S(2)}) collective-permute-start(f32[16,128]{1,0:T(8,128)S(1)} %add.39.mine_ref), channel_id=1, source_target_pairs={{0,4},{4,0},{8,12},{12,8},{1,5},{5,1},{9,13},{13,9},{2,6},{6,2},{1... | collective-permute-start | bytes 24584 | tf_op jit(solution)/shard_map/ppermute | solution.py:287

commit v7 on v6

--- a/solution.py
+++ b/solution.py
@@ -199,7 +199,7 @@
         sums_ref[8:] = norm_ref[...]
 
     outs = [(dims, cols), (SUMS, LANES)]
-    scratch = tile_scratch(dims, rows, cols)
+    scratch = tile_scratch(dims, rows, cols, rows, cols // 2)
     return call(body, "tile_open", outs, scratch, tile_cost(rows, cols), delta, rows_in, kept, passed, norm)
 
 

time: 51.2 us -> 51.2 us (level)
  waiting for transfers between devices: 14.3 us -> 13.6 us
  transfers between devices with their start and end apart: 17 -> 17, of which waited for: 10 -> 10; matrix products, arithmetic and copies ran while one was open for 0% -> 0% of each run, Pallas kernels for 10% -> 11%
where the time goes in v7:
time: 51.2 us; the launch traced here: 50.5 us
  starting transfers between devices  23.8 us (46%)
  waiting for transfers between devices  13.6 us (27%)
  Pallas kernels  9.47 us (18%)
  local copies, waits for them, and re-layouts  1.93 us (4%)
  other arithmetic  0.87 us (2%)
  between operations  0.75 us (1%)
    ppermute x9, starting transfers between devices, send(): return lax.ppermute(value, AXES, self.pairs(source))  13.5 us
    pallas_call x5, Pallas kernels, call(): pl.pallas_call(body, out_shape=[jax.ShapeDtypeStruct(shape, f32) for shap...  8.91 us
    ppermute x3, starting transfers between devices, across(): lax.ppermute(value, axis, [(i, i ^ bit) for i in range(lax.axis_size(axis...  8.62 us
    ppermute x3, waiting for transfers between devices, across(): lax.ppermute(value, axis, [(i, i ^ bit) for i in range(lax.axis_size(axis...  5.68 us
    ppermute x9, waiting for transfers between devices, send(): return lax.ppermute(value, AXES, self.pairs(source))  4.29 us
    ppermute x5, waiting for transfers between devices, other_core(): return lax.ppermute(value, 'aux', [(0, 1), (1, 0)])  3.67 us
    unnamed x4, local copies, waits for them, and re-layouts  1.93 us
    ppermute x5, starting transfers between devices, other_core(): return lax.ppermute(value, 'aux', [(0, 1), (1, 0)])  1.72 us
  transfers between devices with their start and end apart: 17, of which 10 were waited for; matrix products, arithmetic and copies ran while one was open for 0% of the time, Pallas kernels for 11%

profile of v7, /device:TPU:0, one launch (start us, length us, event | category | flops | bytes accessed | tf_op | source)
XLA Modules:
  0.0 50.5 jit_solution(9619566949902061021)
XLA Ops:
  0.6 3.0 %collective-permute-start = (f32[64,1280]{1,0:T(8,128)}, f32[64,1280]{1,0:T(8,128)S(1)}, u32[]{:S(2)}, u32[]{:S(2)}) collective-permute-start(f32[64,1280]{1,0:T(8,128)} %bitcast.3), channel_id=1, source_target_pairs={{2,0},{4,1},{0,2},{6,3},{1,4},{7,5},{3,6},{5,7},{10,8},{12,9},{8,1... | collective-permute-start | bytes 983048 | tf_op jit(solution)/shard_map/ppermute | solution.py:281
  3.6 1.9 %copy-done = bf16[1280,1280]{1,0:T(8,128)(2,1)S(1)} copy-done((bf16[1280,1280]{1,0:T(8,128)(2,1)S(1)}, bf16[1280,1280]{1,0:T(8,128)(2,1)}, u32[]{:S(2)}) %copy-start) | copy-done | bytes 3276824
  5.6 0.8 %norm.1.norm_ref = f32[8,128]{1,0:T(8,128)S(1)} custom-call(bf16[1280,1280]{1,0:T(8,128)(2,1)S(1)} %copy-done), custom_call_target="tpu_custom_call" | custom-call | flops 6553600 | bytes 3276800 | tf_op jit(solution)/shard_map/norm/pallas_call | solution.py:127
  6.3 2.6 %collective-permute-done.got_ref = f32[64,1280]{1,0:T(8,128)S(1)} collective-permute-done((f32[64,1280]{1,0:T(8,128)}, f32[64,1280]{1,0:T(8,128)S(1)}, u32[]{:S(2)}, u32[]{:S(2)}) %collective-permute-start) | collective-permute-done | bytes 327712 | tf_op jit(solution)/shard_map/ppermute | solution.py:281
  9.0 1.5 %collective-permute-done.1.passed_ref = f32[64,1280]{1,0:T(8,128)S(1)} collective-permute-done((f32[64,1280]{1,0:T(8,128)S(1)}, f32[64,1280]{1,0:T(8,128)S(1)}, u32[]{:S(2)}, u32[]{:S(2)}) %collective-permute-start.1) | collective-permute-done | bytes 327712 | tf_op jit(solution)/shard_map/ppermute | solution.py:284
  10.5 2.5 %tile_first.1 = (f32[64,640]{1,0:T(8,128)S(1)}, f32[64,640]{1,0:T(8,128)S(1)}) custom-call(bf16[1280,1280]{1,0:T(8,128)(2,1)S(1)} %copy-done, f32[64,1280]{1,0:T(8,128)S(1)} %bitcast.4, f32[64,1280]{1,0:T(8,128)S(1)} %collective-permute-done.got_ref, f32[64,1280]{1,0:T(8,128)S(1)} %collective-permute-done.1.passed_ref), custom_call_target="tpu_custom_call" | custom-call | flops 2516582400 | bytes 3276800 | tf_op jit(solution)/shard_map/tile_first/pallas_call | solution.py:127
  13.3 1.3 %collective-permute-done.2 = f32[64,640]{1,0:T(8,128)S(1)} collective-permute-done((f32[64,640]{1,0:T(8,128)S(1)}, f32[64,640]{1,0:T(8,128)S(1)}, u32[]{:S(2)}, u32[]{:S(2)}) %collective-permute-start.2) | collective-permute-done | bytes 163872 | tf_op jit(solution)/shard_map/ppermute | solution.py:284
  14.6 2.1 %collective-permute-start.3 = (f32[64,640]{1,0:T(8,128)S(1)}, f32[64,640]{1,0:T(8,128)S(1)}, u32[]{:S(2)}, u32[]{:S(2)}) collective-permute-start(f32[64,640]{1,0:T(8,128)S(1)} %add.31), channel_id=1, source_target_pairs={{0,2},{2,0},{1,3},{3,1},{4,6},{6,4},{5,7},{7,5},{8,10},{10,8},{9,1... | collective-permute-start | bytes 491528 | tf_op jit(solution)/shard_map/ppermute | solution.py:287
  16.6 2.6 %collective-permute-start.5 = (f32[64,640]{1,0:T(8,128)S(1)}, f32[64,640]{1,0:T(8,128)S(1)}, u32[]{:S(2)}, u32[]{:S(2)}) collective-permute-start(f32[64,640]{1,0:T(8,128)S(1)} %add.31), channel_id=1, source_target_pairs={{1,0},{6,1},{10,2},{13,3},{3,4},{4,5},{8,6},{15,7},{0,8},{7,9},{11... | collective-permute-start | bytes 491528 | tf_op jit(solution)/shard_map/ppermute | solution.py:281
  19.2 0.9 %collective-permute-start.6 = (f32[64,640]{1,0:T(8,128)S(1)}, f32[64,640]{1,0:T(8,128)S(1)}, u32[]{:S(2)}, u32[]{:S(2)}) collective-permute-start(f32[64,640]{1,0:T(8,128)S(1)} %add.31), channel_id=1, source_target_pairs={{3,0},{4,1},{8,2},{15,3},{1,4},{6,5},{10,6},{13,7},{2,8},{5,9},{9,... | collective-permute-start | bytes 491528 | tf_op jit(solution)/shard_map/ppermute | solution.py:281
  20.1 3.1 %collective-permute-done.3 = f32[64,640]{1,0:T(8,128)S(1)} collective-permute-done((f32[64,640]{1,0:T(8,128)S(1)}, f32[64,640]{1,0:T(8,128)S(1)}, u32[]{:S(2)}, u32[]{:S(2)}) %collective-permute-start.3) | collective-permute-done | bytes 163872 | tf_op jit(solution)/shard_map/ppermute | solution.py:287
  23.3 1.0 %collective-permute-start.4 = (f32[64,640]{1,0:T(8,128)S(1)}, f32[64,640]{1,0:T(8,128)S(1)}, u32[]{:S(2)}, u32[]{:S(2)}) collective-permute-start(f32[64,640]{1,0:T(8,128)S(1)} %add.32.kept_ref.columns_ref), channel_id=1, source_target_pairs={{2,0},{5,1},{11,2},{12,3},{0,4},{7,5},{9,6},{14,7},{1,8},{6,9},{8,... | collective-permute-start | bytes 491528 | tf_op jit(solution)/shard_map/ppermute | solution.py:281
  24.7 2.6 %tile_open.1 = (f32[64,1280]{1,0:T(8,128)S(1)}, f32[16,128]{1,0:T(8,128)S(1)}) custom-call(bf16[1280,1280]{1,0:T(8,128)(2,1)S(1)} %copy-done, f32[64,640]{1,0:T(8,128)S(1)} %add.33.rows_ref, f32[64,640]{1,0:T(8,128)S(1)} %add.32.kept_ref.columns_ref, f32[64,640]{1,0:T(8,128)S(1)} %collective-permute-done.7.passed_ref.columns_ref, f32[8,128]{1,0:T(8,128)S(1)} %norm.1.norm_ref), custom_call_target="tpu_custom_call" | custom-call | flops 1258291200 | bytes 1638400 | tf_op jit(solution)/shard_map/tile_open/pallas_call | solution.py:127
  27.3 1.4 %collective-permute-done.4.rows_ref = f32[64,640]{1,0:T(8,128)S(1)} collective-permute-done((f32[64,640]{1,0:T(8,128)S(1)}, f32[64,640]{1,0:T(8,128)S(1)}, u32[]{:S(2)}, u32[]{:S(2)}) %collective-permute-start.4) | collective-permute-done | bytes 163872 | tf_op jit(solution)/shard_map/ppermute | solution.py:281
  28.7 1.5 %tile_close.2 = (f32[64,640]{1,0:T(8,128)S(1)}, f32[16,128]{1,0:T(8,128)S(1)}) custom-call(bf16[1280,1280]{1,0:T(8,128)(2,1)S(1)} %copy-done, f32[64,640]{1,0:T(8,128)S(1)} %collective-permute-done.4.rows_ref, f32[64,640]{1,0:T(8,128)S(1)} %collective-permute-done.7.passed_ref.columns_ref, f32[64,1280]{1,0:T(8,128)S(1)} %get-tuple-element.19.part_ref, ...), custom_call_target="tpu_custom_call" | custom-call | flops 629145600 | bytes 819200 | tf_op jit(solution)/shard_map/tile_close/pallas_call | solution.py:127
  30.9 1.5 %tile_close.3 = (f32[64,640]{1,0:T(8,128)S(1)}, f32[16,128]{1,0:T(8,128)S(1)}) custom-call(bf16[1280,1280]{1,0:T(8,128)(2,1)S(1)} %copy-done, f32[64,640]{1,0:T(8,128)S(1)} %collective-permute-done.4.rows_ref, f32[64,640]{1,0:T(8,128)S(1)} %add.32.kept_ref.columns_ref, f32[64,1280]{1,0:T(8,128)S(1)} %get-tuple-element.19.part_ref, ...), custom_call_target="tpu_custom_call" | custom-call | flops 629145600 | bytes 819200 | tf_op jit(solution)/shard_map/tile_close/pallas_call | solution.py:127
  32.4 3.7 %collective-permute-start.9 = (f32[64,640]{1,0:T(8,128)S(1)}, f32[64,640]{1,0:T(8,128)S(1)}, u32[]{:S(2)}, u32[]{:S(2)}) collective-permute-start(f32[64,640]{1,0:T(8,128)S(1)} %add.34), channel_id=1, source_target_pairs={{0,2},{2,0},{1,3},{3,1},{4,6},{6,4},{5,7},{7,5},{8,10},{10,8},{9,1... | collective-permute-start | bytes 491528 | tf_op jit(solution)/shard_map/ppermute | solution.py:287
  36.8 1.8 %collective-permute-start.13 = (f32[16,128]{1,0:T(8,128)S(1)}, f32[16,128]{1,0:T(8,128)S(1)}, u32[]{:S(2)}, u32[]{:S(2)}) collective-permute-start(f32[16,128]{1,0:T(8,128)S(1)} %get-tuple-element.24), channel_id=1, source_target_pairs={{10,0},{11,1},{8,2},{9,3},{14,4},{15,5},{12,6},{13,7},{2,8},{3,9},... | collective-permute-start | bytes 24584 | tf_op jit(solution)/shard_map/ppermute | solution.py:281
  38.6 1.9 %collective-permute-start.14 = (f32[16,128]{1,0:T(8,128)S(1)}, f32[16,128]{1,0:T(8,128)S(1)}, u32[]{:S(2)}, u32[]{:S(2)}) collective-permute-start(f32[16,128]{1,0:T(8,128)S(1)} %get-tuple-element.24), channel_id=1, source_target_pairs={{2,0},{3,1},{0,2},{1,3},{6,4},{7,5},{4,6},{5,7},{10,8},{11,9},{8,1... | collective-permute-start | bytes 24584 | tf_op jit(solution)/shard_map/ppermute | solution.py:281
  41.0 1.6 %collective-permute-start.10 = (f32[64,640]{1,0:T(8,128)S(1)}, f32[64,640]{1,0:T(8,128)S(1)}, u32[]{:S(2)}, u32[]{:S(2)}) collective-permute-start(f32[64,640]{1,0:T(8,128)S(1)} %add.35), channel_id=1, source_target_pairs={{1,0},{6,1},{10,2},{13,3},{3,4},{4,5},{8,6},{15,7},{0,8},{7,9},{11... | collective-permute-start | bytes 491528 | tf_op jit(solution)/shard_map/ppermute | solution.py:281
  43.3 0.8 %collective-permute-done.15 = f32[16,128]{1,0:T(8,128)S(1)} collective-permute-done((f32[16,128]{1,0:T(8,128)S(1)}, f32[16,128]{1,0:T(8,128)S(1)}, u32[]{:S(2)}, u32[]{:S(2)}) %collective-permute-start.15) | collective-permute-done | bytes 8224 | tf_op jit(solution)/shard_map/ppermute | solution.py:284
  44.2 2.8 %collective-permute-start.16 = (f32[16,128]{1,0:T(8,128)S(1)}, f32[16,128]{1,0:T(8,128)S(1)}, u32[]{:S(2)}, u32[]{:S(2)}) collective-permute-start(f32[16,128]{1,0:T(8,128)S(1)} %add.39.mine_ref), channel_id=1, source_target_pairs={{0,4},{4,0},{8,12},{12,8},{1,5},{5,1},{9,13},{13,9},{2,6},{6,2},{1... | collective-permute-start | bytes 24584 | tf_op jit(solution)/shard_map/ppermute | solution.py:287
  47.0 2.1 %collective-permute-done.16.other_ref = f32[16,128]{1,0:T(8,128)S(1)} collective-permute-done((f32[16,128]{1,0:T(8,128)S(1)}, f32[16,128]{1,0:T(8,128)S(1)}, u32[]{:S(2)}, u32[]{:S(2)}) %collective-permute-start.16) | collective-permute-done | bytes 8224 | tf_op jit(solution)/shard_map/ppermute | solution.py:287
  49.7 0.7 %fusion = f32[1280,64]{0,1:T(8,128)} fusion(f32[64,640]{1,0:T(8,128)S(1)} %collective-permute-done.11, f32[64,640]{1,0:T(8,128)S(1)} %collective-permute-done.10, pred[]{:T(512)S(6)} %eq.3), kind=kLoop, calls=%fused_computation.1 | loop fusion | flops 245760 | bytes 655361 | tf_op jit(solution)/shard_map/transpose | solution.py:375
  (28 shorter events, 3.9 us)
Async XLA Ops:
  0.6 8.3 %collective-permute-start = (f32[64,1280]{1,0:T(8,128)}, f32[64,1280]{1,0:T(8,128)S(1)}, u32[]{:S(2)}, u32[]{:S(2)}) collective-permute-start(f32[64,1280]{1,0:T(8,128)} %bitcast.3), channel_id=1, source_target_pairs={{2,0},{4,1},{0,2},{6,3},{1,4},{7,5},{3,6},{5,7},{10,8},{12,9},{8,1... | collective-permute-start | bytes 983048 | tf_op jit(solution)/shard_map/ppermute | solution.py:281
  3.6 1.9 %copy-start = (bf16[1280,1280]{1,0:T(8,128)(2,1)S(1)}, bf16[1280,1280]{1,0:T(8,128)(2,1)}, u32[]{:S(2)}) copy-start(bf16[1280,1280]{1,0:T(8,128)(2,1)} %delta_ref.9) | copy-start | bytes 9830404
  5.6 5.0 %copy-start.1 = (f32[1280,64]{0,1:T(8,128)S(1)}, f32[1280,64]{0,1:T(8,128)}, u32[]{:S(2)}) copy-start(f32[1280,64]{0,1:T(8,128)} %param.3) | copy-start | bytes 983044
  8.9 1.6 %collective-permute-start.1 = (f32[64,1280]{1,0:T(8,128)S(1)}, f32[64,1280]{1,0:T(8,128)S(1)}, u32[]{:S(2)}, u32[]{:S(2)}) collective-permute-start(f32[64,1280]{1,0:T(8,128)S(1)} %collective-permute-done.got_ref), channel_id=1, source_target_pairs={{0,1},{1,0},{2,3},{3,2},{4,5},{5,4},{6,7},{7,6},{8,9},{9,8},{10,11... | collective-permute-start | bytes 983048 | tf_op jit(solution)/shard_map/ppermute | solution.py:284
  13.1 1.5 %collective-permute-start.2 = (f32[64,640]{1,0:T(8,128)S(1)}, f32[64,640]{1,0:T(8,128)S(1)}, u32[]{:S(2)}, u32[]{:S(2)}) collective-permute-start(f32[64,640]{1,0:T(8,128)S(1)} %get-tuple-element.17), channel_id=1, source_target_pairs={{0,1},{1,0},{2,3},{3,2},{4,5},{5,4},{6,7},{7,6},{8,9},{9,8},{10,11... | collective-permute-start | bytes 491528 | tf_op jit(solution)/shard_map/ppermute | solution.py:284
  14.6 8.6 %collective-permute-start.3 = (f32[64,640]{1,0:T(8,128)S(1)}, f32[64,640]{1,0:T(8,128)S(1)}, u32[]{:S(2)}, u32[]{:S(2)}) collective-permute-start(f32[64,640]{1,0:T(8,128)S(1)} %add.31), channel_id=1, source_target_pairs={{0,2},{2,0},{1,3},{3,1},{4,6},{6,4},{5,7},{7,5},{8,10},{10,8},{9,1... | collective-permute-start | bytes 491528 | tf_op jit(solution)/shard_map/ppermute | solution.py:287
  16.6 7.7 %collective-permute-start.5 = (f32[64,640]{1,0:T(8,128)S(1)}, f32[64,640]{1,0:T(8,128)S(1)}, u32[]{:S(2)}, u32[]{:S(2)}) collective-permute-start(f32[64,640]{1,0:T(8,128)S(1)} %add.31), channel_id=1, source_target_pairs={{1,0},{6,1},{10,2},{13,3},{3,4},{4,5},{8,6},{15,7},{0,8},{7,9},{11... | collective-permute-start | bytes 491528 | tf_op jit(solution)/shard_map/ppermute | solution.py:281
  19.2 5.4 %collective-permute-start.6 = (f32[64,640]{1,0:T(8,128)S(1)}, f32[64,640]{1,0:T(8,128)S(1)}, u32[]{:S(2)}, u32[]{:S(2)}) collective-permute-start(f32[64,640]{1,0:T(8,128)S(1)} %add.31), channel_id=1, source_target_pairs={{3,0},{4,1},{8,2},{15,3},{1,4},{6,5},{10,6},{13,7},{2,8},{5,9},{9,... | collective-permute-start | bytes 491528 | tf_op jit(solution)/shard_map/ppermute | solution.py:281
  23.2 1.5 %collective-permute-start.7 = (f32[64,640]{1,0:T(8,128)S(1)}, f32[64,640]{1,0:T(8,128)S(1)}, u32[]{:S(2)}, u32[]{:S(2)}) collective-permute-start(f32[64,640]{1,0:T(8,128)S(1)} %add.32.kept_ref.columns_ref), channel_id=1, source_target_pairs={{0,1},{1,0},{2,3},{3,2},{4,5},{5,4},{6,7},{7,6},{8,9},{9,8},{10,11... | collective-permute-start | bytes 491528 | tf_op jit(solution)/shard_map/ppermute | solution.py:284
  23.3 5.4 %collective-permute-start.4 = (f32[64,640]{1,0:T(8,128)S(1)}, f32[64,640]{1,0:T(8,128)S(1)}, u32[]{:S(2)}, u32[]{:S(2)}) collective-permute-start(f32[64,640]{1,0:T(8,128)S(1)} %add.32.kept_ref.columns_ref), channel_id=1, source_target_pairs={{2,0},{5,1},{11,2},{12,3},{0,4},{7,5},{9,6},{14,7},{1,8},{6,9},{8,... | collective-permute-start | bytes 491528 | tf_op jit(solution)/shard_map/ppermute | solution.py:281
  30.2 2.2 %collective-permute-start.8 = (f32[64,640]{1,0:T(8,128)S(1)}, f32[64,640]{1,0:T(8,128)S(1)}, u32[]{:S(2)}, u32[]{:S(2)}) collective-permute-start(f32[64,640]{1,0:T(8,128)S(1)} %get-tuple-element.23), channel_id=1, source_target_pairs={{0,1},{1,0},{2,3},{3,2},{4,5},{5,4},{6,7},{7,6},{8,9},{9,8},{10,11... | collective-permute-start | bytes 491528 | tf_op jit(solution)/shard_map/ppermute | solution.py:284
  32.4 8.6 %collective-permute-start.9 = (f32[64,640]{1,0:T(8,128)S(1)}, f32[64,640]{1,0:T(8,128)S(1)}, u32[]{:S(2)}, u32[]{:S(2)}) collective-permute-start(f32[64,640]{1,0:T(8,128)S(1)} %add.34), channel_id=1, source_target_pairs={{0,2},{2,0},{1,3},{3,1},{4,6},{6,4},{5,7},{7,5},{8,10},{10,8},{9,1... | collective-permute-start | bytes 491528 | tf_op jit(solution)/shard_map/ppermute | solution.py:287
  36.1 6.5 %collective-permute-start.12 = (f32[16,128]{1,0:T(8,128)S(1)}, f32[16,128]{1,0:T(8,128)S(1)}, u32[]{:S(2)}, u32[]{:S(2)}) collective-permute-start(f32[16,128]{1,0:T(8,128)S(1)} %get-tuple-element.24), channel_id=1, source_target_pairs={{8,0},{9,1},{10,2},{11,3},{12,4},{13,5},{14,6},{15,7},{0,8},{1,9},... | collective-permute-start | bytes 24584 | tf_op jit(solution)/shard_map/ppermute | solution.py:281
  36.8 5.8 %collective-permute-start.13 = (f32[16,128]{1,0:T(8,128)S(1)}, f32[16,128]{1,0:T(8,128)S(1)}, u32[]{:S(2)}, u32[]{:S(2)}) collective-permute-start(f32[16,128]{1,0:T(8,128)S(1)} %get-tuple-element.24), channel_id=1, source_target_pairs={{10,0},{11,1},{8,2},{9,3},{14,4},{15,5},{12,6},{13,7},{2,8},{3,9},... | collective-permute-start | bytes 24584 | tf_op jit(solution)/shard_map/ppermute | solution.py:281
  38.6 4.0 %collective-permute-start.14 = (f32[16,128]{1,0:T(8,128)S(1)}, f32[16,128]{1,0:T(8,128)S(1)}, u32[]{:S(2)}, u32[]{:S(2)}) collective-permute-start(f32[16,128]{1,0:T(8,128)S(1)} %get-tuple-element.24), channel_id=1, source_target_pairs={{2,0},{3,1},{0,2},{1,3},{6,4},{7,5},{4,6},{5,7},{10,8},{11,9},{8,1... | collective-permute-start | bytes 24584 | tf_op jit(solution)/shard_map/ppermute | solution.py:281
  41.0 8.7 %collective-permute-start.10 = (f32[64,640]{1,0:T(8,128)S(1)}, f32[64,640]{1,0:T(8,128)S(1)}, u32[]{:S(2)}, u32[]{:S(2)}) collective-permute-start(f32[64,640]{1,0:T(8,128)S(1)} %add.35), channel_id=1, source_target_pairs={{1,0},{6,1},{10,2},{13,3},{3,4},{4,5},{8,6},{15,7},{0,8},{7,9},{11... | collective-permute-start | bytes 491528 | tf_op jit(solution)/shard_map/ppermute | solution.py:281
  42.6 7.1 %collective-permute-start.11 = (f32[64,640]{1,0:T(8,128)S(1)}, f32[64,640]{1,0:T(8,128)S(1)}, u32[]{:S(2)}, u32[]{:S(2)}) collective-permute-start(f32[64,640]{1,0:T(8,128)S(1)} %add.35), channel_id=1, source_target_pairs={{2,0},{5,1},{11,2},{12,3},{0,4},{7,5},{9,6},{14,7},{1,8},{6,9},{8,... | collective-permute-start | bytes 491528 | tf_op jit(solution)/shard_map/ppermute | solution.py:281
  42.7 1.5 %collective-permute-start.15 = (f32[16,128]{1,0:T(8,128)S(1)}, f32[16,128]{1,0:T(8,128)S(1)}, u32[]{:S(2)}, u32[]{:S(2)}) collective-permute-start(f32[16,128]{1,0:T(8,128)S(1)} %add_add_fusion), channel_id=1, source_target_pairs={{0,1},{1,0},{2,3},{3,2},{4,5},{5,4},{6,7},{7,6},{8,9},{9,8},{10,11... | collective-permute-start | bytes 24584 | tf_op jit(solution)/shard_map/ppermute | solution.py:284
  44.2 5.0 %collective-permute-start.16 = (f32[16,128]{1,0:T(8,128)S(1)}, f32[16,128]{1,0:T(8,128)S(1)}, u32[]{:S(2)}, u32[]{:S(2)}) collective-permute-start(f32[16,128]{1,0:T(8,128)S(1)} %add.39.mine_ref), channel_id=1, source_target_pairs={{0,4},{4,0},{8,12},{12,8},{1,5},{5,1},{9,13},{13,9},{2,6},{6,2},{1... | collective-permute-start | bytes 24584 | tf_op jit(solution)/shard_map/ppermute | solution.py:287

commit v8 on v6

--- a/solution.py
+++ b/solution.py
@@ -353,6 +353,7 @@
     keep, sums = close_tile(late, mine, scale, dissimilarity, second, half, part, sums)
 
     half = keep + grid.other_core(send)
+    sums = sums + grid.other_core(sums)
     if grid.wide == 4:
         across = [grid.send(sums, lambda x, a, z, m=m, n=n: (x ^ m, a, z ^ n)) for m, n in ((0, 2), (1, 2), (1, 0))]
         sums = sums + across[0] + across[1] + across[2]
@@ -365,7 +366,6 @@
         half = half + grid.across(half, "narrow", bit)
     first = grid.send(half, grid.spread(False))
     second = grid.send(half, grid.spread(True))
-    sums = sums + grid.other_core(sums)
     stress = stress_call(sums, grid.across(sums, "wide", 1))
     first, second, stress = lax.optimization_barrier((first, second, stress))
     in_order = grid.spread_half() == 0

time: 51.2 us -> 51.2 us (level)
  starting transfers between devices: 23.9 us -> 21.9 us
  waiting for transfers between devices: 14.3 us -> 15.9 us
    ppermute x9, waiting for transfers between devices: 4.69 us -> 5.82 us  [send(): return lax.ppermute(value, AXES, self.pairs(source))]
    ppermute x3, starting transfers between devices: 9.11 us -> 8.02 us  [across(): lax.ppermute(value, axis, [(i, i ^ bit) for i in range(lax.axis_size(axis...]
    ppermute x9, starting transfers between devices: 13.3 us -> 12.6 us  [send(): return lax.ppermute(value, AXES, self.pairs(source))]
  transfers between devices with their start and end apart: 17 -> 17, of which waited for: 10 -> 11; matrix products, arithmetic and copies ran while one was open for 0% -> 0% of each run, Pallas kernels for 10% -> 10%
where the time goes in v8:
time: 51.2 us; the launch traced here: 50.4 us
  starting transfers between devices  21.9 us (43%)
  waiting for transfers between devices  15.9 us (31%)
  Pallas kernels  9.07 us (18%)
  local copies, waits for them, and re-layouts  1.93 us (4%)
  other arithmetic  0.87 us (2%)
  between operations  0.74 us (1%)
    ppermute x9, starting transfers between devices, send(): return lax.ppermute(value, AXES, self.pairs(source))  12.6 us
    pallas_call x5, Pallas kernels, call(): pl.pallas_call(body, out_shape=[jax.ShapeDtypeStruct(shape, f32) for shap...  8.51 us
    ppermute x3, starting transfers between devices, across(): lax.ppermute(value, axis, [(i, i ^ bit) for i in range(lax.axis_size(axis...  8.02 us
    ppermute x3, waiting for transfers between devices, across(): lax.ppermute(value, axis, [(i, i ^ bit) for i in range(lax.axis_size(axis...  6.27 us
    ppermute x9, waiting for transfers between devices, send(): return lax.ppermute(value, AXES, self.pairs(source))  5.82 us
    ppermute x5, waiting for transfers between devices, other_core(): return lax.ppermute(value, 'aux', [(0, 1), (1, 0)])  3.78 us
    unnamed x4, local copies, waits for them, and re-layouts  1.93 us
    ppermute x5, starting transfers between devices, other_core(): return lax.ppermute(value, 'aux', [(0, 1), (1, 0)])  1.27 us
  transfers between devices with their start and end apart: 17, of which 11 were waited for; matrix products, arithmetic and copies ran while one was open for 0% of the time, Pallas kernels for 10%

profile of v8, /device:TPU:0, one launch (start us, length us, event | category | flops | bytes accessed | tf_op | source)
XLA Modules:
  0.0 50.4 jit_solution(10972236055808522516)
XLA Ops:
  0.6 3.0 %collective-permute-start = (f32[64,1280]{1,0:T(8,128)}, f32[64,1280]{1,0:T(8,128)S(1)}, u32[]{:S(2)}, u32[]{:S(2)}) collective-permute-start(f32[64,1280]{1,0:T(8,128)} %bitcast.3), channel_id=1, source_target_pairs={{2,0},{4,1},{0,2},{6,3},{1,4},{7,5},{3,6},{5,7},{10,8},{12,9},{8,1... | collective-permute-start | bytes 983048 | tf_op jit(solution)/shard_map/ppermute | solution.py:281
  3.6 1.9 %copy-done = bf16[1280,1280]{1,0:T(8,128)(2,1)S(1)} copy-done((bf16[1280,1280]{1,0:T(8,128)(2,1)S(1)}, bf16[1280,1280]{1,0:T(8,128)(2,1)}, u32[]{:S(2)}) %copy-start) | copy-done | bytes 3276824
  5.6 0.8 %norm.1.norm_ref = f32[8,128]{1,0:T(8,128)S(1)} custom-call(bf16[1280,1280]{1,0:T(8,128)(2,1)S(1)} %copy-done), custom_call_target="tpu_custom_call" | custom-call | flops 6553600 | bytes 3276800 | tf_op jit(solution)/shard_map/norm/pallas_call | solution.py:127
  6.3 2.6 %collective-permute-done.got_ref = f32[64,1280]{1,0:T(8,128)S(1)} collective-permute-done((f32[64,1280]{1,0:T(8,128)}, f32[64,1280]{1,0:T(8,128)S(1)}, u32[]{:S(2)}, u32[]{:S(2)}) %collective-permute-start) | collective-permute-done | bytes 327712 | tf_op jit(solution)/shard_map/ppermute | solution.py:281
  9.0 1.5 %collective-permute-done.1.passed_ref = f32[64,1280]{1,0:T(8,128)S(1)} collective-permute-done((f32[64,1280]{1,0:T(8,128)S(1)}, f32[64,1280]{1,0:T(8,128)S(1)}, u32[]{:S(2)}, u32[]{:S(2)}) %collective-permute-start.1) | collective-permute-done | bytes 327712 | tf_op jit(solution)/shard_map/ppermute | solution.py:284
  10.5 2.5 %tile_first.1 = (f32[64,640]{1,0:T(8,128)S(1)}, f32[64,640]{1,0:T(8,128)S(1)}) custom-call(bf16[1280,1280]{1,0:T(8,128)(2,1)S(1)} %copy-done, f32[64,1280]{1,0:T(8,128)S(1)} %bitcast.4, f32[64,1280]{1,0:T(8,128)S(1)} %collective-permute-done.got_ref, f32[64,1280]{1,0:T(8,128)S(1)} %collective-permute-done.1.passed_ref), custom_call_target="tpu_custom_call" | custom-call | flops 2516582400 | bytes 3276800 | tf_op jit(solution)/shard_map/tile_first/pallas_call | solution.py:127
  13.3 1.3 %collective-permute-done.2 = f32[64,640]{1,0:T(8,128)S(1)} collective-permute-done((f32[64,640]{1,0:T(8,128)S(1)}, f32[64,640]{1,0:T(8,128)S(1)}, u32[]{:S(2)}, u32[]{:S(2)}) %collective-permute-start.2) | collective-permute-done | bytes 163872 | tf_op jit(solution)/shard_map/ppermute | solution.py:284
  14.6 2.1 %collective-permute-start.3 = (f32[64,640]{1,0:T(8,128)S(1)}, f32[64,640]{1,0:T(8,128)S(1)}, u32[]{:S(2)}, u32[]{:S(2)}) collective-permute-start(f32[64,640]{1,0:T(8,128)S(1)} %add.31), channel_id=1, source_target_pairs={{0,2},{2,0},{1,3},{3,1},{4,6},{6,4},{5,7},{7,5},{8,10},{10,8},{9,1... | collective-permute-start | bytes 491528 | tf_op jit(solution)/shard_map/ppermute | solution.py:287
  16.6 2.6 %collective-permute-start.5 = (f32[64,640]{1,0:T(8,128)S(1)}, f32[64,640]{1,0:T(8,128)S(1)}, u32[]{:S(2)}, u32[]{:S(2)}) collective-permute-start(f32[64,640]{1,0:T(8,128)S(1)} %add.31), channel_id=1, source_target_pairs={{1,0},{6,1},{10,2},{13,3},{3,4},{4,5},{8,6},{15,7},{0,8},{7,9},{11... | collective-permute-start | bytes 491528 | tf_op jit(solution)/shard_map/ppermute | solution.py:281
  19.2 0.9 %collective-permute-start.6 = (f32[64,640]{1,0:T(8,128)S(1)}, f32[64,640]{1,0:T(8,128)S(1)}, u32[]{:S(2)}, u32[]{:S(2)}) collective-permute-start(f32[64,640]{1,0:T(8,128)S(1)} %add.31), channel_id=1, source_target_pairs={{3,0},{4,1},{8,2},{15,3},{1,4},{6,5},{10,6},{13,7},{2,8},{5,9},{9,... | collective-permute-start | bytes 491528 | tf_op jit(solution)/shard_map/ppermute | solution.py:281
  20.1 3.1 %collective-permute-done.3 = f32[64,640]{1,0:T(8,128)S(1)} collective-permute-done((f32[64,640]{1,0:T(8,128)S(1)}, f32[64,640]{1,0:T(8,128)S(1)}, u32[]{:S(2)}, u32[]{:S(2)}) %collective-permute-start.3) | collective-permute-done | bytes 163872 | tf_op jit(solution)/shard_map/ppermute | solution.py:287
  23.3 1.0 %collective-permute-start.4 = (f32[64,640]{1,0:T(8,128)S(1)}, f32[64,640]{1,0:T(8,128)S(1)}, u32[]{:S(2)}, u32[]{:S(2)}) collective-permute-start(f32[64,640]{1,0:T(8,128)S(1)} %add.32.kept_ref.columns_ref), channel_id=1, source_target_pairs={{2,0},{5,1},{11,2},{12,3},{0,4},{7,5},{9,6},{14,7},{1,8},{6,9},{8,... | collective-permute-start | bytes 491528 | tf_op jit(solution)/shard_map/ppermute | solution.py:281
  24.7 2.2 %tile_open.1 = (f32[64,1280]{1,0:T(8,128)S(1)}, f32[16,128]{1,0:T(8,128)S(1)}) custom-call(bf16[1280,1280]{1,0:T(8,128)(2,1)S(1)} %copy-done, f32[64,640]{1,0:T(8,128)S(1)} %add.33.rows_ref, f32[64,640]{1,0:T(8,128)S(1)} %add.32.kept_ref.columns_ref, f32[64,640]{1,0:T(8,128)S(1)} %collective-permute-done.7.passed_ref.columns_ref, f32[8,128]{1,0:T(8,128)S(1)} %norm.1.norm_ref), custom_call_target="tpu_custom_call" | custom-call | flops 1258291200 | bytes 1638400 | tf_op jit(solution)/shard_map/tile_open/pallas_call | solution.py:127
  26.9 1.8 %collective-permute-done.4.rows_ref = f32[64,640]{1,0:T(8,128)S(1)} collective-permute-done((f32[64,640]{1,0:T(8,128)S(1)}, f32[64,640]{1,0:T(8,128)S(1)}, u32[]{:S(2)}, u32[]{:S(2)}) %collective-permute-start.4) | collective-permute-done | bytes 163872 | tf_op jit(solution)/shard_map/ppermute | solution.py:281
  28.7 1.5 %tile_close.2 = (f32[64,640]{1,0:T(8,128)S(1)}, f32[16,128]{1,0:T(8,128)S(1)}) custom-call(bf16[1280,1280]{1,0:T(8,128)(2,1)S(1)} %copy-done, f32[64,640]{1,0:T(8,128)S(1)} %collective-permute-done.4.rows_ref, f32[64,640]{1,0:T(8,128)S(1)} %collective-permute-done.7.passed_ref.columns_ref, f32[64,1280]{1,0:T(8,128)S(1)} %get-tuple-element.19.part_ref, ...), custom_call_target="tpu_custom_call" | custom-call | flops 629145600 | bytes 819200 | tf_op jit(solution)/shard_map/tile_close/pallas_call | solution.py:127
  30.9 1.5 %tile_close.3 = (f32[64,640]{1,0:T(8,128)S(1)}, f32[16,128]{1,0:T(8,128)S(1)}) custom-call(bf16[1280,1280]{1,0:T(8,128)(2,1)S(1)} %copy-done, f32[64,640]{1,0:T(8,128)S(1)} %collective-permute-done.4.rows_ref, f32[64,640]{1,0:T(8,128)S(1)} %add.32.kept_ref.columns_ref, f32[64,1280]{1,0:T(8,128)S(1)} %get-tuple-element.19.part_ref, ...), custom_call_target="tpu_custom_call" | custom-call | flops 629145600 | bytes 819200 | tf_op jit(solution)/shard_map/tile_close/pallas_call | solution.py:127
  32.4 3.7 %collective-permute-start.9 = (f32[64,640]{1,0:T(8,128)S(1)}, f32[64,640]{1,0:T(8,128)S(1)}, u32[]{:S(2)}, u32[]{:S(2)}) collective-permute-start(f32[64,640]{1,0:T(8,128)S(1)} %add.34), channel_id=1, source_target_pairs={{0,2},{2,0},{1,3},{3,1},{4,6},{6,4},{5,7},{7,5},{8,10},{10,8},{9,1... | collective-permute-start | bytes 491528 | tf_op jit(solution)/shard_map/ppermute | solution.py:287
  36.4 0.9 %collective-permute-done.12 = f32[16,128]{1,0:T(8,128)S(1)} collective-permute-done((f32[16,128]{1,0:T(8,128)S(1)}, f32[16,128]{1,0:T(8,128)S(1)}, u32[]{:S(2)}, u32[]{:S(2)}) %collective-permute-start.12) | collective-permute-done | bytes 8224 | tf_op jit(solution)/shard_map/ppermute | solution.py:284
  38.0 2.0 %collective-permute-start.14 = (f32[16,128]{1,0:T(8,128)S(1)}, f32[16,128]{1,0:T(8,128)S(1)}, u32[]{:S(2)}, u32[]{:S(2)}) collective-permute-start(f32[16,128]{1,0:T(8,128)S(1)} %add.36), channel_id=1, source_target_pairs={{10,0},{11,1},{8,2},{9,3},{14,4},{15,5},{12,6},{13,7},{2,8},{3,9},... | collective-permute-start | bytes 24584 | tf_op jit(solution)/shard_map/ppermute | solution.py:281
  39.9 1.8 %collective-permute-start.15 = (f32[16,128]{1,0:T(8,128)S(1)}, f32[16,128]{1,0:T(8,128)S(1)}, u32[]{:S(2)}, u32[]{:S(2)}) collective-permute-start(f32[16,128]{1,0:T(8,128)S(1)} %add.36), channel_id=1, source_target_pairs={{2,0},{3,1},{0,2},{1,3},{6,4},{7,5},{4,6},{5,7},{10,8},{11,9},{8,1... | collective-permute-start | bytes 24584 | tf_op jit(solution)/shard_map/ppermute | solution.py:281
  42.5 1.0 %collective-permute-done.14 = f32[16,128]{1,0:T(8,128)S(1)} collective-permute-done((f32[16,128]{1,0:T(8,128)S(1)}, f32[16,128]{1,0:T(8,128)S(1)}, u32[]{:S(2)}, u32[]{:S(2)}) %collective-permute-start.14) | collective-permute-done | bytes 8224 | tf_op jit(solution)/shard_map/ppermute | solution.py:281
  43.6 2.2 %collective-permute-start.16 = (f32[16,128]{1,0:T(8,128)S(1)}, f32[16,128]{1,0:T(8,128)S(1)}, u32[]{:S(2)}, u32[]{:S(2)}) collective-permute-start(f32[16,128]{1,0:T(8,128)S(1)} %add_add_fusion.mine_ref), channel_id=1, source_target_pairs={{0,4},{4,0},{8,12},{12,8},{1,5},{5,1},{9,13},{13,9},{2,6},{6,2},{1... | collective-permute-start | bytes 24584 | tf_op jit(solution)/shard_map/ppermute | solution.py:287
  45.8 3.2 %collective-permute-done.16.other_ref = f32[16,128]{1,0:T(8,128)S(1)} collective-permute-done((f32[16,128]{1,0:T(8,128)S(1)}, f32[16,128]{1,0:T(8,128)S(1)}, u32[]{:S(2)}, u32[]{:S(2)}) %collective-permute-start.16) | collective-permute-done | bytes 8224 | tf_op jit(solution)/shard_map/ppermute | solution.py:287
  49.6 0.7 %fusion = f32[1280,64]{0,1:T(8,128)} fusion(f32[64,640]{1,0:T(8,128)S(1)} %collective-permute-done.11, f32[64,640]{1,0:T(8,128)S(1)} %collective-permute-done.10, pred[]{:T(512)S(6)} %eq.3), kind=kLoop, calls=%fused_computation.1 | loop fusion | flops 245760 | bytes 655361 | tf_op jit(solution)/shard_map/transpose | solution.py:375
  (28 shorter events, 3.8 us)
Async XLA Ops:
  0.6 8.3 %collective-permute-start = (f32[64,1280]{1,0:T(8,128)}, f32[64,1280]{1,0:T(8,128)S(1)}, u32[]{:S(2)}, u32[]{:S(2)}) collective-permute-start(f32[64,1280]{1,0:T(8,128)} %bitcast.3), channel_id=1, source_target_pairs={{2,0},{4,1},{0,2},{6,3},{1,4},{7,5},{3,6},{5,7},{10,8},{12,9},{8,1... | collective-permute-start | bytes 983048 | tf_op jit(solution)/shard_map/ppermute | solution.py:281
  3.6 1.9 %copy-start = (bf16[1280,1280]{1,0:T(8,128)(2,1)S(1)}, bf16[1280,1280]{1,0:T(8,128)(2,1)}, u32[]{:S(2)}) copy-start(bf16[1280,1280]{1,0:T(8,128)(2,1)} %delta_ref.9) | copy-start | bytes 9830404
  5.6 5.0 %copy-start.1 = (f32[1280,64]{0,1:T(8,128)S(1)}, f32[1280,64]{0,1:T(8,128)}, u32[]{:S(2)}) copy-start(f32[1280,64]{0,1:T(8,128)} %param.3) | copy-start | bytes 983044
  8.9 1.6 %collective-permute-start.1 = (f32[64,1280]{1,0:T(8,128)S(1)}, f32[64,1280]{1,0:T(8,128)S(1)}, u32[]{:S(2)}, u32[]{:S(2)}) collective-permute-start(f32[64,1280]{1,0:T(8,128)S(1)} %collective-permute-done.got_ref), channel_id=1, source_target_pairs={{0,1},{1,0},{2,3},{3,2},{4,5},{5,4},{6,7},{7,6},{8,9},{9,8},{10,11... | collective-permute-start | bytes 983048 | tf_op jit(solution)/shard_map/ppermute | solution.py:284
  13.1 1.5 %collective-permute-start.2 = (f32[64,640]{1,0:T(8,128)S(1)}, f32[64,640]{1,0:T(8,128)S(1)}, u32[]{:S(2)}, u32[]{:S(2)}) collective-permute-start(f32[64,640]{1,0:T(8,128)S(1)} %get-tuple-element.17), channel_id=1, source_target_pairs={{0,1},{1,0},{2,3},{3,2},{4,5},{5,4},{6,7},{7,6},{8,9},{9,8},{10,11... | collective-permute-start | bytes 491528 | tf_op jit(solution)/shard_map/ppermute | solution.py:284
  14.6 8.6 %collective-permute-start.3 = (f32[64,640]{1,0:T(8,128)S(1)}, f32[64,640]{1,0:T(8,128)S(1)}, u32[]{:S(2)}, u32[]{:S(2)}) collective-permute-start(f32[64,640]{1,0:T(8,128)S(1)} %add.31), channel_id=1, source_target_pairs={{0,2},{2,0},{1,3},{3,1},{4,6},{6,4},{5,7},{7,5},{8,10},{10,8},{9,1... | collective-permute-start | bytes 491528 | tf_op jit(solution)/shard_map/ppermute | solution.py:287
  16.6 7.7 %collective-permute-start.5 = (f32[64,640]{1,0:T(8,128)S(1)}, f32[64,640]{1,0:T(8,128)S(1)}, u32[]{:S(2)}, u32[]{:S(2)}) collective-permute-start(f32[64,640]{1,0:T(8,128)S(1)} %add.31), channel_id=1, source_target_pairs={{1,0},{6,1},{10,2},{13,3},{3,4},{4,5},{8,6},{15,7},{0,8},{7,9},{11... | collective-permute-start | bytes 491528 | tf_op jit(solution)/shard_map/ppermute | solution.py:281
  19.2 5.4 %collective-permute-start.6 = (f32[64,640]{1,0:T(8,128)S(1)}, f32[64,640]{1,0:T(8,128)S(1)}, u32[]{:S(2)}, u32[]{:S(2)}) collective-permute-start(f32[64,640]{1,0:T(8,128)S(1)} %add.31), channel_id=1, source_target_pairs={{3,0},{4,1},{8,2},{15,3},{1,4},{6,5},{10,6},{13,7},{2,8},{5,9},{9,... | collective-permute-start | bytes 491528 | tf_op jit(solution)/shard_map/ppermute | solution.py:281
  23.2 1.5 %collective-permute-start.7 = (f32[64,640]{1,0:T(8,128)S(1)}, f32[64,640]{1,0:T(8,128)S(1)}, u32[]{:S(2)}, u32[]{:S(2)}) collective-permute-start(f32[64,640]{1,0:T(8,128)S(1)} %add.32.kept_ref.columns_ref), channel_id=1, source_target_pairs={{0,1},{1,0},{2,3},{3,2},{4,5},{5,4},{6,7},{7,6},{8,9},{9,8},{10,11... | collective-permute-start | bytes 491528 | tf_op jit(solution)/shard_map/ppermute | solution.py:284
  23.3 5.4 %collective-permute-start.4 = (f32[64,640]{1,0:T(8,128)S(1)}, f32[64,640]{1,0:T(8,128)S(1)}, u32[]{:S(2)}, u32[]{:S(2)}) collective-permute-start(f32[64,640]{1,0:T(8,128)S(1)} %add.32.kept_ref.columns_ref), channel_id=1, source_target_pairs={{2,0},{5,1},{11,2},{12,3},{0,4},{7,5},{9,6},{14,7},{1,8},{6,9},{8,... | collective-permute-start | bytes 491528 | tf_op jit(solution)/shard_map/ppermute | solution.py:281
  30.2 2.2 %collective-permute-start.8 = (f32[64,640]{1,0:T(8,128)S(1)}, f32[64,640]{1,0:T(8,128)S(1)}, u32[]{:S(2)}, u32[]{:S(2)}) collective-permute-start(f32[64,640]{1,0:T(8,128)S(1)} %get-tuple-element.23), channel_id=1, source_target_pairs={{0,1},{1,0},{2,3},{3,2},{4,5},{5,4},{6,7},{7,6},{8,9},{9,8},{10,11... | collective-permute-start | bytes 491528 | tf_op jit(solution)/shard_map/ppermute | solution.py:284
  32.4 9.3 %collective-permute-start.9 = (f32[64,640]{1,0:T(8,128)S(1)}, f32[64,640]{1,0:T(8,128)S(1)}, u32[]{:S(2)}, u32[]{:S(2)}) collective-permute-start(f32[64,640]{1,0:T(8,128)S(1)} %add.34), channel_id=1, source_target_pairs={{0,2},{2,0},{1,3},{3,1},{4,6},{6,4},{5,7},{7,5},{8,10},{10,8},{9,1... | collective-permute-start | bytes 491528 | tf_op jit(solution)/shard_map/ppermute | solution.py:287
  36.1 1.2 %collective-permute-start.12 = (f32[16,128]{1,0:T(8,128)S(1)}, f32[16,128]{1,0:T(8,128)S(1)}, u32[]{:S(2)}, u32[]{:S(2)}) collective-permute-start(f32[16,128]{1,0:T(8,128)S(1)} %get-tuple-element.24), channel_id=1, source_target_pairs={{0,1},{1,0},{2,3},{3,2},{4,5},{5,4},{6,7},{7,6},{8,9},{9,8},{10,11... | collective-permute-start | bytes 24584 | tf_op jit(solution)/shard_map/ppermute | solution.py:284
  37.3 5.1 %collective-permute-start.13 = (f32[16,128]{1,0:T(8,128)S(1)}, f32[16,128]{1,0:T(8,128)S(1)}, u32[]{:S(2)}, u32[]{:S(2)}) collective-permute-start(f32[16,128]{1,0:T(8,128)S(1)} %add.36), channel_id=1, source_target_pairs={{8,0},{9,1},{10,2},{11,3},{12,4},{13,5},{14,6},{15,7},{0,8},{1,9},... | collective-permute-start | bytes 24584 | tf_op jit(solution)/shard_map/ppermute | solution.py:281
  38.0 5.4 %collective-permute-start.14 = (f32[16,128]{1,0:T(8,128)S(1)}, f32[16,128]{1,0:T(8,128)S(1)}, u32[]{:S(2)}, u32[]{:S(2)}) collective-permute-start(f32[16,128]{1,0:T(8,128)S(1)} %add.36), channel_id=1, source_target_pairs={{10,0},{11,1},{8,2},{9,3},{14,4},{15,5},{12,6},{13,7},{2,8},{3,9},... | collective-permute-start | bytes 24584 | tf_op jit(solution)/shard_map/ppermute | solution.py:281
  39.9 3.7 %collective-permute-start.15 = (f32[16,128]{1,0:T(8,128)S(1)}, f32[16,128]{1,0:T(8,128)S(1)}, u32[]{:S(2)}, u32[]{:S(2)}) collective-permute-start(f32[16,128]{1,0:T(8,128)S(1)} %add.36), channel_id=1, source_target_pairs={{2,0},{3,1},{0,2},{1,3},{6,4},{7,5},{4,6},{5,7},{10,8},{11,9},{8,1... | collective-permute-start | bytes 24584 | tf_op jit(solution)/shard_map/ppermute | solution.py:281
  41.7 7.8 %collective-permute-start.10 = (f32[64,640]{1,0:T(8,128)S(1)}, f32[64,640]{1,0:T(8,128)S(1)}, u32[]{:S(2)}, u32[]{:S(2)}) collective-permute-start(f32[64,640]{1,0:T(8,128)S(1)} %add.35), channel_id=1, source_target_pairs={{1,0},{6,1},{10,2},{13,3},{3,4},{4,5},{8,6},{15,7},{0,8},{7,9},{11... | collective-permute-start | bytes 491528 | tf_op jit(solution)/shard_map/ppermute | solution.py:281
  42.4 7.2 %collective-permute-start.11 = (f32[64,640]{1,0:T(8,128)S(1)}, f32[64,640]{1,0:T(8,128)S(1)}, u32[]{:S(2)}, u32[]{:S(2)}) collective-permute-start(f32[64,640]{1,0:T(8,128)S(1)} %add.35), channel_id=1, source_target_pairs={{2,0},{5,1},{11,2},{12,3},{0,4},{7,5},{9,6},{14,7},{1,8},{6,9},{8,... | collective-permute-start | bytes 491528 | tf_op jit(solution)/shard_map/ppermute | solution.py:281
  43.6 5.4 %collective-permute-start.16 = (f32[16,128]{1,0:T(8,128)S(1)}, f32[16,128]{1,0:T(8,128)S(1)}, u32[]{:S(2)}, u32[]{:S(2)}) collective-permute-start(f32[16,128]{1,0:T(8,128)S(1)} %add_add_fusion.mine_ref), channel_id=1, source_target_pairs={{0,4},{4,0},{8,12},{12,8},{1,5},{5,1},{9,13},{13,9},{2,6},{6,2},{1... | collective-permute-start | bytes 24584 | tf_op jit(solution)/shard_map/ppermute | solution.py:287
